TPU v7x, 32 devices: a whole 2x2x4 slice. The times are simulated.
32 devices in a mesh: dp: 8 (over y, x, core), mp: 4 (over z).
Axes of the slice: x: 2, y: 2, z: 4, core: 2. Of those that a mesh axis runs over, the one named last changes fastest.
Arguments:
- activations: bfloat16 [8192, 1024], P(('dp', 'mp')), may hold values from -6 to 6
- lengths: int32 [8, 4], P('dp'), may hold values from 1 to 1024, as said below
- cotangent: bfloat16 [8192, 1024], P(('dp', 'mp')), may hold values from -6 to 6
- gain_attn: float32 [2, 1024], replicated, may hold values from 0.5 to 1.5
- shift_attn: float32 [2, 1024], replicated, may hold values from -3 to 3
- w_query: bfloat16 [2, 1024, 1024], P(None, None, 'mp'), may hold values from -0.1875 to 0.1875
- b_query: float32 [2, 1024], P(None, 'mp'), may hold values from -3 to 3
- w_key: bfloat16 [2, 1024, 1024], P(None, None, 'mp'), may hold values from -0.1875 to 0.1875
- w_value: bfloat16 [2, 1024, 1024], P(None, None, 'mp'), may hold values from -0.1875 to 0.1875
- b_value: float32 [2, 1024], P(None, 'mp'), may hold values from -3 to 3
- w_out: bfloat16 [2, 1024, 1024], P(None, 'mp'), may hold values from -0.75 to 0.75
- b_out: float32 [2, 1024], replicated, may hold values from -3 to 3
- gain_ffn: float32 [2, 1024], replicated, may hold values from 0.5 to 1.5
- shift_ffn: float32 [2, 1024], replicated, may hold values from -3 to 3
- w_up: bfloat16 [2, 1024, 4096], P(None, None, 'mp'), may hold values from -0.1875 to 0.1875
- b_up: float32 [2, 4096], replicated, may hold values from -3 to 3
- w_down: bfloat16 [2, 4096, 1024], P(None, 'mp'), may hold values from -0.09375 to 0.09375
- b_down: float32 [2, 1024], replicated, may hold values from -3 to 3
Outputs:
- activations_out: bfloat16 [8192, 1024], P(('dp', 'mp'))
- input_grad: bfloat16 [8192, 1024], P(('dp', 'mp'))
- grad_gain_attn: float32 [2, 1024], replicated
- grad_shift_attn: float32 [2, 1024], replicated
- grad_w_query: float32 [2, 1024, 1024], P(None, None, 'mp')
- grad_b_query: float32 [2, 1024], P(None, 'mp')
- grad_w_key: float32 [2, 1024, 1024], P(None, None, 'mp')
- grad_w_value: float32 [2, 1024, 1024], P(None, None, 'mp')
- grad_b_value: float32 [2, 1024], P(None, 'mp')
- grad_w_out: float32 [2, 1024, 1024], P(None, 'mp')
- grad_b_out: float32 [2, 1024], replicated
- grad_gain_ffn: float32 [2, 1024], replicated
- grad_shift_ffn: float32 [2, 1024], replicated
- grad_w_up: float32 [2, 1024, 4096], P(None, None, 'mp')
- grad_b_up: float32 [2, 4096], P(None, 'mp')
- grad_w_down: float32 [2, 4096, 1024], P(None, 'mp')
- grad_b_down: float32 [2, 1024], replicated
Inputs may be any that keep to these rules, and one draw needn't show every extreme that they name: Each row holds 4 lengths that sum to 1024; one of them, at a place drawn from the seed, is more than 768, the others are under 256 / 4.
All inputs are finite; a program needn't handle non-finite values.
Results may differ from a plain program's by a relative error of at most 0.024.
Values may be sent and summed in bfloat16 or wider, within the bound.
No kernel may reach another device: no remote copies, remote signals or barrier semaphores. Data moves between devices by JAX's collectives and lax.ppermute only.
A program may use at most 192 MiB of HBM per device.

v0:
```python
import jax
import jax.numpy as jnp
from jax import lax
from jax.sharding import PartitionSpec as P

H = 8
HD = 128
LAYERS = 2


norm_eps = 1e-05


def gelu_tanh(values):
    return jax.nn.gelu(values, approximate=True)


def norm_parts(stream):
    centred = stream - jnp.mean(stream, axis=-1, keepdims=True)
    inverse = lax.rsqrt(jnp.mean(centred * centred, axis=-1, keepdims=True) + norm_eps)
    return (centred * inverse, inverse)


def norm_back(grad_normed, unit_rows, inverse, gain):
    scaled = grad_normed * gain
    return inverse * (
        scaled
        - jnp.mean(scaled, axis=-1, keepdims=True)
        - unit_rows * jnp.mean(scaled * unit_rows, axis=-1, keepdims=True)
    )


def segment_ids(row_lengths, total_rows):
    doc_ends = jnp.cumsum(row_lengths)
    positions = jnp.arange(total_rows, dtype=jnp.int32)
    return jnp.sum((positions[:, None] >= doc_ends[None, :]).astype(jnp.int32), axis=1)


def block_scores(query_block, key_block, query_pos, key_pos, query_seg, key_seg, slopes):
    logits = jnp.einsum(
        "qhd,khd->hqk", query_block, key_block, preferred_element_type=jnp.float32
    ) * HD ** (-0.5)
    distance = (query_pos[:, None] - key_pos[None, :]).astype(jnp.float32)
    logits = logits - slopes[:, None, None] * distance[None]
    allowed = (query_seg[:, None] == key_seg[None, :]) & (key_pos[None, :] <= query_pos[:, None])
    return jnp.where(allowed[None], logits, -1e30)


def attend_forward(query_rows, key_rows, value_rows, segments, slopes):
    total_rows = query_rows.shape[0]
    head_count = slopes.shape[0]
    block_rows = min(512, total_rows)
    positions = jnp.arange(total_rows, dtype=jnp.int32)
    query_heads = query_rows.reshape(total_rows, head_count, HD)
    key_heads = key_rows.reshape(total_rows, head_count, HD)
    value_heads = value_rows.reshape(total_rows, head_count, HD)
    outputs = []
    log_parts = []
    for block_index in range(total_rows // block_rows):
        begin_row = block_index * block_rows
        finish = begin_row + block_rows
        scores = block_scores(
            query_heads[begin_row:finish],
            key_heads[:finish],
            positions[begin_row:finish],
            positions[:finish],
            segments[begin_row:finish],
            segments[:finish],
            slopes,
        )
        row_max = jnp.max(scores, axis=-1, keepdims=True)
        weights = jnp.exp(scores - row_max)
        totals = jnp.sum(weights, axis=-1, keepdims=True)
        probabilities = (weights / totals).astype(jnp.bfloat16)
        mixed_block = jnp.einsum(
            "hqk,khd->qhd", probabilities, value_heads[:finish], preferred_element_type=jnp.float32
        )
        outputs.append(mixed_block.reshape(block_rows, head_count * HD))
        log_parts.append(row_max[..., 0] + jnp.log(totals[..., 0]))
    return (jnp.concatenate(outputs, 0).astype(jnp.bfloat16), jnp.concatenate(log_parts, 1))


def attend_backward(query_rows, key_rows, value_rows, segments, slopes, log_totals, grad_mixed):
    total_rows = query_rows.shape[0]
    head_count = slopes.shape[0]
    block_rows = min(512, total_rows)
    score_scale = HD ** (-0.5)
    positions = jnp.arange(total_rows, dtype=jnp.int32)
    query_heads = query_rows.reshape(total_rows, head_count, HD)
    key_heads = key_rows.reshape(total_rows, head_count, HD)
    value_heads = value_rows.reshape(total_rows, head_count, HD)
    grad_heads = grad_mixed.reshape(total_rows, head_count, HD)
    grad_keys = jnp.zeros((total_rows, head_count, HD), jnp.float32)
    grad_values = jnp.zeros((total_rows, head_count, HD), jnp.float32)
    query_parts = []
    for block_index in range(total_rows // block_rows):
        begin_row = block_index * block_rows
        finish = begin_row + block_rows
        scores = block_scores(
            query_heads[begin_row:finish],
            key_heads[:finish],
            positions[begin_row:finish],
            positions[:finish],
            segments[begin_row:finish],
            segments[:finish],
            slopes,
        )
        probabilities = jnp.exp(scores - log_totals[:, begin_row:finish, None])
        rounded = probabilities.astype(jnp.bfloat16)
        grad_block = grad_heads[begin_row:finish]
        grad_values = grad_values.at[:finish].add(
            jnp.einsum("hqk,qhd->khd", rounded, grad_block, preferred_element_type=jnp.float32)
        )
        grad_probs = jnp.einsum(
            "qhd,khd->hqk", grad_block, value_heads[:finish], preferred_element_type=jnp.float32
        )
        centre = jnp.sum(grad_probs * probabilities, axis=-1, keepdims=True)
        grad_scores = (probabilities * (grad_probs - centre)).astype(jnp.bfloat16)
        query_parts.append(
            jnp.einsum(
                "hqk,khd->qhd", grad_scores, key_heads[:finish], preferred_element_type=jnp.float32
            )
            * score_scale
        )
        grad_keys = grad_keys.at[:finish].add(
            jnp.einsum(
                "hqk,qhd->khd",
                grad_scores,
                query_heads[begin_row:finish],
                preferred_element_type=jnp.float32,
            )
            * score_scale
        )
    width = head_count * HD
    grad_queries = jnp.concatenate(query_parts, 0).reshape(total_rows, width).astype(jnp.bfloat16)
    return (
        grad_queries,
        grad_keys.reshape(total_rows, width).astype(jnp.bfloat16),
        grad_values.reshape(total_rows, width).astype(jnp.bfloat16),
    )


def local(
    activations,
    lengths,
    cotangent,
    gain_attn,
    shift_attn,
    w_query,
    b_query,
    w_key,
    w_value,
    b_value,
    w_out,
    b_out,
    gain_ffn,
    shift_ffn,
    w_up,
    b_up,
    w_down,
    b_down,
):
    local_rows = activations.shape[0]
    group_rows = local_rows * lax.axis_size("mp")
    segments = segment_ids(lengths[0], group_rows)
    head_count = w_query.shape[2] // HD
    head_ids = (lax.axis_index("mp") * head_count + jnp.arange(head_count, dtype=jnp.int32)).astype(
        jnp.float32
    )
    slopes = 2.0 ** (-8.0 * (head_ids + 1.0) / H)
    hidden_share = w_up.shape[2]
    hidden_start = lax.axis_index("mp") * hidden_share
    stream = activations.astype(jnp.float32)
    stored = []
    for layer_index in range(LAYERS):
        unit_rows, inverse = norm_parts(stream)
        normed = (unit_rows * gain_attn[layer_index] + shift_attn[layer_index]).astype(jnp.bfloat16)
        inputs = lax.all_gather(normed, "mp", axis=0, tiled=True)
        query_rows = (
            jnp.dot(inputs, w_query[layer_index], preferred_element_type=jnp.float32)
            + b_query[layer_index]
        ).astype(jnp.bfloat16)
        key_rows = jnp.dot(inputs, w_key[layer_index], preferred_element_type=jnp.float32).astype(
            jnp.bfloat16
        )
        value_rows = (
            jnp.dot(inputs, w_value[layer_index], preferred_element_type=jnp.float32)
            + b_value[layer_index]
        ).astype(jnp.bfloat16)
        mixed_rows, log_totals = attend_forward(query_rows, key_rows, value_rows, segments, slopes)
        out_weight = w_out[layer_index]
        middle = stream + (
            lax.psum_scatter(
                jnp.dot(mixed_rows, out_weight, preferred_element_type=jnp.float32).astype(
                    jnp.bfloat16
                ),
                "mp",
                scatter_dimension=0,
                tiled=True,
            ).astype(jnp.float32)
            + b_out[layer_index]
        )
        unit_mid, inverse_mid = norm_parts(middle)
        normed_mid = (unit_mid * gain_ffn[layer_index] + shift_ffn[layer_index]).astype(
            jnp.bfloat16
        )
        full_up = w_up[layer_index]
        full_down = w_down[layer_index]
        inputs_mid = lax.all_gather(normed_mid, "mp", axis=0, tiled=True)
        bias_share = lax.dynamic_slice_in_dim(b_up[layer_index], hidden_start, hidden_share, 0)
        hidden = jnp.dot(inputs_mid, full_up, preferred_element_type=jnp.float32) + bias_share
        active = gelu_tanh(hidden).astype(jnp.bfloat16)

        def ffn_term(first_row, row_count, active=active, full_down=full_down):
            return jnp.dot(active, full_down, preferred_element_type=jnp.float32)

        stream = middle + (
            lax.psum_scatter(
                ffn_term(jnp.int32(0), local_rows * lax.axis_size("mp")).astype(jnp.bfloat16),
                "mp",
                scatter_dimension=0,
                tiled=True,
            ).astype(jnp.float32)
            + b_down[layer_index]
        )
        stored.append(
            (
                unit_rows,
                inverse,
                inputs,
                query_rows,
                key_rows,
                value_rows,
                mixed_rows,
                log_totals,
                unit_mid,
                inverse_mid,
                inputs_mid,
                hidden,
                active,
                full_up,
                full_down,
            )
        )
    activations_out = stream.astype(jnp.bfloat16)
    grad_stream = cotangent.astype(jnp.float32)
    sharded_list = [None] * LAYERS
    shared_list = [None] * LAYERS
    for layer_index in reversed(range(LAYERS)):
        (
            unit_rows,
            inverse,
            inputs,
            query_rows,
            key_rows,
            value_rows,
            mixed_rows,
            log_totals,
            unit_mid,
            inverse_mid,
            inputs_mid,
            hidden,
            active,
            up_weight,
            down_weight,
        ) = stored[layer_index]
        out_weight = w_out[layer_index]
        grad_branch = grad_stream.astype(jnp.bfloat16)
        grad_b_down = jnp.sum(grad_branch, axis=0, dtype=jnp.float32)

        def down_fold(running, shard_piece, first_row, active=active, down_weight=down_weight):
            grad_active = jnp.einsum(
                "td,fd->tf", shard_piece, down_weight, preferred_element_type=jnp.float32
            )
            grad_w_down = jnp.einsum(
                "tf,td->fd", active, shard_piece, preferred_element_type=jnp.float32
            )
            return (grad_active, grad_w_down)

        grad_active, grad_w_down = down_fold(
            (jnp.zeros(hidden.shape, jnp.float32), jnp.zeros(down_weight.shape, jnp.float32)),
            lax.all_gather(grad_branch, "mp", axis=0, tiled=True),
            jnp.int32(0),
        )
        activated, gelu_pull = jax.vjp(gelu_tanh, hidden)
        grad_hidden = gelu_pull(grad_active)[0].astype(jnp.bfloat16)
        grad_b_up = jnp.sum(grad_hidden, axis=0, dtype=jnp.float32)
        grad_w_up = jnp.einsum(
            "td,tf->df", inputs_mid, grad_hidden, preferred_element_type=jnp.float32
        )

        def up_term(first_row, row_count, grad_hidden=grad_hidden, up_weight=up_weight):
            return jnp.einsum(
                "tf,df->td", grad_hidden, up_weight, preferred_element_type=jnp.float32
            )

        grad_normed_mid = lax.psum_scatter(
            up_term(jnp.int32(0), local_rows * lax.axis_size("mp")).astype(jnp.bfloat16),
            "mp",
            scatter_dimension=0,
            tiled=True,
        ).astype(jnp.float32)
        grad_gain_ffn = jnp.sum(grad_normed_mid * unit_mid, axis=0)
        grad_shift_ffn = jnp.sum(grad_normed_mid, axis=0)
        grad_middle = grad_stream + norm_back(
            grad_normed_mid, unit_mid, inverse_mid, gain_ffn[layer_index]
        )
        grad_attn_branch = grad_middle.astype(jnp.bfloat16)
        grad_b_out = jnp.sum(grad_attn_branch, axis=0, dtype=jnp.float32)

        def out_fold(running, shard_piece, first_row, mixed_rows=mixed_rows, out_weight=out_weight):
            grad_mixed = jnp.einsum(
                "td,ed->te", shard_piece, out_weight, preferred_element_type=jnp.float32
            )
            grad_w_out = jnp.einsum(
                "te,td->ed", mixed_rows, shard_piece, preferred_element_type=jnp.float32
            )
            return (grad_mixed, grad_w_out)

        grad_mixed, grad_w_out = out_fold(
            (jnp.zeros(mixed_rows.shape, jnp.float32), jnp.zeros(out_weight.shape, jnp.float32)),
            lax.all_gather(grad_attn_branch, "mp", axis=0, tiled=True),
            jnp.int32(0),
        )
        grad_queries, grad_keys, grad_values = attend_backward(
            query_rows,
            key_rows,
            value_rows,
            segments,
            slopes,
            log_totals,
            grad_mixed.astype(jnp.bfloat16),
        )
        grad_b_query = jnp.sum(grad_queries, axis=0, dtype=jnp.float32)
        grad_b_value = jnp.sum(grad_values, axis=0, dtype=jnp.float32)
        grad_w_query = jnp.einsum(
            "td,te->de", inputs, grad_queries, preferred_element_type=jnp.float32
        )
        grad_w_key = jnp.einsum("td,te->de", inputs, grad_keys, preferred_element_type=jnp.float32)
        grad_w_value = jnp.einsum(
            "td,te->de", inputs, grad_values, preferred_element_type=jnp.float32
        )
        query_weight = w_query[layer_index]
        key_weight = w_key[layer_index]
        value_weight = w_value[layer_index]

        def in_term(
            first_row,
            row_count,
            grad_queries=grad_queries,
            grad_keys=grad_keys,
            grad_values=grad_values,
            query_weight=query_weight,
            key_weight=key_weight,
            value_weight=value_weight,
        ):
            return (
                jnp.einsum(
                    "te,de->td", grad_queries, query_weight, preferred_element_type=jnp.float32
                )
                + jnp.einsum("te,de->td", grad_keys, key_weight, preferred_element_type=jnp.float32)
                + jnp.einsum(
                    "te,de->td", grad_values, value_weight, preferred_element_type=jnp.float32
                )
            )

        grad_normed = lax.psum_scatter(
            in_term(jnp.int32(0), local_rows * lax.axis_size("mp")).astype(jnp.bfloat16),
            "mp",
            scatter_dimension=0,
            tiled=True,
        ).astype(jnp.float32)
        grad_gain_attn = jnp.sum(grad_normed * unit_rows, axis=0)
        grad_shift_attn = jnp.sum(grad_normed, axis=0)
        grad_stream = grad_middle + norm_back(
            grad_normed, unit_rows, inverse, gain_attn[layer_index]
        )
        sharded = (
            grad_w_query,
            grad_b_query,
            grad_w_key,
            grad_w_value,
            grad_b_value,
            grad_w_out,
            grad_w_up,
            grad_b_up,
            grad_w_down,
        )
        shared = (
            grad_gain_attn,
            grad_shift_attn,
            grad_b_out,
            grad_gain_ffn,
            grad_shift_ffn,
            grad_b_down,
        )
        sharded_list[layer_index] = sharded
        shared_list[layer_index] = shared
    sharded_stack = [
        jnp.stack([sharded_list[depth_index][member_index] for depth_index in range(LAYERS)])
        for member_index in range(9)
    ]
    shared_stack = [
        jnp.stack([shared_list[depth_index][member_index] for depth_index in range(LAYERS)])
        for member_index in range(6)
    ]
    sharded_stack = (
        lax.psum(sharded_stack[0].astype(jnp.bfloat16), "dp").astype(jnp.float32),
        lax.psum(sharded_stack[1].astype(jnp.bfloat16), "dp").astype(jnp.float32),
        lax.psum(sharded_stack[2].astype(jnp.bfloat16), "dp").astype(jnp.float32),
        lax.psum(sharded_stack[3].astype(jnp.bfloat16), "dp").astype(jnp.float32),
        lax.psum(sharded_stack[4].astype(jnp.bfloat16), "dp").astype(jnp.float32),
        lax.psum(sharded_stack[5].astype(jnp.bfloat16), "dp").astype(jnp.float32),
        lax.psum(sharded_stack[6].astype(jnp.bfloat16), "dp").astype(jnp.float32),
        lax.psum(sharded_stack[7].astype(jnp.bfloat16), "dp").astype(jnp.float32),
        lax.psum(sharded_stack[8].astype(jnp.bfloat16), "dp").astype(jnp.float32),
    )
    shared_stack = lax.psum(
        (
            shared_stack[0],
            shared_stack[1],
            shared_stack[2],
            shared_stack[3],
            shared_stack[4],
            shared_stack[5],
        ),
        ("dp", "mp"),
    )
    return (
        activations_out,
        grad_stream.astype(jnp.bfloat16),
        shared_stack[0],
        shared_stack[1],
        sharded_stack[0],
        sharded_stack[1],
        sharded_stack[2],
        sharded_stack[3],
        sharded_stack[4],
        sharded_stack[5],
        shared_stack[2],
        shared_stack[3],
        shared_stack[4],
        sharded_stack[6],
        sharded_stack[7],
        sharded_stack[8],
        shared_stack[5],
    )


def solution(mesh):
    return jax.shard_map(
        local,
        mesh=mesh,
        in_specs=(
            P(("dp", "mp"), None),
            P("dp", None),
            P(("dp", "mp"), None),
            P(),
            P(),
            P(None, None, "mp"),
            P(None, "mp"),
            P(None, None, "mp"),
            P(None, None, "mp"),
            P(None, "mp"),
            P(None, "mp", None),
            P(),
            P(),
            P(),
            P(None, None, "mp"),
            P(),
            P(None, "mp", None),
            P(),
        ),
        out_specs=(
            P(("dp", "mp"), None),
            P(("dp", "mp"), None),
            P(),
            P(),
            P(None, None, "mp"),
            P(None, "mp"),
            P(None, None, "mp"),
            P(None, None, "mp"),
            P(None, "mp"),
            P(None, "mp", None),
            P(),
            P(),
            P(),
            P(None, None, "mp"),
            P(None, "mp"),
            P(None, "mp", None),
            P(),
        ),
        check_vma=False,
    )
```

profile of v0, /device:TPU:0, one launch (start us, length us, event | category | flops | bytes accessed | tf_op | source)
XLA Modules:
  0.0 1051.2 jit_solution(4859836832526510684)
XLA Ops:
  19.7 42.7 %all-gather.9.cloned.1.call-done = bf16[1024,1024]{1,0:T(8,128)(2,1)} async-done(((bf16[256,1024]{1,0:T(8,128)(2,1)}), bf16[1024,1024]{1,0:T(8,128)(2,1)}) %all-gather.9.cloned.1.call-update) | async-done | bytes 2097168 | tf_op jit(solution)/shard_map/all_gather | solution.py:178
  62.4 2.5 fusion.111
  75.9 42.6 %reduce-scatter.9.cloned.1.call-done = bf16[256,1024]{1,0:T(8,128)(2,1)} async-done(((bf16[1024,1024]{1,0:T(8,128)(2,1)}), bf16[256,1024]{1,0:T(8,128)(2,1)}) %reduce-scatter.9.cloned.1.call-update) | async-done | bytes 524304 | tf_op jit(solution)/shard_map/reduce_scatter | solution.py:193
  121.2 2.1 add_convert_fusion.5
  124.0 44.8 %all-gather.11.cloned.1.call-done = bf16[1024,1024]{1,0:T(8,128)(2,1)} async-done(((bf16[256,1024]{1,0:T(8,128)(2,1)}), bf16[1024,1024]{1,0:T(8,128)(2,1)}) %all-gather.11.cloned.1.call-update) | async-done | bytes 2097168 | tf_op jit(solution)/shard_map/all_gather | solution.py:209
  168.8 4.7 fusion.44
  175.4 4.1 fusion.54
  179.7 42.7 %reduce-scatter.11.cloned.1.call-done = bf16[256,1024]{1,0:T(8,128)(2,1)} async-done(((bf16[1024,1024]{1,0:T(8,128)(2,1)}), bf16[256,1024]{1,0:T(8,128)(2,1)}) %reduce-scatter.11.cloned.1.call-update) | async-done | bytes 524304 | tf_op jit(solution)/shard_map/reduce_scatter | solution.py:218
  225.8 45.4 %all-gather.13.cloned.1.call-done = bf16[1024,1024]{1,0:T(8,128)(2,1)} async-done(((bf16[256,1024]{1,0:T(8,128)(2,1)}), bf16[1024,1024]{1,0:T(8,128)(2,1)}) %all-gather.13.cloned.1.call-update) | async-done | bytes 2097168 | tf_op jit(solution)/shard_map/all_gather | solution.py:178
  271.2 2.6 fusion.113
  285.6 42.7 %reduce-scatter.13.cloned.1.call-done = bf16[256,1024]{1,0:T(8,128)(2,1)} async-done(((bf16[1024,1024]{1,0:T(8,128)(2,1)}), bf16[256,1024]{1,0:T(8,128)(2,1)}) %reduce-scatter.13.cloned.1.call-update) | async-done | bytes 524304 | tf_op jit(solution)/shard_map/reduce_scatter | solution.py:193
  333.0 44.4 %all-gather.15.cloned.1.call-done = bf16[1024,1024]{1,0:T(8,128)(2,1)} async-done(((bf16[256,1024]{1,0:T(8,128)(2,1)}), bf16[1024,1024]{1,0:T(8,128)(2,1)}) %all-gather.15.cloned.1.call-update) | async-done | bytes 2097168 | tf_op jit(solution)/shard_map/all_gather | solution.py:209
  377.4 6.6 fusion.34
  383.9 39.8 %all-gather.17.cloned.1.call-done = bf16[1024,1024]{1,0:T(8,128)(2,1)} async-done(((bf16[256,1024]{1,0:T(8,128)(2,1)}), bf16[1024,1024]{1,0:T(8,128)(2,1)}) %all-gather.17.cloned.1.call-update) | async-done | bytes 2097168 | tf_op jit(solution)/shard_map/all_gather | solution.py:282
  423.7 8.4 fusion.237
  433.4 3.7 fusion.57
  437.2 7.0 fusion.60
  444.3 35.6 %reduce-scatter.17.cloned.1.call-done = bf16[256,1024]{1,0:T(8,128)(2,1)} async-done(((bf16[1024,1024]{1,0:T(8,128)(2,1)}), bf16[256,1024]{1,0:T(8,128)(2,1)}) %reduce-scatter.17.cloned.1.call-update) | async-done | bytes 524304 | tf_op jit(solution)/shard_map/reduce_scatter | solution.py:297
  481.8 44.0 %reduce-scatter.15.cloned.1.call-done = bf16[256,1024]{1,0:T(8,128)(2,1)} async-done(((bf16[1024,1024]{1,0:T(8,128)(2,1)}), bf16[256,1024]{1,0:T(8,128)(2,1)}) %reduce-scatter.15.cloned.1.call-update) | async-done | bytes 524304 | tf_op jit(solution)/shard_map/reduce_scatter | solution.py:218
  525.8 3.6 convert_reduce_fusion.7
  529.8 45.1 %all-gather.19.cloned.1.call-done = bf16[1024,1024]{1,0:T(8,128)(2,1)} async-done(((bf16[256,1024]{1,0:T(8,128)(2,1)}), bf16[1024,1024]{1,0:T(8,128)(2,1)}) %all-gather.19.cloned.1.call-update) | async-done | bytes 2097168 | tf_op jit(solution)/shard_map/all_gather | solution.py:322
  574.9 2.6 convolution_convert_fusion.11
  587.6 2.1 add_convert_fusion.1
  589.8 42.7 %reduce-scatter.19.cloned.1.call-done = bf16[256,1024]{1,0:T(8,128)(2,1)} async-done(((bf16[1024,1024]{1,0:T(8,128)(2,1)}), bf16[256,1024]{1,0:T(8,128)(2,1)}) %reduce-scatter.19.cloned.1.call-update) | async-done | bytes 524304 | tf_op jit(solution)/shard_map/reduce_scatter | solution.py:367
  634.4 3.2 convert_reduce_fusion.6
  638.2 44.9 %all-gather.21.cloned.1.call-done = bf16[1024,1024]{1,0:T(8,128)(2,1)} async-done(((bf16[256,1024]{1,0:T(8,128)(2,1)}), bf16[1024,1024]{1,0:T(8,128)(2,1)}) %all-gather.21.cloned.1.call-update) | async-done | bytes 2097168 | tf_op jit(solution)/shard_map/all_gather | solution.py:282
  683.1 8.4 fusion.238
  692.8 3.7 fusion.51
  696.6 42.7 %reduce-scatter.21.cloned.1.call-done = bf16[256,1024]{1,0:T(8,128)(2,1)} async-done(((bf16[1024,1024]{1,0:T(8,128)(2,1)}), bf16[256,1024]{1,0:T(8,128)(2,1)}) %reduce-scatter.21.cloned.1.call-update) | async-done | bytes 524304 | tf_op jit(solution)/shard_map/reduce_scatter | solution.py:297
  741.0 3.0 convert_reduce_fusion.8
  744.3 6.1 convert_bitcast_fusion.2
  750.4 4.4 convert_bitcast_fusion
  756.4 33.1 %all-gather.23.cloned.1.call-done = bf16[1024,1024]{1,0:T(8,128)(2,1)} async-done(((bf16[256,1024]{1,0:T(8,128)(2,1)}), bf16[1024,1024]{1,0:T(8,128)(2,1)}) %all-gather.23.cloned.1.call-update) | async-done | bytes 2097168 | tf_op jit(solution)/shard_map/all_gather | solution.py:322
  789.4 2.5 convolution_convert_fusion.10
  804.1 2.5 fusion.130
  806.6 2.4 fusion.126
  809.0 2.4 convert_bitcast_fusion.3
  811.5 2.5 pad_maximum_fusion
  815.8 3.1 convert_bitcast_fusion.1
  818.9 2.4 pad_maximum_fusion.1
  829.8 14.3 %all-reduce.5 = (bf16[2,256]{1,0:T(2,128)(2,1)S(1)}, bf16[2,256]{1,0:T(2,128)(2,1)S(1)}, bf16[2,1024]{1,0:T(2,128)(2,1)S(1)}) all-reduce(bf16[2,256]{1,0:T(2,128)(2,1)S(1)} %pad_maximum_fusion.19, bf16[2,256]{1,0:T(2,128)(2,1)S(1)} %pad_maximum_fusion.20, ...), channel_id=1, replica_groups=mesh['dp'=8,'mp'=4] {'dp'}, use_global_device_ids=true, to_apply=%region_47.48 | all-reduce | flops 3072 | bytes 12288 | tf_op jit(solution)/shard_map/psum | solution.py:409
  848.2 41.4 %all-reduce.4 = (f32[2,1024]{1,0:T(2,128)}, f32[2,1024]{1,0:T(2,128)}, f32[2,1024]{1,0:T(2,128)}, f32[2,1024]{1,0:T(2,128)}, f32[2,1024]{1,0:T(2,128)}, /*index=5*/f32[2,1024]{1,0:T(2,128)}) all-reduce(f32[2,1024]{1,0:T(2,128)S(1)} %get-tuple-element.251, ...), channel_id=1, replica_groups=mesh['dp'=8,'mp'=4] {'dp','mp'}, use_global_device_ids=true, to_apply=%region_40.41 | all-reduce | flops 12288 | bytes 98304 | tf_op jit(solution)/shard_map/psum | solution.py:418
  889.6 2.3 fusion.140
  891.9 134.8 %all-reduce.9.cloned.1.call-done = (bf16[2,1024,256]{2,1,0:T(8,128)(2,1)}, bf16[2,1024,256]{2,1,0:T(8,128)(2,1)}, bf16[2,1024,256]{2,1,0:T(8,128)(2,1)}, bf16[2,...) async-done(((bf16[2,1024,256]{2,1,0:T(8,128)(2,1)}, bf16[2,1024,256]{2,1,0:T(8,128)(2,1)}, bf16[2,1024,256]{2,1,0:T(8,128)(2,1)}, ...) | async-done | bytes 12582928 | tf_op jit(solution)/shard_map/psum | solution.py:408
  1026.6 2.9 convert_element_type.369
  1029.5 2.9 convert_element_type.373
  1035.4 4.4 convert_element_type.381
  1039.8 4.4 convert_element_type.385
  (377 shorter events, 98.2 us)
Async XLA Ops:
  7.2 55.2 %copy-start.55 = (bf16[2,1024,256]{2,1,0:T(8,128)(2,1)S(1)}, bf16[2,1024,256]{2,1,0:T(8,128)(2,1)}, u32[]{:S(2)}) copy-start(bf16[2,1024,256]{2,1,0:T(8,128)(2,1)} %param.50) | copy-start | bytes 3145732
  7.2 55.2 %all-gather.9.cloned.1.call-start = ((), (), s32[]{:S(2)}) async-start(), calls=%async_computation.8 | async-start | bytes 2621440 | tf_op jit(solution)/shard_map/all_gather | solution.py:178
  8.5 7.9 copy-start.78
  9.9 5.5 copy-start.80
  10.7 5.8 copy-start.75
  13.6 104.9 %reduce-scatter.9.cloned.1.call-start = ((), (), s32[]{:S(2)}) async-start(), calls=%async_computation.9 | async-start | bytes 2621440 | tf_op jit(solution)/shard_map/reduce_scatter | solution.py:193
  16.2 48.8 %copy-start.51 = (bf16[2,1024,256]{2,1,0:T(8,128)(2,1)S(1)}, bf16[2,1024,256]{2,1,0:T(8,128)(2,1)}, u32[]{:S(2)}) copy-start(bf16[2,1024,256]{2,1,0:T(8,128)(2,1)} %param.47) | copy-start | bytes 3145732
  17.0 51.3 %copy-start.14 = (pred[512,1024]{1,0:T(8,128)(4,1)}, pred[512,1024]{1,0:T(8,128)(4,1)S(1)}, u32[]{:S(2)}) copy-start(pred[512,1024]{1,0:T(8,128)(4,1)S(1)} %fusion.48) | copy-start | bytes 1572868
  64.9 7.3 copy-start.43
  68.4 5.0 copy-start.67
  73.3 50.0 %copy-start.69 = (bf16[2,128,512]{2,1,0:T(8,128)(2,1)}, bf16[2,128,512]{2,1,0:T(8,128)(2,1)S(1)}, u32[]{:S(2)}) copy-start(bf16[2,128,512]{2,1,0:T(8,128)(2,1)S(1)} %fusion.134) | copy-start | bytes 786436
  73.4 45.2 %copy-start.4 = (bf16[256,1024]{1,0:T(8,128)(2,1)S(1)}, bf16[256,1024]{1,0:T(8,128)(2,1)}, u32[]{:S(2)}) copy-start(bf16[256,1024]{1,0:T(8,128)(2,1)} %param.42) | copy-start | bytes 1572868
  73.7 50.2 %copy-start.77 = (f32[2,4096]{1,0:T(2,128)S(1)}, f32[2,4096]{1,0:T(2,128)}, u32[]{:S(2)}) copy-start(f32[2,4096]{1,0:T(2,128)} %param.57) | copy-start | bytes 98308
  75.8 93.0 %all-gather.11.cloned.1.call-start = ((), (), s32[]{:S(2)}) async-start(), calls=%async_computation.10 | async-start | bytes 2621440 | tf_op jit(solution)/shard_map/all_gather | solution.py:209
  123.4 98.9 %reduce-scatter.11.cloned.1.call-start = ((), (), s32[]{:S(2)}) async-start(), calls=%async_computation.11 | async-start | bytes 2621440 | tf_op jit(solution)/shard_map/reduce_scatter | solution.py:218
  168.8 6.7 copy-start.86
  175.4 46.9 %copy-start.11 = (bf16[256,1024]{1,0:T(8,128)(2,1)S(1)}, bf16[256,1024]{1,0:T(8,128)(2,1)}, u32[]{:S(2)}) copy-start(bf16[256,1024]{1,0:T(8,128)(2,1)} %reduce-scatter.9.cloned.1.call-done) | copy-start | bytes 1572868
  179.6 91.6 %all-gather.13.cloned.1.call-start = ((), (), s32[]{:S(2)}) async-start(), calls=%async_computation.12 | async-start | bytes 2621440 | tf_op jit(solution)/shard_map/all_gather | solution.py:178
  225.8 102.5 %reduce-scatter.13.cloned.1.call-start = ((), (), s32[]{:S(2)}) async-start(), calls=%async_computation.13 | async-start | bytes 2621440 | tf_op jit(solution)/shard_map/reduce_scatter | solution.py:193
  273.8 7.8 copy-start.45
  277.8 5.0 copy-start.71
  285.6 91.8 %all-gather.15.cloned.1.call-start = ((), (), s32[]{:S(2)}) async-start(), calls=%async_computation.14 | async-start | bytes 2621440 | tf_op jit(solution)/shard_map/all_gather | solution.py:209
  332.0 91.7 %all-gather.17.cloned.1.call-start = ((), (), s32[]{:S(2)}) async-start(), calls=%async_computation.16 | async-start | bytes 2621440 | tf_op jit(solution)/shard_map/all_gather | solution.py:282
  332.7 147.2 %reduce-scatter.17.cloned.1.call-start = ((), (), s32[]{:S(2)}) async-start(), calls=%async_computation.17 | async-start | bytes 2621440 | tf_op jit(solution)/shard_map/reduce_scatter | solution.py:297
  423.7 9.7 copy-start.87
  437.1 88.7 %reduce-scatter.15.cloned.1.call-start = ((), (), s32[]{:S(2)}) async-start(), calls=%async_computation.15 | async-start | bytes 2621440 | tf_op jit(solution)/shard_map/reduce_scatter | solution.py:218
  444.2 130.7 %all-gather.19.cloned.1.call-start = ((), (), s32[]{:S(2)}) async-start(), calls=%async_computation.18 | async-start | bytes 2621440 | tf_op jit(solution)/shard_map/all_gather | solution.py:322
  529.5 103.0 %reduce-scatter.19.cloned.1.call-start = ((), (), s32[]{:S(2)}) async-start(), calls=%async_computation.19 | async-start | bytes 2621440 | tf_op jit(solution)/shard_map/reduce_scatter | solution.py:367
  529.8 48.2 %copy-start.63 = (bf16[512,256]{0,1:T(8,128)(2,1)S(1)}, bf16[512,256]{0,1:T(8,128)(2,1)}, u32[]{:S(2)}) copy-start(bf16[512,256]{0,1:T(8,128)(2,1)} %copy-done.62) | copy-start | bytes 786436
  589.7 93.3 %all-gather.21.cloned.1.call-start = ((), (), s32[]{:S(2)}) async-start(), calls=%async_computation.20 | async-start | bytes 2621440 | tf_op jit(solution)/shard_map/all_gather | solution.py:282
  637.7 101.6 %reduce-scatter.21.cloned.1.call-start = ((), (), s32[]{:S(2)}) async-start(), calls=%async_computation.21 | async-start | bytes 2621440 | tf_op jit(solution)/shard_map/reduce_scatter | solution.py:297
  683.1 9.7 copy-start.88
  696.5 92.9 %all-gather.23.cloned.1.call-start = ((), (), s32[]{:S(2)}) async-start(), calls=%async_computation.22 | async-start | bytes 2621440 | tf_op jit(solution)/shard_map/all_gather | solution.py:322
  744.0 102.6 %reduce-scatter.23.cloned.1.call-start = ((), (), s32[]{:S(2)}) async-start(), calls=%async_computation.23 | async-start | bytes 2621440 | tf_op jit(solution)/shard_map/reduce_scatter | solution.py:367
  744.3 6.1 copy-start.95
  744.3 6.1 copy-start.100
  750.4 4.4 copy-start.38
  803.8 222.8 %all-reduce.9.cloned.1.call-start = ((), (), s32[]{:S(2)}) async-start(), calls=%async_computation.24 | async-start | bytes 25165824 | tf_op jit(solution)/shard_map/psum | solution.py:408
  804.1 4.9 copy-start.91
  804.1 4.9 copy-start.103
  829.6 17.0 %copy-start.76 = (f32[1,1024]{1,0:T(1,128)S(1)}, f32[1,1024]{1,0:T(1,128)}, u32[]{:S(2)}) copy-start(f32[1,1024]{1,0:T(1,128)} %copy-done.75) | copy-start | bytes 12292
  829.6 17.0 %copy-start.79 = (f32[256]{0:T(256)S(1)}, f32[256]{0:T(256)}, u32[]{:S(2)}) copy-start(f32[256]{0:T(256)} %copy-done.78) | copy-start | bytes 3076
  829.6 17.0 %copy-start.81 = (f32[256]{0:T(256)S(1)}, f32[256]{0:T(256)}, u32[]{:S(2)}) copy-start(f32[256]{0:T(256)} %copy-done.80) | copy-start | bytes 3076
  829.6 60.0 %copy-start.18 = (f32[256,1024]{1,0:T(8,128)S(1)}, f32[256,1024]{1,0:T(8,128)}, u32[]{:S(2)}) copy-start(f32[256,1024]{1,0:T(8,128)} %get-tuple-element.185) | copy-start | bytes 3145732
  1026.6 5.7 copy-start.59
  1026.6 7.2 copy-start.58
  1029.5 5.9 copy-start.17
  1035.4 4.4 copy-start.16
  (73 other events, 157.9 us)
Sparse Core Ops, SparseCore 0:
  13.7 48.6 all-gather.8
  75.9 42.5 reduce-scatter.8
  123.5 45.2 all-gather.10
  179.7 42.5 reduce-scatter.10
  225.9 45.2 all-gather.12
  285.7 42.5 reduce-scatter.12
  332.1 45.2 all-gather.14
  379.0 44.6 all-gather.16
  437.3 42.5 reduce-scatter.16
  482.6 43.1 reduce-scatter.14
  529.6 45.2 all-gather.18
  589.9 42.5 reduce-scatter.18
  637.8 45.2 all-gather.20
  696.6 42.5 reduce-scatter.20
  744.1 45.2 all-gather.22
  803.9 42.5 reduce-scatter.22
  852.2 174.3 all-reduce.8
where the time goes:
time: 1060 us; the launch traced here: 1050 us
  waiting for transfers between devices  770 us (73%)
  matrix products  116 us (11%)
  other arithmetic  72.8 us (7%)
  blocking collectives  55.7 us (5%)
  local copies, waits for them, and re-layouts  18.6 us (2%)
  between operations  16.2 us (2%)
    psum x1, waiting for transfers between devices, local(): lax.psum(sharded_stack[0].astype(jnp.bfloat16), 'dp').astype(jnp.float32)  135 us
    all_gather x2, waiting for transfers between devices, local(): inputs_mid = lax.all_gather(normed_mid, 'mp', axis=0, tiled=True)  89.2 us
    all_gather x2, waiting for transfers between devices, local(): inputs = lax.all_gather(normed, 'mp', axis=0, tiled=True)  88 us
    reduce_scatter x2, waiting for transfers between devices, local(): lax.psum_scatter(ffn_term(jnp.int32(0), local_rows * lax.axis_size('mp'))...  86.7 us
    reduce_scatter x2, waiting for transfers between devices, local(): lax.psum_scatter(jnp.dot(mixed_rows, out_weight, preferred_element_type=j...  85.3 us
    all_gather x2, waiting for transfers between devices, local(): lax.all_gather(grad_branch, 'mp', axis=0, tiled=True)  84.7 us
    reduce_scatter x2, waiting for transfers between devices, local(): lax.psum_scatter(up_term(jnp.int32(0), local_rows * lax.axis_size('mp'))....  78.3 us
    all_gather x2, waiting for transfers between devices, local(): lax.all_gather(grad_attn_branch, 'mp', axis=0, tiled=True)  78.2 us
  transfers between devices with their start and end apart: 17, of which 17 were waited for; matrix products, arithmetic and copies ran while one was open for 6% of the time, Pallas kernels for 0%

commit v1 on v0

v1 whole, which is shorter than its diff:
```python
import functools

import jax
import jax.numpy as jnp
from jax import lax
from jax.experimental import pallas as pl
from jax.experimental.pallas import tpu as pltpu
from jax.sharding import Mesh
from jax.sharding import PartitionSpec as P

H = 8
HD = 128
LAYERS = 2
norm_eps = 1e-05
F32 = jnp.float32
BF16 = jnp.bfloat16


def gelu_tanh(values):
    return jax.nn.gelu(values, approximate=True)


def norm_parts(stream):
    centred = stream - jnp.mean(stream, axis=-1, keepdims=True)
    inverse = lax.rsqrt(jnp.mean(centred * centred, axis=-1, keepdims=True) + norm_eps)
    return centred * inverse, inverse


def norm_back(grad_normed, unit_rows, inverse, gain):
    scaled = grad_normed * gain
    return inverse * (
        scaled
        - jnp.mean(scaled, axis=-1, keepdims=True)
        - unit_rows * jnp.mean(scaled * unit_rows, axis=-1, keepdims=True)
    )


def dot(left, right):
    return jnp.dot(left, right, preferred_element_type=F32)


def dot_nt(left, right):
    return jnp.einsum("ti,oi->to", left, right, preferred_element_type=F32)


def dot_tn(left, right):
    return jnp.einsum("ti,to->io", left, right, preferred_element_type=F32)


def after(value, *others):
    return lax.optimization_barrier((value,) + others)[0]


def swap(value, axis):
    return lax.ppermute(value, axis, [(0, 1), (1, 0)])


def swap_one(value, axes):
    return lax.ppermute(value, axes, [(2, 3), (3, 2)])


def gather_rows(rows):
    if lax.axis_size("r") == 2:
        across = swap(rows, "r")
        beside = swap(rows, "c")
        return jnp.concatenate([rows, across, beside, swap(across, "c")], 0)
    mine = lax.all_gather(rows, "r", axis=0, tiled=True)
    return jnp.concatenate([mine, swap(mine, "c")], 0)


def axis_order(axis):
    size = lax.axis_size(axis)
    if size == 2:
        return [lax.axis_index(axis), 1 - lax.axis_index(axis)]
    return list(range(size))


def row_places(chunk, rows):
    pieces = []
    across = lax.axis_size("r")
    for core in axis_order("c"):
        for place in axis_order("r"):
            pieces.append(((chunk * across + place) * 2 + core) * rows + jnp.arange(rows, dtype=jnp.int32))
    return jnp.concatenate(pieces)


def scatter_rows(partial):
    half = partial.shape[0] // 2
    beside = swap(partial[half:], "c")
    if lax.axis_size("r") == 2:
        rows = half // 2
        send = (partial[rows:half].astype(F32) + beside[rows:].astype(F32)).astype(BF16)
        across = swap(send, "r")
        return partial[:rows].astype(F32) + beside[:rows].astype(F32) + across.astype(F32)
    total = (partial[:half].astype(F32) + beside.astype(F32)).astype(BF16)
    return lax.psum_scatter(total, "r", scatter_dimension=0, tiled=True).astype(F32)


def to_chunks(value):
    half = value.shape[0] // 2
    low, high = value[:half], value[half:]
    core, block = lax.axis_index("c"), lax.axis_index("b")
    first = jnp.where(block == 0, low, high)
    second = jnp.where(block == 0, high, low)
    first = lax.ppermute(first, ("c", "b"), [(0, 0), (1, 2), (2, 1), (3, 3)])
    second = lax.ppermute(second, ("c", "b"), [(0, 2), (1, 0), (2, 3), (3, 1)])
    return [jnp.where(core == 0, first, second), jnp.where(core == 0, second, first)]


def from_chunks(chunks):
    core, block = lax.axis_index("c"), lax.axis_index("b")
    first = jnp.where(core == 0, chunks[0], chunks[1])
    second = jnp.where(core == 0, chunks[1], chunks[0])
    first = lax.ppermute(first, ("c", "b"), [(0, 0), (2, 1), (1, 2), (3, 3)])
    second = lax.ppermute(second, ("c", "b"), [(2, 0), (0, 1), (3, 2), (1, 3)])
    low = jnp.where(block == 0, first, second)
    high = jnp.where(block == 0, second, first)
    return jnp.concatenate([low, high], 0)


def gather_axis(pieces, axis, only_last):
    size = lax.axis_size(axis)
    if size == 2:
        if only_last:
            other = [lax.ppermute(piece, (axis, "c"), [(1, 3), (3, 1)]) for piece in pieces]
        else:
            other = [swap(piece, axis) for piece in pieces]
        return [pieces, other]
    whole = [lax.all_gather(piece, axis, axis=0) for piece in pieces]
    return [[piece[place] for piece in whole] for place in range(size)]


def gather_plane(piece, axes, only_last):
    inner = [group[0] for group in gather_axis([piece], axes[1], only_last)]
    outer = gather_axis(inner, axes[0], only_last)
    width = lax.axis_size(axes[1])
    pieces, places = [], []
    for slow, group in zip(axis_order(axes[0]), outer):
        for fast, member in zip(axis_order(axes[1]), group):
            pieces.append(member)
            places.append(slow * width + fast)
    return pieces, places


def plane_place(axes):
    return lax.axis_index(axes[0]) * lax.axis_size(axes[1]) + lax.axis_index(axes[1])


def reduce_half(value, axis):
    if lax.axis_size(axis) == 2:
        index = lax.axis_index(axis)
        send = lax.dynamic_index_in_dim(value, 1 - index, 0, keepdims=False)
        keep = lax.dynamic_index_in_dim(value, index, 0, keepdims=False)
        return keep.astype(F32) + swap(send, axis).astype(F32)
    return lax.psum_scatter(value, axis, scatter_dimension=0, tiled=False).astype(F32)


def sum_small(value):
    for axis in ("c", "kx", "ky", "r", "b"):
        if lax.axis_size(axis) == 2:
            value = value + swap(value, axis)
        else:
            value = lax.psum(value, axis)
    return value


def place_kernel(count, rows, info, *refs):
    own, pieces, out, sems = refs[0], refs[1 : 1 + count], refs[1 + count], refs[2 + count]

    @pl.when(info[0] == 0)
    def _():
        copy = pltpu.make_async_copy(own, out, sems.at[0])
        copy.start()
        copy.wait()

    @pl.when(info[0] != 0)
    def _():
        copies = []
        for index in range(count):
            begin = pl.multiple_of(info[1 + index] * rows, rows)
            copies.append(pltpu.make_async_copy(pieces[index], out.at[pl.ds(begin, rows)], sems.at[index]))
        for copy in copies:
            copy.start()
        for copy in copies:
            copy.wait()


def place_pieces(own, pieces, places):
    count, rows = len(pieces), pieces[0].shape[0]
    core = lax.axis_index("c")
    info = jnp.stack([jnp.asarray(v, jnp.int32) for v in [core] + places])
    return pl.pallas_call(
        functools.partial(place_kernel, count, rows),
        out_shape=jax.ShapeDtypeStruct(own.shape, own.dtype),
        in_specs=[pl.BlockSpec(memory_space=pltpu.SMEM)] + [pl.BlockSpec(memory_space=pl.ANY)] * (1 + count),
        out_specs=pl.BlockSpec(memory_space=pl.ANY),
        scratch_shapes=[pltpu.SemaphoreType.DMA((count,))],
        cost_estimate=pl.CostEstimate(flops=0, bytes_accessed=2 * own.size * 2, transcendentals=0),
    )(info, own, *pieces)


def start_fetch(own, axes):
    count = lax.axis_size("ky") * lax.axis_size("kx")
    rows = own.shape[0] // count
    return lax.dynamic_slice_in_dim(own, plane_place(axes) * rows, rows, 0)


def finish_fetch(own, piece, axes):
    pieces, places = gather_plane(piece, axes, True)
    return place_pieces(own, pieces, places)


def reduce_plane(grad, axes):
    outer, inner = lax.axis_size(axes[0]), lax.axis_size(axes[1])
    rows, cols = grad.shape
    part = rows // (outer * inner)
    value = reduce_half(grad.reshape(outer, inner * part, cols), axes[0]).astype(BF16)
    value = reduce_half(value.reshape(inner, part, cols), axes[1])
    return value


def reduce_pair(value):
    core = lax.axis_index("c")
    half = value.shape[0] // 2
    low, high = value[:half], value[half:]
    send = jnp.where(core == 0, high, low).astype(BF16)
    got = lax.ppermute(send, ("c", "b"), [(2, 1), (3, 0), (0, 2), (1, 3)])
    far = swap_one(high.astype(BF16), ("c", "b"))
    return (jnp.where(core == 0, low, far.astype(F32)) + got.astype(F32)).astype(BF16)


def spread_weight(piece, axes):
    pieces, places = gather_plane(piece, axes, False)
    core = lax.axis_index("c")
    beside = [swap(member, "c") for member in pieces]
    return (
        pieces + beside,
        [place * 2 + core for place in places] + [place * 2 + 1 - core for place in places],
    )


def store_kernel(count, rows, column, layer, info, *refs):
    pieces = refs[:count]
    out, loaded, ready, in_sems, out_sems = refs[-5], refs[-4], refs[-3], refs[-2], refs[-1]
    width = out.shape[2]
    loads, stores = [], []
    for index in range(count):
        source = pieces[index].at[:, pl.ds(column, width)]
        loads.append(pltpu.make_async_copy(source, loaded.at[index], in_sems.at[index]))
        begin = pl.multiple_of(info[index] * rows, rows)
        stores.append(
            pltpu.make_async_copy(ready.at[index], out.at[layer, pl.ds(begin, rows)], out_sems.at[index])
        )
    for load in loads:
        load.start()
    for index in range(count):
        loads[index].wait()
        ready[index] = loaded[index].astype(F32)
        stores[index].start()
    for store in stores:
        store.wait()


def store_pieces(pieces, places, column, width, layer, before):
    count, rows = len(pieces), pieces[0].shape[0]
    info = jnp.stack([jnp.asarray(v, jnp.int32) for v in places])
    shape = jax.ShapeDtypeStruct((LAYERS, count * rows, width), F32)
    given = [] if before is None else [before]
    size = count * rows * width
    return pl.pallas_call(
        functools.partial(store_kernel, count, rows, column, layer),
        out_shape=shape,
        in_specs=[pl.BlockSpec(memory_space=pltpu.SMEM)]
        + [pl.BlockSpec(memory_space=pl.ANY)] * (count + len(given)),
        out_specs=pl.BlockSpec(memory_space=pl.ANY),
        scratch_shapes=[
            pltpu.VMEM((count, rows, width), BF16),
            pltpu.VMEM((count, rows, width), F32),
            pltpu.SemaphoreType.DMA((count,)),
            pltpu.SemaphoreType.DMA((count,)),
        ],
        input_output_aliases={} if before is None else {1 + count: 0},
        compiler_params=pltpu.CompilerParams(vmem_limit_bytes=size * 6 + (4 << 20)),
        cost_estimate=pl.CostEstimate(flops=0, bytes_accessed=size * 6, transcendentals=0),
    )(info, *pieces, *given)


def chunk_scores(query_heads, key_heads, query_pos, key_pos, query_seg, key_seg, slopes):
    logits = jnp.einsum("qhd,khd->hqk", query_heads, key_heads, preferred_element_type=F32) * HD ** (-0.5)
    distance = (query_pos[:, None] - key_pos[None, :]).astype(F32)
    logits = logits - slopes[:, None, None] * distance[None]
    allowed = (query_seg[:, None] == key_seg[None, :]) & (key_pos[None, :] <= query_pos[:, None])
    return jnp.where(allowed[None], logits, -1e30)


def heads_of(rows):
    return rows.reshape(rows.shape[0], -1, HD)


def attend(query, key, value, places, slopes):
    scores = chunk_scores(heads_of(query), heads_of(key), *places, slopes)
    row_max = jnp.max(scores, axis=-1, keepdims=True)
    weights = jnp.exp(scores - row_max)
    totals = jnp.sum(weights, axis=-1, keepdims=True)
    probabilities = (weights / totals).astype(BF16)
    mixed = jnp.einsum("hqk,khd->qhd", probabilities, heads_of(value), preferred_element_type=F32)
    return mixed.reshape(query.shape).astype(BF16), row_max + jnp.log(totals)


def attend_back(query, key, value, places, slopes, log_totals, grad_mixed):
    scale = HD ** (-0.5)
    query_heads, key_heads, value_heads, grad_heads = map(heads_of, (query, key, value, grad_mixed))
    scores = chunk_scores(query_heads, key_heads, *places, slopes)
    probabilities = jnp.exp(scores - log_totals)
    rounded = probabilities.astype(BF16)
    grad_value = jnp.einsum("hqk,qhd->khd", rounded, grad_heads, preferred_element_type=F32)
    grad_probs = jnp.einsum("qhd,khd->hqk", grad_heads, value_heads, preferred_element_type=F32)
    centre = jnp.sum(grad_probs * probabilities, axis=-1, keepdims=True)
    grad_scores = (probabilities * (grad_probs - centre)).astype(BF16)
    grad_query = jnp.einsum("hqk,khd->qhd", grad_scores, key_heads, preferred_element_type=F32) * scale
    grad_key = jnp.einsum("hqk,qhd->khd", grad_scores, query_heads, preferred_element_type=F32) * scale
    return (
        grad_query.reshape(query.shape).astype(BF16),
        grad_key.reshape(key.shape),
        grad_value.reshape(value.shape),
    )


def local(
    activations,
    lengths,
    cotangent,
    gain_attn,
    shift_attn,
    w_query,
    b_query,
    w_key,
    w_value,
    b_value,
    w_out,
    b_out,
    gain_ffn,
    shift_ffn,
    w_up,
    b_up,
    w_down,
    b_down,
):
    core, block, place = lax.axis_index("c"), lax.axis_index("b"), lax.axis_index("r")
    across = lax.axis_size("r")
    shard = ((block + core) % 2) * across + place
    home = block * across + place
    rows = activations.shape[0] // 2
    head_width = w_query.shape[2]
    head_count = head_width // HD
    hidden_width = w_up.shape[2]

    doc_ends = jnp.cumsum(jnp.where(core == block, lengths[0], swap(lengths[0], "c")))
    places, segments = [], []
    for chunk in range(2):
        spots = row_places(chunk, rows)
        places.append(spots)
        segments.append(jnp.sum((spots[:, None] >= doc_ends[None, :]).astype(jnp.int32), axis=1))
    places_both = jnp.concatenate(places)
    segments_both = jnp.concatenate(segments)
    spot_sets = [
        (places[0], places[0], segments[0], segments[0]),
        (places[1], places_both, segments[1], segments_both),
    ]
    head_ids = (shard * head_count + jnp.arange(head_count, dtype=jnp.int32)).astype(F32)
    slopes = 2.0 ** (-8.0 * (head_ids + 1.0) / H)

    streams = [value.astype(F32) for value in to_chunks(activations)]

    bias_own = jnp.concatenate([b_query, b_value], 1)
    bias_use = jnp.where(core == 0, bias_own, swap_one(bias_own, ("c", "b")))
    zero = jnp.zeros((head_width,), F32)
    bias_qkv = [
        jnp.concatenate([bias_use[layer, :head_width], zero, bias_use[layer, head_width:]])
        for layer in range(LAYERS)
    ]
    bias_up = [
        lax.dynamic_slice_in_dim(b_up[layer], shard * hidden_width, hidden_width, 0) for layer in range(LAYERS)
    ]

    yx, xy = ("ky", "kx"), ("kx", "ky")
    used = []
    previous = streams[0]
    for layer in range(LAYERS):
        owns = [
            (jnp.concatenate([w_query[layer], w_key[layer], w_value[layer]], 1), yx),
            (w_out[layer], xy),
            (w_up[layer], yx),
            (w_down[layer], xy),
        ]
        members = []
        for own, axes in owns:
            piece = after(start_fetch(own, axes), previous)
            piece = swap_one(piece, ("c", "b"))
            previous = piece
            members.append(finish_fetch(own, piece, axes))
        used.append(members)

    stored = []
    for layer in range(LAYERS):
        weight_qkv, weight_out, weight_up, weight_down = used[layer]
        saved = []
        for chunk in range(2):
            stream = streams[chunk]
            unit, inverse = norm_parts(stream)
            normed = (unit * gain_attn[layer] + shift_attn[layer]).astype(BF16)
            inputs = gather_rows(normed)
            qkv = (dot(inputs, weight_qkv) + bias_qkv[layer]).astype(BF16)
            query, key, value = (
                qkv[:, :head_width],
                qkv[:, head_width : 2 * head_width],
                qkv[:, 2 * head_width :],
            )
            if chunk == 1:
                key = jnp.concatenate([saved[0][4], key], 0)
                value = jnp.concatenate([saved[0][5], value], 0)
            mixed, log_totals = attend(query, key, value, spot_sets[chunk], slopes)
            middle = stream + (scatter_rows(dot(mixed, weight_out).astype(BF16)) + b_out[layer])
            unit_mid, inverse_mid = norm_parts(middle)
            normed_mid = (unit_mid * gain_ffn[layer] + shift_ffn[layer]).astype(BF16)
            inputs_mid = gather_rows(normed_mid)
            hidden = dot(inputs_mid, weight_up) + bias_up[layer]
            active = gelu_tanh(hidden).astype(BF16)
            streams[chunk] = middle + (scatter_rows(dot(active, weight_down).astype(BF16)) + b_down[layer])
            saved.append(
                (
                    unit,
                    inverse,
                    inputs,
                    query,
                    key,
                    value,
                    mixed,
                    log_totals,
                    unit_mid,
                    inverse_mid,
                    inputs_mid,
                    hidden,
                    active,
                )
            )
        stored.append(saved)
    activations_out = from_chunks([value.astype(BF16) for value in streams])

    grads = [value.astype(F32) for value in to_chunks(cotangent)]
    outs = [None] * 6
    small = [None] * LAYERS
    for layer in reversed(range(LAYERS)):
        weight_qkv, weight_out, weight_up, weight_down = used[layer]
        sums = {}

        def add(name, value):
            sums[name] = value if name not in sums else sums[name] + value

        key_carry = value_carry = None
        for chunk in (1, 0):
            (
                unit,
                inverse,
                inputs,
                query,
                key,
                value,
                mixed,
                log_totals,
                unit_mid,
                inverse_mid,
                inputs_mid,
                hidden,
                active,
            ) = stored[layer][chunk]
            grad_stream = grads[chunk]
            grad_branch = grad_stream.astype(BF16)
            add("b_down", jnp.sum(grad_branch, axis=0, dtype=F32))
            branch_all = gather_rows(grad_branch)
            grad_active = dot_nt(branch_all, weight_down)
            grad_hidden = jax.vjp(gelu_tanh, hidden)[1](grad_active)[0].astype(BF16)
            add("w_down", dot_tn(active, branch_all))
            add("b_up", jnp.sum(grad_hidden, axis=0, dtype=F32))
            grad_normed_mid = scatter_rows(dot_nt(grad_hidden, weight_up).astype(BF16))
            add("w_up", dot_tn(inputs_mid, grad_hidden))
            add("gain_ffn", jnp.sum(grad_normed_mid * unit_mid, axis=0))
            add("shift_ffn", jnp.sum(grad_normed_mid, axis=0))
            grad_middle = grad_stream + norm_back(grad_normed_mid, unit_mid, inverse_mid, gain_ffn[layer])
            grad_attn = grad_middle.astype(BF16)
            add("b_out", jnp.sum(grad_attn, axis=0, dtype=F32))
            attn_all = gather_rows(grad_attn)
            grad_mixed = dot_nt(attn_all, weight_out).astype(BF16)
            add("w_out", dot_tn(mixed, attn_all))
            grad_query, grad_key, grad_value = attend_back(
                query, key, value, spot_sets[chunk], slopes, log_totals, grad_mixed
            )
            chunk_rows = query.shape[0]
            if chunk == 1:
                key_carry, value_carry = grad_key[:chunk_rows], grad_value[:chunk_rows]
                grad_key, grad_value = grad_key[chunk_rows:], grad_value[chunk_rows:]
            else:
                grad_key, grad_value = grad_key + key_carry, grad_value + value_carry
            grad_qkv = jnp.concatenate([grad_query, grad_key.astype(BF16), grad_value.astype(BF16)], 1)
            add("b_qkv", jnp.sum(grad_qkv, axis=0, dtype=F32))
            grad_normed = scatter_rows(dot_nt(grad_qkv, weight_qkv).astype(BF16))
            add("w_qkv", dot_tn(inputs, grad_qkv))
            add("gain_attn", jnp.sum(grad_normed * unit, axis=0))
            add("shift_attn", jnp.sum(grad_normed, axis=0))
            grads[chunk] = grad_middle + norm_back(grad_normed, unit, inverse, gain_attn[layer])

        for name, axes, members in (
            ("w_down", xy, ((5, 0, w_down.shape[2]),)),
            ("w_up", yx, ((4, 0, hidden_width),)),
            ("w_out", xy, ((3, 0, w_out.shape[2]),)),
            ("w_qkv", yx, tuple((index, index * head_width, head_width) for index in range(3))),
        ):
            piece = reduce_pair(reduce_plane(sums[name].astype(BF16), axes))
            pieces, spots = spread_weight(piece, axes)
            for index, column, width in members:
                outs[index] = store_pieces(pieces, spots, column, width, layer, outs[index])

        def spread(values, total):
            return lax.dynamic_update_slice_in_dim(
                jnp.zeros((total,), F32), values, shard * values.shape[0], 0
            )

        whole = head_width * 2 * across
        packed = jnp.concatenate(
            [sums[name] for name in ("gain_attn", "shift_attn", "b_out", "gain_ffn", "shift_ffn", "b_down")]
            + [
                spread(sums["b_qkv"][:head_width], whole),
                spread(sums["b_qkv"][2 * head_width :], whole),
                spread(sums["b_up"], b_up.shape[1]),
            ]
        )
        small[layer] = sum_small(packed.reshape(-1, 128)).reshape(-1)

    input_grad = from_chunks([value.astype(BF16) for value in grads])
    table = jnp.stack(small)
    wide = gain_attn.shape[1]
    shared = [table[:, index * wide : (index + 1) * wide] for index in range(6)]
    begin = 6 * wide
    whole = head_width * 2 * across
    grad_b_query = lax.dynamic_slice_in_dim(table[:, begin : begin + whole], home * head_width, head_width, 1)
    begin += whole
    grad_b_value = lax.dynamic_slice_in_dim(table[:, begin : begin + whole], home * head_width, head_width, 1)
    begin += whole
    grad_b_up = lax.dynamic_slice_in_dim(table[:, begin:], home * hidden_width, hidden_width, 1)
    return (
        activations_out,
        input_grad,
        shared[0],
        shared[1],
        outs[0],
        grad_b_query,
        outs[1],
        outs[2],
        grad_b_value,
        outs[3],
        shared[2],
        shared[3],
        shared[4],
        outs[4],
        grad_b_up,
        outs[5],
        shared[5],
    )


def solution(mesh):
    groups, parts = mesh.shape["dp"], mesh.shape["mp"]
    fine = Mesh(
        mesh.devices.reshape(2, groups // 4, 2, 2, parts // 2), ("ky", "kx", "c", "b", "r")
    )
    dp, mp = ("ky", "kx", "c"), ("b", "r")
    rows, whole = P(dp + mp, None), P()
    columns3, columns2, rows3 = P(None, None, mp), P(None, mp), P(None, mp, None)
    return jax.shard_map(
        local,
        mesh=fine,
        in_specs=(
            rows,
            P(dp, None),
            rows,
            whole,
            whole,
            columns3,
            columns2,
            columns3,
            columns3,
            columns2,
            rows3,
            whole,
            whole,
            whole,
            columns3,
            whole,
            rows3,
            whole,
        ),
        out_specs=(
            rows,
            rows,
            whole,
            whole,
            columns3,
            columns2,
            columns3,
            columns3,
            columns2,
            rows3,
            whole,
            whole,
            whole,
            columns3,
            columns2,
            rows3,
            whole,
        ),
        check_vma=False,
    )
```

time: 1060 us -> 1140 us (1.075)
  waiting for transfers between devices: 770 us -> 250 us
  Pallas kernels: 0 us -> 422 us
  starting transfers between devices: 2.34 us -> 227 us
  blocking collectives: 55.7 us -> 0 us
  local copies, waits for them, and re-layouts: 18.6 us -> 69.6 us
  other arithmetic: 72.8 us -> 45.9 us
    pallas_call x0 -> x20, Pallas kernels: none -> 422 us  [the longest x8 396 us: place_pieces(): pl.pallas_call(functools.partial(place_kernel, count, rows), out_shape=ja...]
    all_gather x8 -> x0, waiting for transfers between devices: 340 us -> none  [the longest x2 89.2 us: local(): inputs_mid = lax.all_gather(normed_mid, 'mp', axis=0, tiled=True)]
    reduce_scatter x8 -> x0, waiting for transfers between devices: 294 us -> none  [the longest x2 86.7 us: local(): lax.psum_scatter(ffn_term(jnp.int32(0), local_rows * lax.axis_size('mp'))...]
    ppermute x0 -> x220, waiting for transfers between devices: none -> 250 us  [the longest x163 226 us: swap(): return lax.ppermute(value, axis, [(0, 1), (1, 0)])]
    ppermute x0 -> x220, starting transfers between devices: none -> 227 us  [the longest x163 157 us: swap(): return lax.ppermute(value, axis, [(0, 1), (1, 0)])]
    psum x1 -> x0, waiting for transfers between devices: 135 us -> none  [local(): lax.psum(sharded_stack[0].astype(jnp.bfloat16), 'dp').astype(jnp.float32)]
    psum x2 -> x0, blocking collectives: 55.7 us -> none  [the longest x1 41.4 us: local(): lax.psum((shared_stack[0], shared_stack[1], shared_stack[2], shared_stack...]
    convert_element_type x20 -> x42, other arithmetic: 33.5 us -> 15.4 us  [the longest x16 5.51 us: scatter_rows(): (partial[rows:half].astype(F32) + beside[rows:].astype(F32)).astype(BF16)]
  transfers between devices with their start and end apart: 17 -> 220, of which waited for: 17 -> 48; matrix products, arithmetic and copies ran while one was open for 6% -> 16% of each run, Pallas kernels for 0% -> 31%
where the time goes in v1:
time: 1140 us; the launch traced here: 1130 us
  Pallas kernels  422 us (37%)
  waiting for transfers between devices  250 us (22%)
  starting transfers between devices  227 us (20%)
  matrix products  113 us (10%)
  local copies, waits for them, and re-layouts  69.6 us (6%)
  other arithmetic  45.9 us (4%)
    pallas_call x8, Pallas kernels, place_pieces(): pl.pallas_call(functools.partial(place_kernel, count, rows), out_shape=ja...  396 us
    ppermute x163, waiting for transfers between devices, swap(): return lax.ppermute(value, axis, [(0, 1), (1, 0)])  226 us
    ppermute x163, starting transfers between devices, swap(): return lax.ppermute(value, axis, [(0, 1), (1, 0)])  157 us
    dot_general x16, matrix products, dot(): return jnp.dot(left, right, preferred_element_type=F32)  34.7 us
    ppermute x24, starting transfers between devices, gather_axis(): lax.ppermute(piece, (axis, 'c'), [(1, 3), (3, 1)])  28.4 us
    dot_general x16, matrix products, dot_tn(): return jnp.einsum('ti,to->io', left, right, preferred_element_type=F32)  27.9 us
    dot_general x16, matrix products, dot_nt(): return jnp.einsum('ti,oi->to', left, right, preferred_element_type=F32)  26.7 us
    pallas_call x12, Pallas kernels, store_pieces(): pl.pallas_call(functools.partial(store_kernel, count, rows, column, layer...  26.4 us
  transfers between devices with their start and end apart: 220, of which 48 were waited for; matrix products, arithmetic and copies ran while one was open for 16% of the time, Pallas kernels for 31%

profile of v1, /device:TPU:0, one launch (start us, length us, event | category | flops | bytes accessed | tf_op | source)
XLA Modules:
  0.0 1132.7 jit_solution(13954190582797969310)
XLA Ops:
  12.0 4.8 collective-permute-start.1
  26.1 4.5 fusion.190
  52.9 14.3 %collective-permute-start.57 = (bf16[128,1024]{1,0:T(8,128)(2,1)}, bf16[128,1024]{1,0:T(8,128)(2,1)}, u32[]{:S(2)}, u32[]{:S(2)}) collective-permute-start(bf16[128,1024]{1,0:T(8,128)(2,1)} %get-tuple-element.188), channel_id=1, source_target_pairs={{0,4},{4,0},{1,5},{5,1},{2,6},{6,2},{3,7},{7,3},{8,12},{12,8},{9,1... | collective-permute-start | bytes 786440 | tf_op jit(solution)/shard_map/ppermute | solution.py:55
  69.2 17.7 %shard_map.306 = bf16[256,1024]{1,0:T(8,128)(2,1)} custom-call(s32[5]{0:T(128)} %stack.70.info, bf16[256,1024]{1,0:T(8,128)(2,1)} %get-tuple-element.128.refs_0_, bf16[64,1024]{1,0:T(8,128)(2,1)} %copy-done.102, bf16[64,1024]{1,0:T(8,128)(2,1)} %copy-done.103, bf16[64,1024]{1,0:T(8,128)(2,1)} %copy-done.104, bf16[64,1024]{1,0:T(8,128)(2,1)} %copy-done.105), custom_call_target="tpu_custom_call" | custom-call | bytes 1048576 | tf_op jit(solution)/shard_map/pallas_call | solution.py:192
  87.4 49.4 %shard_map.305 = bf16[1024,768]{1,0:T(8,128)(2,1)} custom-call(s32[5]{0:T(128)} %stack.65.info, bf16[1024,768]{1,0:T(8,128)(2,1)} %copy-done.24, bf16[256,768]{1,0:T(8,128)(2,1)} %collective-permute-done.5.refs_1_, bf16[256,768]{1,0:T(8,128)(2,1)} %collective-permute-done.6.refs_2_, bf16[256,768]{1,0:T(8,128)(2,1)} %collective-permute-done.7.refs_3_, ...), custom_call_target="tpu_custom_call" | custom-call | bytes 3145728 | tf_op jit(solution)/shard_map/pallas_call | solution.py:192
  180.1 5.8 collective-permute-done.60
  185.9 7.9 collective-permute-done.16
  199.9 8.5 collective-permute-start.62
  211.5 65.3 %shard_map.307 = bf16[1024,1024]{1,0:T(8,128)(2,1)} custom-call(s32[5]{0:T(128)} %stack.65.info, bf16[1024,1024]{1,0:T(8,128)(2,1)} %get-tuple-element.112.refs_0_, bf16[256,1024]{1,0:T(8,128)(2,1)} %copy-done.78, bf16[256,1024]{1,0:T(8,128)(2,1)} %collective-permute-done.21.refs_2_, bf16[256,1024]{1,0:T(8,128)(2,1)} %copy-done.79, ...), custom_call_target="tpu_custom_call" | custom-call | bytes 4194304 | tf_op jit(solution)/shard_map/pallas_call | solution.py:192
  276.8 10.6 collective-permute-start.18
  290.1 4.4 fusion.128
  298.5 65.3 %shard_map.308 = bf16[1024,1024]{1,0:T(8,128)(2,1)} custom-call(s32[5]{0:T(128)} %stack.70.info, bf16[1024,1024]{1,0:T(8,128)(2,1)} %get-tuple-element.116.refs_0_, bf16[256,1024]{1,0:T(8,128)(2,1)} %collective-permute-done.24.refs_1_, bf16[256,1024]{1,0:T(8,128)(2,1)} %collective-permute-done.25.refs_2_, bf16[256,1024]{1,0:T(8,128)(2,1)} %collective-permute-done.26.refs_3_, ...), custom_call_target="tpu_custom_call" | custom-call | bytes 4194304 | tf_op jit(solution)/shard_map/pallas_call | solution.py:192
  378.3 6.8 collective-permute-done.65
  385.1 7.0 collective-permute-done.29
  399.2 11.2 collective-permute-start.67
  412.3 17.7 %shard_map.310 = bf16[256,1024]{1,0:T(8,128)(2,1)} custom-call(s32[5]{0:T(128)} %stack.70.info, bf16[256,1024]{1,0:T(8,128)(2,1)} %get-tuple-element.129.refs_0_, bf16[64,1024]{1,0:T(8,128)(2,1)} %copy-done.100, bf16[64,1024]{1,0:T(8,128)(2,1)} %copy-done.101, bf16[64,1024]{1,0:T(8,128)(2,1)} %copy-done.106, bf16[64,1024]{1,0:T(8,128)(2,1)} %copy-done.107), custom_call_target="tpu_custom_call" | custom-call | bytes 1048576 | tf_op jit(solution)/shard_map/pallas_call | solution.py:192
  432.8 49.4 %shard_map.309 = bf16[1024,768]{1,0:T(8,128)(2,1)} custom-call(s32[5]{0:T(128)} %stack.65.info, bf16[1024,768]{1,0:T(8,128)(2,1)} %copy-done.25, bf16[256,768]{1,0:T(8,128)(2,1)} %collective-permute-done.33.refs_1_, bf16[256,768]{1,0:T(8,128)(2,1)} %collective-permute-done.34.refs_2_, bf16[256,768]{1,0:T(8,128)(2,1)} %copy-done.82, bf16[256,768]{1,0:T(8,128)(2,1)} %copy-done.83), custom_call_target="tpu_custom_call" | custom-call | bytes 3145728 | tf_op jit(solution)/shard_map/pallas_call | solution.py:192
  529.3 9.4 collective-permute-done.42
  545.4 65.3 %shard_map.311 = bf16[1024,1024]{1,0:T(8,128)(2,1)} custom-call(s32[5]{0:T(128)} %stack.65.info, bf16[1024,1024]{1,0:T(8,128)(2,1)} %get-tuple-element.111.refs_0_, bf16[256,1024]{1,0:T(8,128)(2,1)} %collective-permute-done.46.refs_1_, bf16[256,1024]{1,0:T(8,128)(2,1)} %collective-permute-done.47.refs_2_, bf16[256,1024]{1,0:T(8,128)(2,1)} %collective-permute-done.48.refs_3_, ...), custom_call_target="tpu_custom_call" | custom-call | bytes 4194304 | tf_op jit(solution)/shard_map/pallas_call | solution.py:192
  610.8 10.5 collective-permute-start.44
  623.7 65.3 %shard_map.312 = bf16[1024,1024]{1,0:T(8,128)(2,1)} custom-call(s32[5]{0:T(128)} %stack.70.info, bf16[1024,1024]{1,0:T(8,128)(2,1)} %get-tuple-element.117.refs_0_, bf16[256,1024]{1,0:T(8,128)(2,1)} %collective-permute-done.50.refs_1_, bf16[256,1024]{1,0:T(8,128)(2,1)} %collective-permute-done.51.refs_2_, bf16[256,1024]{1,0:T(8,128)(2,1)} %collective-permute-done.52.refs_3_, ...), custom_call_target="tpu_custom_call" | custom-call | bytes 4194304 | tf_op jit(solution)/shard_map/pallas_call | solution.py:192
  707.7 4.0 convert_reduce_fusion
  728.1 12.2 %collective-permute-done.92 = bf16[128,1024]{1,0:T(8,128)(2,1)S(1)} collective-permute-done((bf16[128,1024]{1,0:T(8,128)(2,1)S(1)}, bf16[128,1024]{1,0:T(8,128)(2,1)S(1)}, u32[]{:S(2)}, u32[]{:S(2)}) %collective-permute-start.92) | collective-permute-done | bytes 262176 | tf_op jit(solution)/shard_map/ppermute | solution.py:55
  740.9 9.1 collective-permute-done.84
  752.5 4.7 collective-permute-start.77
  760.0 8.6 collective-permute-start.86
  798.0 19.1 %collective-permute-done.166 = bf16[64,1024]{1,0:T(8,128)(2,1)S(1)} collective-permute-done((bf16[64,1024]{1,0:T(8,128)(2,1)S(1)}, bf16[64,1024]{1,0:T(8,128)(2,1)S(1)}, u32[]{:S(2)}, u32[]{:S(2)}) %collective-permute-start.166) | collective-permute-done | bytes 131104 | tf_op jit(solution)/shard_map/ppermute | solution.py:55
  825.4 10.4 collective-permute-done.107
  836.2 8.3 collective-permute-done.97
  857.3 12.2 %collective-permute-done.130 = f32[96,128]{1,0:T(8,128)S(1)} collective-permute-done((f32[96,128]{1,0:T(8,128)S(1)}, f32[96,128]{1,0:T(8,128)S(1)}, u32[]{:S(2)}, u32[]{:S(2)}) %collective-permute-start.130) | collective-permute-done | bytes 49184 | tf_op jit(solution)/shard_map/ppermute | solution.py:55
  881.1 4.0 convert_reduce_fusion.2
  898.8 6.9 collective-permute-done.112
  906.1 4.0 collective-permute-done.102
  911.5 9.3 collective-permute-done.176
  922.9 5.6 collective-permute-done.103
  950.8 7.5 collective-permute-done.154
  965.8 9.3 collective-permute-done.157
  979.5 4.7 collective-permute-done.119
  995.4 5.6 collective-permute-done.213.refs_1_
  1001.0 5.4 collective-permute-done.201
  1012.1 5.7 collective-permute-done.132
  1018.5 4.0 collective-permute-done.193.refs_3_
  1025.2 5.7 collective-permute-done.147.refs_1_
  1033.5 5.1 collective-permute-done.148.refs_2_
  1050.6 6.3 collective-permute-done.160.refs_3_
  1061.3 4.1 collective-permute-done.133
  1075.2 4.8 collective-permute-done.126
  1088.1 4.3 collective-permute-start.121
  (1123 shorter events, 434.8 us)
Async XLA Ops:
  7.4 34.0 %collective-permute-start.5 = (bf16[256,768]{1,0:T(8,128)(2,1)}, bf16[256,768]{1,0:T(8,128)(2,1)}, u32[]{:S(2)}, u32[]{:S(2)}) collective-permute-start(bf16[256,768]{1,0:T(8,128)(2,1)} %constant_dynamic-slice_fusion.7), channel_id=1, source_target_pairs={{4,6},{6,4},{5,7},{7,5},{12,14},{14,12},{13,15},{15,13},{20,22},{2... | collective-permute-start | bytes 1179656 | tf_op jit(solution)/shard_map/ppermute | solution.py:59
  10.0 39.3 %collective-permute-start.9 = (f32[2,512]{1,0:T(2,128)}, f32[2,512]{1,0:T(2,128)}, u32[]{:S(2)}, u32[]{:S(2)}) collective-permute-start(f32[2,512]{1,0:T(2,128)} %constant_dynamic-update-slice_fusion), channel_id=1, source_target_pairs={{4,6},{6,4},{5,7},{7,5},{12,14},{14,12},{13,15},{15,13},{20,22},{2... | collective-permute-start | bytes 12296 | tf_op jit(solution)/shard_map/ppermute | solution.py:59
  12.0 27.7 %collective-permute-start.1 = (bf16[128,1024]{1,0:T(8,128)(2,1)}, bf16[128,1024]{1,0:T(8,128)(2,1)}, u32[]{:S(2)}, u32[]{:S(2)}) collective-permute-start(bf16[128,1024]{1,0:T(8,128)(2,1)} %get-tuple-element.165), channel_id=1, source_target_pairs={{0,4},{2,0},{4,6},{6,2},{1,5},{3,1},{5,7},{7,3},{8,12},{10,8},{12,... | collective-permute-start | bytes 786440 | tf_op jit(solution)/shard_map/ppermute | solution.py:106
  47.8 39.2 %collective-permute-start.7 = (bf16[256,768]{1,0:T(8,128)(2,1)}, bf16[256,768]{1,0:T(8,128)(2,1)}, u32[]{:S(2)}, u32[]{:S(2)}) collective-permute-start(bf16[256,768]{1,0:T(8,128)(2,1)} %collective-permute-done.5.refs_1_), channel_id=1, source_target_pairs={{4,20},{20,4},{5,21},{21,5},{6,22},{22,6},{7,23},{23,7},{12,28},{2... | collective-permute-start | bytes 1179656 | tf_op jit(solution)/shard_map/ppermute | solution.py:125
  50.6 36.9 %collective-permute-start.8 = (bf16[256,768]{1,0:T(8,128)(2,1)}, bf16[256,768]{1,0:T(8,128)(2,1)}, u32[]{:S(2)}, u32[]{:S(2)}) collective-permute-start(bf16[256,768]{1,0:T(8,128)(2,1)} %collective-permute-done.6.refs_2_), channel_id=1, source_target_pairs={{4,20},{20,4},{5,21},{21,5},{6,22},{22,6},{7,23},{23,7},{12,28},{2... | collective-permute-start | bytes 1179656 | tf_op jit(solution)/shard_map/ppermute | solution.py:125
  52.9 84.0 %collective-permute-start.57 = (bf16[128,1024]{1,0:T(8,128)(2,1)}, bf16[128,1024]{1,0:T(8,128)(2,1)}, u32[]{:S(2)}, u32[]{:S(2)}) collective-permute-start(bf16[128,1024]{1,0:T(8,128)(2,1)} %get-tuple-element.188), channel_id=1, source_target_pairs={{0,4},{4,0},{1,5},{5,1},{2,6},{6,2},{3,7},{7,3},{8,12},{12,8},{9,1... | collective-permute-start | bytes 786440 | tf_op jit(solution)/shard_map/ppermute | solution.py:55
  67.9 69.0 %collective-permute-start.58 = (bf16[128,1024]{1,0:T(8,128)(2,1)}, bf16[128,1024]{1,0:T(8,128)(2,1)}, u32[]{:S(2)}, u32[]{:S(2)}) collective-permute-start(bf16[128,1024]{1,0:T(8,128)(2,1)} %collective-permute-done.56), channel_id=1, source_target_pairs={{0,4},{4,0},{1,5},{5,1},{2,6},{6,2},{3,7},{7,3},{8,12},{12,8},{9,1... | collective-permute-start | bytes 786440 | tf_op jit(solution)/shard_map/ppermute | solution.py:55
  86.9 55.5 %collective-permute-start.3 = (bf16[128,1024]{1,0:T(8,128)(2,1)}, bf16[128,1024]{1,0:T(8,128)(2,1)}, u32[]{:S(2)}, u32[]{:S(2)}) collective-permute-start(bf16[128,1024]{1,0:T(8,128)(2,1)} %get-tuple-element.189), channel_id=1, source_target_pairs={{0,4},{4,0},{1,5},{5,1},{2,6},{6,2},{3,7},{7,3},{8,12},{12,8},{9,1... | collective-permute-start | bytes 786440 | tf_op jit(solution)/shard_map/ppermute | solution.py:55
  87.0 55.4 %collective-permute-start.4 = (bf16[128,1024]{1,0:T(8,128)(2,1)}, bf16[128,1024]{1,0:T(8,128)(2,1)}, u32[]{:S(2)}, u32[]{:S(2)}) collective-permute-start(bf16[128,1024]{1,0:T(8,128)(2,1)} %collective-permute-done.2), channel_id=1, source_target_pairs={{0,4},{4,0},{1,5},{5,1},{2,6},{6,2},{3,7},{7,3},{8,12},{12,8},{9,1... | collective-permute-start | bytes 786440 | tf_op jit(solution)/shard_map/ppermute | solution.py:55
  179.4 29.0 %collective-permute-start.22 = (bf16[256,1024]{1,0:T(8,128)(2,1)S(1)}, bf16[256,1024]{1,0:T(8,128)(2,1)S(1)}, u32[]{:S(2)}, u32[]{:S(2)}) collective-permute-start(bf16[256,1024]{1,0:T(8,128)(2,1)S(1)} %collective-permute-done.20.refs_1_), channel_id=1, source_target_pairs={{4,20},{20,4},{5,21},{21,5},{6,22},{22,6},{7,23},{23,7},{12,28},{2... | collective-permute-start | bytes 1572872 | tf_op jit(solution)/shard_map/ppermute | solution.py:125
  197.0 79.9 %collective-permute-start.25 = (bf16[256,1024]{1,0:T(8,128)(2,1)}, bf16[256,1024]{1,0:T(8,128)(2,1)}, u32[]{:S(2)}, u32[]{:S(2)}) collective-permute-start(bf16[256,1024]{1,0:T(8,128)(2,1)} %collective-permute-done.24.refs_1_), channel_id=1, source_target_pairs={{4,20},{20,4},{5,21},{21,5},{6,22},{22,6},{7,23},{23,7},{12,28},{2... | collective-permute-start | bytes 1572872 | tf_op jit(solution)/shard_map/ppermute | solution.py:125
  199.9 87.6 %collective-permute-start.62 = (bf16[128,1024]{1,0:T(8,128)(2,1)S(1)}, bf16[128,1024]{1,0:T(8,128)(2,1)}, u32[]{:S(2)}, u32[]{:S(2)}) collective-permute-start(bf16[128,1024]{1,0:T(8,128)(2,1)S(1)} %get-tuple-element.186), channel_id=1, source_target_pairs={{0,4},{4,0},{1,5},{5,1},{2,6},{6,2},{3,7},{7,3},{8,12},{12,8},{9,1... | collective-permute-start | bytes 786440 | tf_op jit(solution)/shard_map/ppermute | solution.py:55
  209.3 79.9 %collective-permute-start.17 = (bf16[128,1024]{1,0:T(8,128)(2,1)}, bf16[128,1024]{1,0:T(8,128)(2,1)}, u32[]{:S(2)}, u32[]{:S(2)}) collective-permute-start(bf16[128,1024]{1,0:T(8,128)(2,1)} %get-tuple-element.187), channel_id=1, source_target_pairs={{0,1},{1,0},{2,3},{3,2},{4,5},{5,4},{6,7},{7,6},{8,9},{9,8},{10,11... | collective-permute-start | bytes 786440 | tf_op jit(solution)/shard_map/ppermute | solution.py:55
  209.3 80.8 %collective-permute-start.63 = (bf16[128,1024]{1,0:T(8,128)(2,1)}, bf16[128,1024]{1,0:T(8,128)(2,1)}, u32[]{:S(2)}, u32[]{:S(2)}) collective-permute-start(bf16[128,1024]{1,0:T(8,128)(2,1)} %collective-permute-done.61), channel_id=1, source_target_pairs={{0,4},{4,0},{1,5},{5,1},{2,6},{6,2},{3,7},{7,3},{8,12},{12,8},{9,1... | collective-permute-start | bytes 786440 | tf_op jit(solution)/shard_map/ppermute | solution.py:55
  210.0 88.5 %collective-permute-start.26 = (bf16[256,1024]{1,0:T(8,128)(2,1)}, bf16[256,1024]{1,0:T(8,128)(2,1)}, u32[]{:S(2)}, u32[]{:S(2)}) collective-permute-start(bf16[256,1024]{1,0:T(8,128)(2,1)} %collective-permute-done.24.refs_1_), channel_id=1, source_target_pairs={{4,12},{12,4},{5,13},{13,5},{6,14},{14,6},{7,15},{15,7},{20,28},{2... | collective-permute-start | bytes 1572872 | tf_op jit(solution)/shard_map/ppermute | solution.py:125
  394.3 35.8 %collective-permute-start.35 = (bf16[256,768]{1,0:T(8,128)(2,1)}, bf16[256,768]{1,0:T(8,128)(2,1)S(1)}, u32[]{:S(2)}, u32[]{:S(2)}) collective-permute-start(bf16[256,768]{1,0:T(8,128)(2,1)} %collective-permute-done.33.refs_1_), channel_id=1, source_target_pairs={{4,20},{20,4},{5,21},{21,5},{6,22},{22,6},{7,23},{23,7},{12,28},{2... | collective-permute-start | bytes 1179656 | tf_op jit(solution)/shard_map/ppermute | solution.py:125
  395.0 37.0 %collective-permute-start.36 = (bf16[256,768]{1,0:T(8,128)(2,1)}, bf16[256,768]{1,0:T(8,128)(2,1)S(1)}, u32[]{:S(2)}, u32[]{:S(2)}) collective-permute-start(bf16[256,768]{1,0:T(8,128)(2,1)} %collective-permute-done.34.refs_2_), channel_id=1, source_target_pairs={{4,20},{20,4},{5,21},{21,5},{6,22},{22,6},{7,23},{23,7},{12,28},{2... | collective-permute-start | bytes 1179656 | tf_op jit(solution)/shard_map/ppermute | solution.py:125
  397.1 86.6 %collective-permute-start.30 = (bf16[128,1024]{1,0:T(8,128)(2,1)}, bf16[128,1024]{1,0:T(8,128)(2,1)}, u32[]{:S(2)}, u32[]{:S(2)}) collective-permute-start(bf16[128,1024]{1,0:T(8,128)(2,1)} %get-tuple-element.185), channel_id=1, source_target_pairs={{0,1},{1,0},{2,3},{3,2},{4,5},{5,4},{6,7},{7,6},{8,9},{9,8},{10,11... | collective-permute-start | bytes 786440 | tf_op jit(solution)/shard_map/ppermute | solution.py:55
  399.2 84.6 %collective-permute-start.67 = (bf16[128,1024]{1,0:T(8,128)(2,1)S(1)}, bf16[128,1024]{1,0:T(8,128)(2,1)}, u32[]{:S(2)}, u32[]{:S(2)}) collective-permute-start(bf16[128,1024]{1,0:T(8,128)(2,1)S(1)} %get-tuple-element.184), channel_id=1, source_target_pairs={{0,4},{4,0},{1,5},{5,1},{2,6},{6,2},{3,7},{7,3},{8,12},{12,8},{9,1... | collective-permute-start | bytes 786440 | tf_op jit(solution)/shard_map/ppermute | solution.py:55
  410.4 73.4 %collective-permute-start.68 = (bf16[128,1024]{1,0:T(8,128)(2,1)}, bf16[128,1024]{1,0:T(8,128)(2,1)}, u32[]{:S(2)}, u32[]{:S(2)}) collective-permute-start(bf16[128,1024]{1,0:T(8,128)(2,1)} %collective-permute-done.66), channel_id=1, source_target_pairs={{0,4},{4,0},{1,5},{5,1},{2,6},{6,2},{3,7},{7,3},{8,12},{12,8},{9,1... | collective-permute-start | bytes 786440 | tf_op jit(solution)/shard_map/ppermute | solution.py:55
  430.1 81.5 %collective-permute-start.46 = (bf16[256,1024]{1,0:T(8,128)(2,1)}, bf16[256,1024]{1,0:T(8,128)(2,1)}, u32[]{:S(2)}, u32[]{:S(2)}) collective-permute-start(bf16[256,1024]{1,0:T(8,128)(2,1)} %dynamic-slice_bitcast_fusion.11), channel_id=1, source_target_pairs={{4,6},{6,4},{5,7},{7,5},{12,14},{14,12},{13,15},{15,13},{20,22},{2... | collective-permute-start | bytes 1572872 | tf_op jit(solution)/shard_map/ppermute | solution.py:59
  542.2 79.1 %collective-permute-start.43 = (bf16[128,1024]{1,0:T(8,128)(2,1)}, bf16[128,1024]{1,0:T(8,128)(2,1)}, u32[]{:S(2)}, u32[]{:S(2)}) collective-permute-start(bf16[128,1024]{1,0:T(8,128)(2,1)} %get-tuple-element.183), channel_id=1, source_target_pairs={{0,1},{1,0},{2,3},{3,2},{4,5},{5,4},{6,7},{7,6},{8,9},{9,8},{10,11... | collective-permute-start | bytes 786440 | tf_op jit(solution)/shard_map/ppermute | solution.py:55
  542.3 79.2 %collective-permute-start.52 = (bf16[256,1024]{1,0:T(8,128)(2,1)}, bf16[256,1024]{1,0:T(8,128)(2,1)}, u32[]{:S(2)}, u32[]{:S(2)}) collective-permute-start(bf16[256,1024]{1,0:T(8,128)(2,1)} %collective-permute-done.50.refs_1_), channel_id=1, source_target_pairs={{4,12},{12,4},{5,13},{13,5},{6,14},{14,6},{7,15},{15,7},{20,28},{2... | collective-permute-start | bytes 1572872 | tf_op jit(solution)/shard_map/ppermute | solution.py:125
  543.7 79.7 %collective-permute-start.53 = (bf16[256,1024]{1,0:T(8,128)(2,1)}, bf16[256,1024]{1,0:T(8,128)(2,1)}, u32[]{:S(2)}, u32[]{:S(2)}) collective-permute-start(bf16[256,1024]{1,0:T(8,128)(2,1)} %collective-permute-done.51.refs_2_), channel_id=1, source_target_pairs={{4,12},{12,4},{5,13},{13,5},{6,14},{14,6},{7,15},{15,7},{20,28},{2... | collective-permute-start | bytes 1572872 | tf_op jit(solution)/shard_map/ppermute | solution.py:125
  610.8 78.2 %collective-permute-start.44 = (bf16[128,1024]{1,0:T(8,128)(2,1)}, bf16[128,1024]{1,0:T(8,128)(2,1)}, u32[]{:S(2)}, u32[]{:S(2)}) collective-permute-start(bf16[128,1024]{1,0:T(8,128)(2,1)} %get-tuple-element.183), channel_id=1, source_target_pairs={{0,4},{4,0},{1,5},{5,1},{2,6},{6,2},{3,7},{7,3},{8,12},{12,8},{9,1... | collective-permute-start | bytes 786440 | tf_op jit(solution)/shard_map/ppermute | solution.py:55
  621.3 68.2 %collective-permute-start.71 = (bf16[128,1024]{1,0:T(8,128)(2,1)}, bf16[128,1024]{1,0:T(8,128)(2,1)}, u32[]{:S(2)}, u32[]{:S(2)}) collective-permute-start(bf16[128,1024]{1,0:T(8,128)(2,1)} %get-tuple-element.182), channel_id=1, source_target_pairs={{0,1},{1,0},{2,3},{3,2},{4,5},{5,4},{6,7},{7,6},{8,9},{9,8},{10,11... | collective-permute-start | bytes 786440 | tf_op jit(solution)/shard_map/ppermute | solution.py:55
  621.3 68.2 %collective-permute-start.45 = (bf16[128,1024]{1,0:T(8,128)(2,1)}, bf16[128,1024]{1,0:T(8,128)(2,1)}, u32[]{:S(2)}, u32[]{:S(2)}) collective-permute-start(bf16[128,1024]{1,0:T(8,128)(2,1)} %collective-permute-done.43), channel_id=1, source_target_pairs={{0,4},{4,0},{1,5},{5,1},{2,6},{6,2},{3,7},{7,3},{8,12},{12,8},{9,1... | collective-permute-start | bytes 786440 | tf_op jit(solution)/shard_map/ppermute | solution.py:55
  621.5 73.3 %collective-permute-start.88 = (bf16[128,1024]{1,0:T(8,128)(2,1)S(1)}, bf16[128,1024]{1,0:T(8,128)(2,1)}, u32[]{:S(2)}, u32[]{:S(2)}) collective-permute-start(bf16[128,1024]{1,0:T(8,128)(2,1)S(1)} %get-tuple-element.82), channel_id=1, source_target_pairs={{0,1},{1,0},{2,3},{3,2},{4,5},{5,4},{6,7},{7,6},{8,9},{9,8},{10,11... | collective-permute-start | bytes 786440 | tf_op jit(solution)/shard_map/ppermute | solution.py:55
  623.4 78.8 %collective-permute-start.89 = (bf16[128,1024]{1,0:T(8,128)(2,1)S(1)}, bf16[128,1024]{1,0:T(8,128)(2,1)}, u32[]{:S(2)}, u32[]{:S(2)}) collective-permute-start(bf16[128,1024]{1,0:T(8,128)(2,1)S(1)} %get-tuple-element.82), channel_id=1, source_target_pairs={{0,4},{4,0},{1,5},{5,1},{2,6},{6,2},{3,7},{7,3},{8,12},{12,8},{9,1... | collective-permute-start | bytes 786440 | tf_op jit(solution)/shard_map/ppermute | solution.py:55
  698.3 26.3 %collective-permute-start.54 = (bf16[256,1024]{1,0:T(8,128)(2,1)S(1)}, bf16[256,1024]{1,0:T(8,128)(2,1)S(1)}, u32[]{:S(2)}, u32[]{:S(2)}) collective-permute-start(bf16[256,1024]{1,0:T(8,128)(2,1)S(1)} %slice.710), channel_id=1, source_target_pairs={{0,4},{4,0},{1,5},{5,1},{2,6},{6,2},{3,7},{7,3},{8,12},{12,8},{9,1... | collective-permute-start | bytes 1572872 | tf_op jit(solution)/shard_map/ppermute | solution.py:55
  718.5 34.0 %collective-permute-start.187 = (bf16[512,1024]{1,0:T(8,128)(2,1)S(1)}, bf16[512,1024]{1,0:T(8,128)(2,1)S(1)}, u32[]{:S(2)}, u32[]{:S(2)}) collective-permute-start(bf16[512,1024]{1,0:T(8,128)(2,1)S(1)} %dynamic-slice_bitcast_fusion.2), channel_id=1, source_target_pairs={{0,16},{16,0},{1,17},{17,1},{2,18},{18,2},{3,19},{19,3},{4,20},{20... | collective-permute-start | bytes 3145736 | tf_op jit(solution)/shard_map/ppermute | solution.py:55
  724.7 34.8 %collective-permute-start.209 = (bf16[512,1024]{1,0:T(8,128)(2,1)S(1)}, bf16[512,1024]{1,0:T(8,128)(2,1)S(1)}, u32[]{:S(2)}, u32[]{:S(2)}) collective-permute-start(bf16[512,1024]{1,0:T(8,128)(2,1)S(1)} %dynamic-slice_bitcast_fusion), channel_id=1, source_target_pairs={{0,8},{8,0},{1,9},{9,1},{2,10},{10,2},{3,11},{11,3},{4,12},{12,4},... | collective-permute-start | bytes 3145736 | tf_op jit(solution)/shard_map/ppermute | solution.py:55
  725.4 25.7 %collective-permute-start.55 = (bf16[128,1024]{1,0:T(8,128)(2,1)S(1)}, bf16[128,1024]{1,0:T(8,128)(2,1)S(1)}, u32[]{:S(2)}, u32[]{:S(2)}) collective-permute-start(bf16[128,1024]{1,0:T(8,128)(2,1)S(1)} %add_convert_fusion.32), channel_id=1, source_target_pairs={{0,1},{1,0},{2,3},{3,2},{4,5},{5,4},{6,7},{7,6},{8,9},{9,8},{10,11... | collective-permute-start | bytes 786440 | tf_op jit(solution)/shard_map/ppermute | solution.py:55
  768.7 27.1 %collective-permute-start.188 = (bf16[256,1024]{1,0:T(8,128)(2,1)S(1)}, bf16[256,1024]{1,0:T(8,128)(2,1)S(1)}, u32[]{:S(2)}, u32[]{:S(2)}) collective-permute-start(bf16[256,1024]{1,0:T(8,128)(2,1)S(1)} %dynamic-slice_bitcast_fusion.8), channel_id=1, source_target_pairs={{0,8},{8,0},{1,9},{9,1},{2,10},{10,2},{3,11},{11,3},{4,12},{12,4},... | collective-permute-start | bytes 1572872 | tf_op jit(solution)/shard_map/ppermute | solution.py:55
  770.2 27.4 %collective-permute-start.210 = (bf16[256,1024]{1,0:T(8,128)(2,1)S(1)}, bf16[256,1024]{1,0:T(8,128)(2,1)S(1)}, u32[]{:S(2)}, u32[]{:S(2)}) collective-permute-start(bf16[256,1024]{1,0:T(8,128)(2,1)S(1)} %dynamic-slice_bitcast_fusion.6), channel_id=1, source_target_pairs={{0,16},{16,0},{1,17},{17,1},{2,18},{18,2},{3,19},{19,3},{4,20},{20... | collective-permute-start | bytes 1572872 | tf_op jit(solution)/shard_map/ppermute | solution.py:55
  784.7 32.5 %collective-permute-start.106 = (bf16[256,1024]{1,0:T(8,128)(2,1)S(1)}, bf16[256,1024]{1,0:T(8,128)(2,1)S(1)}, u32[]{:S(2)}, u32[]{:S(2)}) collective-permute-start(bf16[256,1024]{1,0:T(8,128)(2,1)S(1)} %slice.765), channel_id=1, source_target_pairs={{0,4},{4,0},{1,5},{5,1},{2,6},{6,2},{3,7},{7,3},{8,12},{12,8},{9,1... | collective-permute-start | bytes 1572872 | tf_op jit(solution)/shard_map/ppermute | solution.py:55
  784.9 37.7 %collective-permute-start.96 = (bf16[256,1024]{1,0:T(8,128)(2,1)S(1)}, bf16[256,1024]{1,0:T(8,128)(2,1)S(1)}, u32[]{:S(2)}, u32[]{:S(2)}) collective-permute-start(bf16[256,1024]{1,0:T(8,128)(2,1)S(1)} %slice.753), channel_id=1, source_target_pairs={{0,4},{4,0},{1,5},{5,1},{2,6},{6,2},{3,7},{7,3},{8,12},{12,8},{9,1... | collective-permute-start | bytes 1572872 | tf_op jit(solution)/shard_map/ppermute | solution.py:55
  795.2 52.0 %collective-permute-start.143 = (bf16[512,768]{1,0:T(8,128)(2,1)S(1)}, bf16[512,768]{1,0:T(8,128)(2,1)S(1)}, u32[]{:S(2)}, u32[]{:S(2)}) collective-permute-start(bf16[512,768]{1,0:T(8,128)(2,1)S(1)} %dynamic-slice_bitcast_fusion.4), channel_id=1, source_target_pairs={{0,16},{16,0},{1,17},{17,1},{2,18},{18,2},{3,19},{19,3},{4,20},{20... | collective-permute-start | bytes 2359304 | tf_op jit(solution)/shard_map/ppermute | solution.py:55
  797.6 54.3 %collective-permute-start.190 = (bf16[128,1024]{1,0:T(8,128)(2,1)S(1)}, bf16[128,1024]{1,0:T(8,128)(2,1)S(1)}, u32[]{:S(2)}, u32[]{:S(2)}) collective-permute-start(bf16[128,1024]{1,0:T(8,128)(2,1)S(1)} %get-tuple-element.124), channel_id=1, source_target_pairs={{4,2},{6,0},{0,4},{2,6},{5,3},{7,1},{1,5},{3,7},{12,10},{14,8},{8,... | collective-permute-start | bytes 786440 | tf_op jit(solution)/shard_map/ppermute | solution.py:227
  821.8 30.3 %collective-permute-start.189 = (bf16[128,1024]{1,0:T(8,128)(2,1)S(1)}, bf16[128,1024]{1,0:T(8,128)(2,1)S(1)}, u32[]{:S(2)}, u32[]{:S(2)}) collective-permute-start(bf16[128,1024]{1,0:T(8,128)(2,1)S(1)} %get-tuple-element.123), channel_id=1, source_target_pairs={{4,6},{6,4},{5,7},{7,5},{12,14},{14,12},{13,15},{15,13},{20,22},{2... | collective-permute-start | bytes 786440 | tf_op jit(solution)/shard_map/ppermute | solution.py:59
  822.6 33.8 %collective-permute-start.212 = (bf16[128,1024]{1,0:T(8,128)(2,1)S(1)}, bf16[128,1024]{1,0:T(8,128)(2,1)S(1)}, u32[]{:S(2)}, u32[]{:S(2)}) collective-permute-start(bf16[128,1024]{1,0:T(8,128)(2,1)S(1)} %get-tuple-element.120), channel_id=1, source_target_pairs={{4,2},{6,0},{0,4},{2,6},{5,3},{7,1},{1,5},{3,7},{12,10},{14,8},{8,... | collective-permute-start | bytes 786440 | tf_op jit(solution)/shard_map/ppermute | solution.py:227
  856.4 121.5 %collective-permute-start.169 = (bf16[32,1024]{1,0:T(8,128)(2,1)S(1)}, bf16[32,1024]{1,0:T(8,128)(2,1)S(1)}, u32[]{:S(2)}, u32[]{:S(2)}) collective-permute-start(bf16[32,1024]{1,0:T(8,128)(2,1)S(1)} %add_convert_fusion.42.refs_0_), channel_id=1, source_target_pairs={{0,16},{16,0},{1,17},{17,1},{2,18},{18,2},{3,19},{19,3},{4,20},{20... | collective-permute-start | bytes 196616 | tf_op jit(solution)/shard_map/ppermute | solution.py:55
  871.0 24.9 %collective-permute-start.146 = (bf16[128,768]{1,0:T(8,128)(2,1)S(1)}, bf16[128,768]{1,0:T(8,128)(2,1)S(1)}, u32[]{:S(2)}, u32[]{:S(2)}) collective-permute-start(bf16[128,768]{1,0:T(8,128)(2,1)S(1)} %get-tuple-element.138), channel_id=1, source_target_pairs={{4,2},{6,0},{0,4},{2,6},{5,3},{7,1},{1,5},{3,7},{12,10},{14,8},{8,... | collective-permute-start | bytes 589832 | tf_op jit(solution)/shard_map/ppermute | solution.py:227
  895.2 25.5 %collective-permute-start.176 = (bf16[512,1024]{1,0:T(8,128)(2,1)S(1)}, bf16[512,1024]{1,0:T(8,128)(2,1)S(1)}, u32[]{:S(2)}, u32[]{:S(2)}) collective-permute-start(bf16[512,1024]{1,0:T(8,128)(2,1)S(1)} %dynamic-slice_bitcast_fusion.3), channel_id=1, source_target_pairs={{0,16},{16,0},{1,17},{17,1},{2,18},{18,2},{3,19},{19,3},{4,20},{20... | collective-permute-start | bytes 3145736 | tf_op jit(solution)/shard_map/ppermute | solution.py:55
  895.9 25.3 %collective-permute-start.198 = (bf16[512,1024]{1,0:T(8,128)(2,1)S(1)}, bf16[512,1024]{1,0:T(8,128)(2,1)S(1)}, u32[]{:S(2)}, u32[]{:S(2)}) collective-permute-start(bf16[512,1024]{1,0:T(8,128)(2,1)S(1)} %dynamic-slice_bitcast_fusion.1), channel_id=1, source_target_pairs={{0,8},{8,0},{1,9},{9,1},{2,10},{10,2},{3,11},{11,3},{4,12},{12,4},... | collective-permute-start | bytes 3145736 | tf_op jit(solution)/shard_map/ppermute | solution.py:55
  922.3 27.2 %collective-permute-start.177 = (bf16[256,1024]{1,0:T(8,128)(2,1)S(1)}, bf16[256,1024]{1,0:T(8,128)(2,1)S(1)}, u32[]{:S(2)}, u32[]{:S(2)}) collective-permute-start(bf16[256,1024]{1,0:T(8,128)(2,1)S(1)} %dynamic-slice_bitcast_fusion.9), channel_id=1, source_target_pairs={{0,8},{8,0},{1,9},{9,1},{2,10},{10,2},{3,11},{11,3},{4,12},{12,4},... | collective-permute-start | bytes 1572872 | tf_op jit(solution)/shard_map/ppermute | solution.py:55
  950.4 26.8 %collective-permute-start.179 = (bf16[128,1024]{1,0:T(8,128)(2,1)S(1)}, bf16[128,1024]{1,0:T(8,128)(2,1)S(1)}, u32[]{:S(2)}, u32[]{:S(2)}) collective-permute-start(bf16[128,1024]{1,0:T(8,128)(2,1)S(1)} %get-tuple-element.126), channel_id=1, source_target_pairs={{4,2},{6,0},{0,4},{2,6},{5,3},{7,1},{1,5},{3,7},{12,10},{14,8},{8,... | collective-permute-start | bytes 786440 | tf_op jit(solution)/shard_map/ppermute | solution.py:227
  1087.4 24.9 %collective-permute-start.120 = (bf16[128,1024]{1,0:T(8,128)(2,1)S(1)}, bf16[128,1024]{1,0:T(8,128)(2,1)S(1)}, u32[]{:S(2)}, u32[]{:S(2)}) collective-permute-start(bf16[128,1024]{1,0:T(8,128)(2,1)S(1)} %get-tuple-element.89), channel_id=1, source_target_pairs={{0,0},{4,2},{2,4},{6,6},{1,1},{5,3},{3,5},{7,7},{8,8},{12,10},{10,... | collective-permute-start | bytes 786440 | tf_op jit(solution)/shard_map/ppermute | solution.py:114
  (348 other events, 4586.7 us)

commit v2 on v1

v2 whole, which is shorter than its diff:
```python
import functools

import jax
import jax.numpy as jnp
from jax import lax
from jax.experimental import pallas as pl
from jax.experimental.pallas import tpu as pltpu
from jax.sharding import Mesh
from jax.sharding import PartitionSpec as P

H = 8
HD = 128
LAYERS = 2
norm_eps = 1e-05
F32 = jnp.float32
BF16 = jnp.bfloat16
PLANE = ("c", "kx", "ky")
FETCH_ATTN = ("r", "0a", None, None), ("0c", "0d", "0e", "1a")
FETCH_FFN = (("s", 3), "0b", "0c", "0c2"), ("0e", "1a", "1c", "1c2")
COTANGENT = "1c"
ACTIVATIONS_OUT = "1f"
REDUCE_FFN = (
    ("0g", ("0h", 3), ("0j", 2), ("t1", 2), "t2", "t3", "t5"),
    ("1g", ("1h", 2), ("1i", 2), ("0f", 3), "0g", ("0g2", 2), "0j"),
)
REDUCE_ATTN = (
    ("0j", ("0j2", 2), "t2", "t3", "t4", "t5", "t6"),
    ("1j", "0f", ("0f2", 2), "0g", ("0h2", 2), ("0j2", 2), "t3"),
)
SUM_SMALL = ("t1", "t2", "t3", "t4", "t5", "t6")


def gelu_tanh(values):
    return jax.nn.gelu(values, approximate=True)


def norm_parts(stream):
    centred = stream - jnp.mean(stream, axis=-1, keepdims=True)
    inverse = lax.rsqrt(jnp.mean(centred * centred, axis=-1, keepdims=True) + norm_eps)
    return centred * inverse, inverse


def norm_back(grad_normed, unit_rows, inverse, gain):
    scaled = grad_normed * gain
    return inverse * (
        scaled
        - jnp.mean(scaled, axis=-1, keepdims=True)
        - unit_rows * jnp.mean(scaled * unit_rows, axis=-1, keepdims=True)
    )


def dot(left, right):
    return jnp.dot(left, right, preferred_element_type=F32)


def dot_nt(left, right):
    return jnp.einsum("ti,oi->to", left, right, preferred_element_type=F32)


def dot_tn(left, right):
    return jnp.einsum("ti,to->io", left, right, preferred_element_type=F32)


def after(value, other):
    return value if other is None else lax.optimization_barrier((value, other))[0]


def swap(value, axis):
    return lax.ppermute(value, axis, [(0, 1), (1, 0)])


def small_plane():
    return all(lax.axis_size(axis) == 2 for axis in PLANE)


def axis_order(axis):
    size = lax.axis_size(axis)
    if size == 2:
        return [lax.axis_index(axis), 1 - lax.axis_index(axis)]
    return list(range(size))


def gather_rows(rows, work, event):
    rows = work.at(event, rows)
    if lax.axis_size("r") == 2:
        across = work.at(event + "2", swap(rows, "r"))
        return jnp.concatenate([rows, across], 0)
    return work.at(event + "2", lax.all_gather(rows, "r", axis=0, tiled=True))


def scatter_rows(product, work, event):
    count = lax.axis_size("r")
    if count == 2:
        send = work.at(event, product(1, 2).astype(BF16))
        across = swap(send, "r")
        near = product(0, 1)
        return near + work.at(event + "2", across).astype(F32)
    partial = work.at(event, product(0, count).astype(BF16))
    across = lax.psum_scatter(partial, "r", scatter_dimension=0, tiled=True)
    return work.at(event + "2", across).astype(F32)


def to_chunks(value, token, at=lambda value: value):
    half = value.shape[0] // 2
    value = after(value, token)
    low, high = value[:half], value[half:]
    core, block = lax.axis_index("c"), lax.axis_index("b")
    first = jnp.where(block == 0, low, high)
    second = jnp.where(block == 0, high, low)
    first = at(first)
    first = lax.ppermute(first, ("c", "b"), [(0, 0), (1, 2), (2, 1), (3, 3)])
    second = lax.ppermute(second, ("c", "b"), [(0, 2), (1, 0), (2, 3), (3, 1)])
    yield [first, second]
    yield jnp.where(core == 0, jnp.concatenate([first, second], 0), jnp.concatenate([second, first], 0))


def from_chunks(rows, token):
    half = rows.shape[0] // 2
    rows = after(rows, token)
    early, late = rows[:half], rows[half:]
    core, block = lax.axis_index("c"), lax.axis_index("b")
    first = jnp.where(core == 0, early, late)
    second = jnp.where(core == 0, late, early)
    first = lax.ppermute(first, ("c", "b"), [(0, 0), (2, 1), (1, 2), (3, 3)])
    second = lax.ppermute(second, ("c", "b"), [(2, 0), (0, 1), (3, 2), (1, 3)])
    yield [first, second]
    yield jnp.where(block == 0, jnp.concatenate([first, second], 0), jnp.concatenate([second, first], 0))


def plane_count():
    return lax.axis_size("c") * lax.axis_size("kx") * lax.axis_size("ky")


def plane_place(c=None, x=None, y=None):
    c = lax.axis_index("c") if c is None else c
    x = lax.axis_index("kx") if x is None else x
    y = lax.axis_index("ky") if y is None else y
    return (c * lax.axis_size("kx") + x) * lax.axis_size("ky") + y


ORDERS = (("kx", "ky"), ("ky", "kx"))


def plane_places(ordered):
    spots = []
    for first, second in ORDERS:
        for c in axis_order("c"):
            for slow in axis_order(second):
                for fast in axis_order(first):
                    if ordered:
                        spots.append((c * 2 + fast) * 2 + slow)
                    else:
                        spots.append(plane_place(c, **{first[1]: fast, second[1]: slow}))
    return jnp.stack(spots).astype(jnp.int32)


def after_all(values, token):
    return [after(value, token) for value in values]


def spread_steps(work, pieces, token):
    token, span = token
    pieces = [piece[None] for piece in pieces]
    for stage in range(2):
        pieces = after_all(pieces, token)
        got = [swap(piece, order[stage]) for piece, order in zip(pieces, ORDERS)]
        work.expect(got, span)
        token, span = yield
        got = after_all(got, token)
        pieces = [jnp.concatenate(pair, 0) for pair in zip(pieces, got)]
        work.latest = pieces[0]
    return pieces, [swap(piece, "c") for piece in pieces]


class Background:
    def __init__(self):
        self.tasks = []
        self.waiting = []
        self.step = 0

    def advance(self, task, events, token):
        try:
            task.send(token)
            while events and (events[0] is None or events[0][0] is None):
                event = events.pop(0)
                task.send((None, event[1] if event else 1))
            self.tasks.append((task, events))
        except StopIteration:
            pass

    def add(self, task, events):
        self.advance(task, list(events), None)

    def expect(self, values, span=1):
        self.waiting += [(self.step + span, value) for value in values]

    def at(self, event, value):
        self.step += 1
        for due, result in self.waiting:
            if due <= self.step:
                value = after(value, result)
        self.waiting = [pair for pair in self.waiting if pair[0] > self.step]
        tasks, self.tasks = self.tasks, []
        for task, events in tasks:
            name, span = (events[0], 1) if isinstance(events[0], str) else events[0]
            if name == event:
                self.advance(task, events[1:], (value, span))
            else:
                self.tasks.append((task, events))
        return value


def sum_small(work, results, value):
    for axis in ("c", "kx", "ky", "r", "b"):
        token, span = yield
        value = after(value, token)
        if lax.axis_size(axis) == 2:
            got = swap(value, axis)
            work.expect([got], span)
            value = value + got
        else:
            value = lax.psum(value, axis)
    token, span = yield
    results["small"] = value


def cut_columns(value, parts):
    width = value.shape[1] // parts
    return jnp.concatenate([value[:, index * width : (index + 1) * width] for index in range(parts)], 0)


def cut_piece(weight, layer):
    size = weight.shape[1] // plane_count()
    return lax.dynamic_slice(weight, (layer, plane_place() * size, 0), (1, size, weight.shape[2]))[0]


def at_core(put, mine, beside):
    @pl.when(pl.program_id(0) < 4)
    def _():
        put(*mine)

    @pl.when(pl.program_id(0) >= 4)
    def _():
        put(*beside)


def place_attn_kernel(spots, kv, qo, kv_beside, qo_beside, query, key, value, out, to_query, to_kv, to_out):
    width = query.shape[2]
    rows = out.shape[1]

    def put(kv, qo):
        to_kv[:, :width] = key[0]
        to_kv[:, width : 2 * width] = kv[0, :, :width]
        to_kv[:, 2 * width : 3 * width] = value[0]
        to_kv[:, 3 * width :] = kv[0, :, width:]
        to_query[:, :width] = query[0]
        to_query[:, width:] = qo[0, :, :width]
        to_out[0] = out[0]
        for index in range(qo.shape[1] // rows):
            to_out[1, :, index * width : (index + 1) * width] = qo[
                0, index * rows : (index + 1) * rows, width:
            ]

    at_core(put, (kv, qo), (kv_beside, qo_beside))


def place_ffn_kernel(spots, up, down, up_beside, down_beside, to_up, to_down):
    def put(up, down):
        to_up[...] = up[0]
        to_down[...] = down[0]

    at_core(put, (up, down), (up_beside, down_beside))


def piece_specs(pieces):
    def spec(piece, core):
        return pl.BlockSpec((1,) + piece.shape[1:], lambda step, spots: (jnp.clip(step - core * 4, 0, 3), 0, 0))

    return [spec(piece, core) for core in range(2) for piece in pieces]


def row_spec(block, order, lead=0):
    if len(block) == 2:
        return pl.BlockSpec(block, lambda step, spots: (spots[order * 8 + step], 0))
    return pl.BlockSpec(block, lambda step, spots: (lead, spots[order * 8 + step], 0))


def place_call(kernel, mine, beside, owns, own_specs, outs, out_specs):
    size = sum(math_prod(shape) for shape in outs)
    return pl.pallas_call(
        kernel,
        out_shape=[jax.ShapeDtypeStruct(shape, BF16) for shape in outs],
        grid_spec=pltpu.PrefetchScalarGridSpec(
            num_scalar_prefetch=1,
            grid=(8,),
            in_specs=piece_specs(mine) + own_specs,
            out_specs=out_specs,
        ),
        compiler_params=pltpu.CompilerParams(vmem_limit_bytes=24 << 20),
        cost_estimate=pl.CostEstimate(flops=0, bytes_accessed=size * 4, transcendentals=0),
    )(plane_places(False), *mine, *beside, *owns)


def math_prod(shape):
    total = 1
    for size in shape:
        total *= size
    return total


def fetch_attn(work, used, layer, w_query, w_key, w_value, w_out):
    count = plane_count()
    depth, width = w_query.shape[1], w_query.shape[2]
    rows, out_rows = depth // count, width // count
    parts = depth // width
    kv = jnp.concatenate([cut_piece(w_key, layer), cut_piece(w_value, layer)], 1)
    qo = jnp.concatenate([cut_piece(w_query, layer), cut_columns(cut_piece(w_out, layer), parts)], 1)
    token, span = yield
    moved = swap(after(jnp.concatenate([kv, qo], 1), token), "b")
    work.expect([moved], span)
    pieces = [moved[:, : 2 * width], moved[:, 2 * width :]]
    token = yield
    if small_plane() and out_rows % 16 == 0:
        mine, beside = yield from spread_steps(work, pieces, token)
        query, kv, out = place_call(
            place_attn_kernel,
            mine,
            beside,
            (w_query, w_key, w_value, w_out),
            [row_spec((1, rows, width), order, layer) for order in (1, 0, 0)]
            + [row_spec((1, out_rows, depth), 1, layer)],
            ((depth, 2 * width), (depth, 4 * width), (2, width, depth)),
            [
                row_spec((rows, 2 * width), 1),
                row_spec((rows, 4 * width), 0),
                row_spec((2, out_rows, depth), 1),
            ],
        )
        used["attn", layer] = (query, kv, out.reshape(2 * width, depth))
        return
    packed = jnp.concatenate([lax.all_gather(piece, PLANE, axis=0) for piece in pieces], 2)
    kv, qo = packed[:, :, : 2 * width], packed[:, :, 2 * width :]
    out = qo[:, :, width:].reshape(count, parts, out_rows, width).transpose(0, 2, 1, 3).reshape(width, depth)
    kv = kv.reshape(depth, 2 * width)
    query = jnp.concatenate([w_query[layer], qo[:, :, :width].reshape(depth, width)], 1)
    kv = jnp.concatenate([w_key[layer], kv[:, :width], w_value[layer], kv[:, width:]], 1)
    used["attn", layer] = (query, kv, jnp.concatenate([w_out[layer], out], 0))


def fetch_ffn(work, used, layer, w_up, w_down):
    count = plane_count()
    depth, width = w_up.shape[1], w_up.shape[2]
    rows, down_rows = depth // count, width // count
    pieces = [cut_piece(weight, layer) for weight in (w_up, w_down)]
    token, span = yield
    if width == depth:
        moved = swap(after(jnp.concatenate(pieces, 1), token), "b")
        pieces = [moved[:, :width], moved[:, width:]]
    else:
        pieces = [swap(piece, "b") for piece in after_all(pieces, token)]
    work.expect(pieces, span)
    token = yield
    if small_plane() and width == depth:
        mine, beside = yield from spread_steps(work, pieces, token)
        used["ffn", layer] = place_call(
            place_ffn_kernel,
            mine,
            beside,
            (),
            [],
            ((depth, width), (width, depth)),
            [row_spec((rows, width), 0), row_spec((down_rows, depth), 1)],
        )
        return
    used["ffn", layer] = [lax.all_gather(piece, PLANE, axis=0, tiled=True) for piece in pieces]


def store_kernel(layout, arrays, given, spots, *refs):
    outs = refs[2 * arrays + given :]

    def put(*pieces):
        for out, (half, begin, width, turn) in zip(outs, layout):
            block = pieces[half][0, :, begin : begin + width].astype(F32)
            out[0] = block.T if turn else block

    at_core(put, refs[:arrays], refs[arrays : 2 * arrays])


def reduce_weights(work, results, name, layer, halves_of, layout):
    depth = halves_of[0][0][0].shape[1]
    widths = [[right.shape[1] // 2 for _, right in pairs] for pairs in halves_of]

    def side(value, half, which):
        parts, begin = [], 0
        for width in widths[half]:
            parts.append(value[:, begin + which * width : begin + (which + 1) * width])
            begin += 2 * width
        return jnp.concatenate(parts, 1)

    def grads_of(place, size, token):
        return [
            jnp.concatenate(
                [
                    dot_tn(lax.dynamic_slice_in_dim(left, place * size, size, 1), right)
                    for left, right in [(after(left, token), right) for left, right in pairs]
                ],
                1,
            ).astype(BF16)
            for pairs in halves_of
        ]

    token, span = yield
    if small_plane():
        core = lax.axis_index("c")
        size = depth // 2
        beside = [swap(grad, "c") for grad in grads_of(1 - core, size, token)]
        kept = grads_of(core, size, token)
        work.expect(kept + beside, span)

        def cut(half, other):
            index = lax.axis_index(ORDERS[half][0])
            begin = (1 - index if other else index) * (size // 2)
            return sum(
                lax.dynamic_slice_in_dim(value[half], begin, size // 2, 0).astype(F32) for value in (kept, beside)
            )

        token, span = yield
        kept, beside = after_all(kept, token), after_all(beside, token)
        got = [swap(cut(half, True).astype(BF16), ORDERS[half][0]) for half in range(2)]
        work.expect(got, span)
        near = [cut(half, False) for half in range(2)]
        token, span = yield
        size = size // 4
        totals = [(value + part.astype(F32)).astype(BF16) for value, part in zip(near, after_all(got, token))]
        work.latest = totals[0]
        index = [lax.axis_index(order[1]) for order in ORDERS]
        got = [
            swap(lax.dynamic_slice_in_dim(value, (1 - i) * size, size, 0), order[1])
            for value, i, order in zip(totals, index, ORDERS)
        ]
        work.expect(got, span)
        near = [lax.dynamic_slice_in_dim(value, i * size, size, 0) for value, i in zip(totals, index)]
        token, span = yield
        totals = [
            (value.astype(F32) + part.astype(F32)).astype(BF16)
            for value, part in zip(near, after_all(got, token))
        ]
        work.latest = totals[0]
    else:
        totals = [
            lax.psum_scatter(grad, PLANE, scatter_dimension=0, tiled=True) for grad in grads_of(0, depth, token)
        ]
        token, span = yield
    other = jnp.concatenate([side(value, half, 1) for half, value in enumerate(totals)], 1)
    got = swap(after(other, token), "b")
    work.expect([got], span)
    token = yield
    other = after(got, token[0])
    pieces, begin = [], 0
    for half, value in enumerate(totals):
        own = side(value, half, 0)
        part = other[:, begin : begin + own.shape[1]]
        begin += own.shape[1]
        pieces.append((own.astype(F32) + part.astype(F32)).astype(BF16))
    work.latest = pieces[0]
    rows = depth // plane_count()
    shapes = [(LAYERS, w, depth) if turn else (LAYERS, depth, w) for _, _, w, turn in layout]
    before = results.get(name)
    if not (small_plane() and rows % 128 == 0):
        stored = []
        for index, (half, begin, width, turn) in enumerate(layout):
            block = lax.all_gather(pieces[half][:, begin : begin + width], PLANE, axis=0, tiled=True)
            block = block.astype(F32)
            block = block.T if turn else block
            base = jnp.zeros(shapes[index], F32) if before is None else before[index]
            stored.append(base.at[layer].set(block))
        results[name] = stored
        return
    mine, beside = yield from spread_steps(work, pieces, token)
    given = list(before or [])
    size = sum(math_prod(shape) for shape in shapes) // LAYERS

    def out_spec(half, width, turn):
        if turn:
            return pl.BlockSpec((1, width, rows), lambda step, spots: (layer, 0, spots[half * 8 + step]))
        return row_spec((1, rows, width), half, layer)

    results[name] = pl.pallas_call(
        functools.partial(store_kernel, layout, len(mine), len(given)),
        out_shape=[jax.ShapeDtypeStruct(shape, F32) for shape in shapes],
        grid_spec=pltpu.PrefetchScalarGridSpec(
            num_scalar_prefetch=1,
            grid=(8,),
            in_specs=piece_specs(mine) + [pl.BlockSpec(memory_space=pl.ANY)] * len(given),
            out_specs=[out_spec(half, width, turn) for half, _, width, turn in layout],
        ),
        input_output_aliases={1 + len(mine + beside) + index: index for index in range(len(given))},
        compiler_params=pltpu.CompilerParams(vmem_limit_bytes=24 << 20),
        cost_estimate=pl.CostEstimate(flops=0, bytes_accessed=size * 6, transcendentals=0),
    )(plane_places(True), *mine, *beside, *given)
    work.expect(list(results[name]))


def halves(ref, size, columns, odd):
    count = ref.shape[0] // size
    return jnp.concatenate(
        [ref[index * size : (index + 1) * size, columns] for index in range(odd, count, 2)], 0
    )


def both_cores(mine, beside, size, columns, odd):
    return jnp.concatenate([halves(mine, size, columns, odd), halves(beside, size, columns, odd)], 0)


def tile_scores(query, keys, at_query, at_keys, slope):
    scores = lax.dot_general(query, keys, (((1,), (1,)), ((), ())), preferred_element_type=F32)
    place, start = at_query
    scores = scores * HD ** (-0.5) - slope * (place - at_keys)
    return jnp.where((at_keys <= place) & (at_keys >= start), scores, -1e30)


def attend_kernel(size, slopes, at_rows, at_keys, query, mine, beside, mixed, log_totals):
    heads = query.shape[1] // HD
    for head in range(heads):
        columns = slice(head * HD, (head + 1) * HD)
        value_columns = slice((heads + head) * HD, (heads + head + 1) * HD)
        keys = [both_cores(mine, beside, size, columns, odd) for odd in range(2)]
        values = [both_cores(mine, beside, size, value_columns, odd) for odd in range(2)]
        for odd in range(2):
            key_rows = keys[0] if odd == 0 else jnp.concatenate(keys, 0)
            value_rows = values[0] if odd == 0 else jnp.concatenate(values, 0)
            spots = at_keys[:, : key_rows.shape[0]]
            scores = tile_scores(
                halves(query, size, columns, odd),
                key_rows,
                (at_rows[:, 2 * odd : 2 * odd + 1], at_rows[:, 2 * odd + 1 : 2 * odd + 2]),
                spots,
                slopes[head],
            )
            row_max = jnp.max(scores, axis=-1, keepdims=True)
            weights = jnp.exp(scores - row_max)
            totals = jnp.sum(weights, axis=-1, keepdims=True)
            probabilities = (weights * (1.0 / totals)).astype(BF16)
            result = jnp.dot(probabilities, value_rows, preferred_element_type=F32).astype(BF16)
            logs = row_max + jnp.log(totals)
            for index in range(result.shape[0] // size):
                rows = slice((2 * index + odd) * size, (2 * index + odd + 1) * size)
                mixed[rows, columns] = result[index * size : (index + 1) * size]
                log_totals[rows, head : head + 1] = logs[index * size : (index + 1) * size]


def attend_back_kernel(
    size, slopes, at_rows, at_keys, query, mine, beside, log_totals, grad, to_query, to_mine, to_beside
):
    heads = query.shape[1] // HD
    scale = HD ** (-0.5)
    for head in range(heads):
        columns = slice(head * HD, (head + 1) * HD)
        value_columns = slice((heads + head) * HD, (heads + head + 1) * HD)
        one = slice(head, head + 1)
        keys = [both_cores(mine, beside, size, columns, odd) for odd in range(2)]
        values = [both_cores(mine, beside, size, value_columns, odd) for odd in range(2)]
        key_total = value_total = None
        for odd in (1, 0):
            key_rows = keys[0] if odd == 0 else jnp.concatenate(keys, 0)
            value_rows = values[0] if odd == 0 else jnp.concatenate(values, 0)
            query_rows = halves(query, size, columns, odd)
            grad_rows = halves(grad, size, columns, odd)
            scores = tile_scores(
                query_rows,
                key_rows,
                (at_rows[:, 2 * odd : 2 * odd + 1], at_rows[:, 2 * odd + 1 : 2 * odd + 2]),
                at_keys[:, : key_rows.shape[0]],
                slopes[head],
            )
            probabilities = jnp.exp(scores - halves(log_totals, size, one, odd))
            grad_probs = lax.dot_general(
                grad_rows, value_rows, (((1,), (1,)), ((), ())), preferred_element_type=F32
            )
            centre = jnp.sum(grad_probs * probabilities, axis=-1, keepdims=True)
            grad_scores = (probabilities * (grad_probs - centre)).astype(BF16)
            grad_value = lax.dot_general(
                probabilities.astype(BF16), grad_rows, (((0,), (0,)), ((), ())), preferred_element_type=F32
            )
            grad_query = jnp.dot(grad_scores, key_rows, preferred_element_type=F32) * scale
            grad_key = (
                lax.dot_general(grad_scores, query_rows, (((0,), (0,)), ((), ())), preferred_element_type=F32)
                * scale
            )
            grad_query = grad_query.astype(BF16)
            for index in range(grad_query.shape[0] // size):
                rows = slice((2 * index + odd) * size, (2 * index + odd + 1) * size)
                to_query[rows, columns] = grad_query[index * size : (index + 1) * size]
            if odd == 1:
                early = keys[0].shape[0]
                results = [(grad_key[early:], grad_value[early:], 1)]
                key_total, value_total = grad_key[:early], grad_value[:early]
            else:
                results = [(grad_key + key_total, grad_value + value_total, 0)]
            for grad_key, grad_value, part in results:
                blocks = grad_key.shape[0] // size // 2
                for index in range(blocks):
                    rows = slice((2 * index + part) * size, (2 * index + part + 1) * size)
                    near = slice(index * size, (index + 1) * size)
                    far = slice((blocks + index) * size, (blocks + index + 1) * size)
                    to_mine[rows, columns] = grad_key[near]
                    to_mine[rows, value_columns] = grad_value[near]
                    to_beside[rows, columns] = grad_key[far].astype(BF16)
                    to_beside[rows, value_columns] = grad_value[far].astype(BF16)


def attention_cost(query, products):
    elements = query.shape[0] * query.shape[0] * 3 // 2 * (query.shape[1] // HD)
    return pl.CostEstimate(
        flops=elements * HD * 2 * products, bytes_accessed=query.size * 16, transcendentals=elements
    )


def attention_specs(count):
    return [pl.BlockSpec(memory_space=pltpu.SMEM)] + [pl.BlockSpec(memory_space=pltpu.VMEM)] * count


def attend(query, mine, beside, info):
    slopes, at_rows, at_keys, size = info
    return pl.pallas_call(
        functools.partial(attend_kernel, size),
        out_shape=[
            jax.ShapeDtypeStruct(query.shape, BF16),
            jax.ShapeDtypeStruct((query.shape[0], query.shape[1] // HD), F32),
        ],
        in_specs=attention_specs(5),
        out_specs=[pl.BlockSpec(memory_space=pltpu.VMEM)] * 2,
        compiler_params=pltpu.CompilerParams(vmem_limit_bytes=48 << 20),
        cost_estimate=attention_cost(query, 2),
    )(slopes, at_rows, at_keys, query, mine, beside)


def attend_back(query, mine, beside, log_totals, grad_mixed, info):
    slopes, at_rows, at_keys, size = info
    return pl.pallas_call(
        functools.partial(attend_back_kernel, size),
        out_shape=[
            jax.ShapeDtypeStruct(query.shape, BF16),
            jax.ShapeDtypeStruct(mine.shape, F32),
            jax.ShapeDtypeStruct(mine.shape, BF16),
        ],
        in_specs=attention_specs(7),
        out_specs=[pl.BlockSpec(memory_space=pltpu.VMEM)] * 3,
        compiler_params=pltpu.CompilerParams(vmem_limit_bytes=48 << 20),
        cost_estimate=attention_cost(query, 5),
    )(slopes, at_rows, at_keys, query, mine, beside, log_totals, grad_mixed)


def attention_info(lengths, slopes, size):
    block, core = lax.axis_index("b"), lax.axis_index("c")
    ends = jnp.cumsum(jnp.where(core == block, lengths, swap(lengths, "c")))
    across = lax.axis_size("r")
    steps = jnp.arange(size, dtype=jnp.int32)

    def spots(which, odd):
        return jnp.concatenate([((odd * across + place) * 2 + which) * size + steps for place in axis_order("r")])

    columns, keys = [], []
    for odd in range(2):
        place = spots(core, odd)
        start = jnp.max(jnp.where(place[:, None] >= ends[None, :], ends[None, :], 0), axis=1)
        columns += [place, start]
        keys += [spots(which, odd) for which in axis_order("c")]
    at_rows = jnp.stack(columns, 1).astype(F32)
    at_keys = jnp.concatenate(keys)[None, :].astype(F32)
    return slopes, at_rows, at_keys, size


def local(
    activations,
    lengths,
    cotangent,
    gain_attn,
    shift_attn,
    w_query,
    b_query,
    w_key,
    w_value,
    b_value,
    w_out,
    b_out,
    gain_ffn,
    shift_ffn,
    w_up,
    b_up,
    w_down,
    b_down,
):
    block, place = lax.axis_index("b"), lax.axis_index("r")
    across = lax.axis_size("r")
    shards = [block * across + place, (1 - block) * across + place]
    head_width = w_query.shape[2]
    head_count = head_width // HD
    hidden_width = w_up.shape[2]

    head_ids = jnp.concatenate(
        [shard * head_count + jnp.arange(head_count, dtype=jnp.int32) for shard in shards]
    ).astype(F32)
    slopes = 2.0 ** (-8.0 * (head_ids + 1.0) / H)
    info = attention_info(lengths[0], slopes, activations.shape[0] // 2)

    bias_own = jnp.concatenate([b_query, b_value], 1)
    bias_other = swap(bias_own, "b")

    used, results = {}, {}
    work = Background()
    for layer in range(LAYERS):
        work.add(
            fetch_attn(work, used, layer, w_query, w_key, w_value, w_out),
            FETCH_ATTN[layer],
        )
        work.add(fetch_ffn(work, used, layer, w_up, w_down), FETCH_FFN[layer])

    def move(name, steps, value):
        token, span = yield
        steps = steps(value, token)
        work.expect(next(steps), span)
        results[name] = next(steps)

    moving = to_chunks(activations, None, lambda value: work.at("r", value))
    next(moving)
    stream = work.at("s", next(moving).astype(F32))
    work.add(move("cotangent", to_chunks, cotangent), (COTANGENT,))

    def rows_of(array, first, last):
        size = array.shape[0] // across
        return array[first * size : last * size]

    stored = []
    zero = jnp.zeros((2 * head_width,), F32)
    for layer in range(LAYERS):
        bias_query = jnp.concatenate([bias_own[layer, :head_width], bias_other[layer, :head_width]])
        bias_kv = jnp.concatenate([zero, bias_own[layer, head_width:], bias_other[layer, head_width:]])
        bias_up = [
            lax.dynamic_slice_in_dim(b_up[layer], shard * hidden_width, hidden_width, 0) for shard in shards
        ]
        unit, inverse = norm_parts(stream)
        inputs = gather_rows((unit * gain_attn[layer] + shift_attn[layer]).astype(BF16), work, str(layer) + "a")
        weight_query, weight_kv, weight_out = used["attn", layer]
        mine = (dot(inputs, weight_kv) + bias_kv).astype(BF16)
        mine = work.at(str(layer) + "b", mine)
        beside = swap(mine, "c")
        query = (dot(inputs, weight_query) + bias_query).astype(BF16)
        mixed, log_totals = attend(query, mine, beside, info)
        middle = stream + (
            scatter_rows(lambda first, last: dot(rows_of(mixed, first, last), weight_out), work, str(layer) + "c") + b_out[layer]
        )
        unit_mid, inverse_mid = norm_parts(middle)
        inputs_mid = gather_rows((unit_mid * gain_ffn[layer] + shift_ffn[layer]).astype(BF16), work, str(layer) + "d")
        ups, downs = zip((w_up[layer], w_down[layer]), used["ffn", layer])
        hidden = [dot(inputs_mid, up) + bias for up, bias in zip(ups, bias_up)]
        active = [gelu_tanh(value).astype(BF16) for value in hidden]
        stream = middle + (
            scatter_rows(lambda first, last: sum(dot(rows_of(value, first, last), down) for value, down in zip(active, downs)),
                work, str(layer) + "e") + b_down[layer]
        )
        stored.append(
            (
                unit,
                inverse,
                inputs,
                query,
                mine,
                beside,
                mixed,
                log_totals,
                unit_mid,
                inverse_mid,
                inputs_mid,
                hidden,
                active,
            )
        )
    work.add(move("activations_out", from_chunks, stream.astype(BF16)), (ACTIVATIONS_OUT,))
    grad_stream = results["cotangent"].astype(F32)
    small = {}
    for layer in reversed(range(LAYERS)):
        weight_query, weight_kv, weight_out = used["attn", layer]
        ups, downs = zip((w_up[layer], w_down[layer]), used["ffn", layer])
        (
            unit,
            inverse,
            inputs,
            query,
            mine,
            beside,
            mixed,
            log_totals,
            unit_mid,
            inverse_mid,
            inputs_mid,
            hidden,
            active,
        ) = stored[layer]
        grad_branch = grad_stream.astype(BF16)
        grad_b_down = jnp.sum(grad_branch, axis=0, dtype=F32)
        branch_all = gather_rows(grad_branch, work, str(layer) + "f")
        grad_hidden = [
            jax.vjp(gelu_tanh, value)[1](dot_nt(branch_all, down))[0].astype(BF16)
            for value, down in zip(hidden, downs)
        ]
        work.add(
            reduce_weights(
                work,
                results,
                "ffn",
                layer,
                ([(inputs_mid, jnp.concatenate(grad_hidden, 1))], [(branch_all, jnp.concatenate(active, 1))]),
                ((0, 0, hidden_width, False), (1, 0, hidden_width, True)),
            ),
            REDUCE_FFN[layer],
        )
        grad_normed_mid = scatter_rows(
            lambda first, last: sum(dot_nt(rows_of(value, first, last), up) for value, up in zip(grad_hidden, ups)),
            work,
            str(layer) + "g",
        )
        grad_b_up = jnp.concatenate([jnp.sum(value, axis=0, dtype=F32) for value in grad_hidden])
        grad_gain_ffn = jnp.sum(grad_normed_mid * unit_mid, axis=0)
        grad_shift_ffn = jnp.sum(grad_normed_mid, axis=0)
        grad_middle = grad_stream + norm_back(grad_normed_mid, unit_mid, inverse_mid, gain_ffn[layer])
        grad_attn = grad_middle.astype(BF16)
        grad_b_out = jnp.sum(grad_attn, axis=0, dtype=F32)
        attn_all = gather_rows(grad_attn, work, str(layer) + "h")
        grad_mixed = dot_nt(attn_all, weight_out).astype(BF16)
        grad_query, grad_mine, grad_beside = attend_back(query, mine, beside, log_totals, grad_mixed, info)
        grad_beside = work.at(str(layer) + "i", grad_beside)
        grad_kv = (grad_mine + swap(grad_beside, "c").astype(F32)).astype(BF16)
        work.add(
            reduce_weights(
                work,
                results,
                "attn",
                layer,
                (
                    [(inputs, grad_kv[:, : 2 * head_width]), (inputs, grad_kv[:, 2 * head_width :])],
                    [(inputs, grad_query), (attn_all, mixed)],
                ),
                (
                    (1, 0, head_width, False),
                    (0, 0, head_width, False),
                    (0, head_width, head_width, False),
                    (1, head_width, head_width, True),
                ),
            ),
            REDUCE_ATTN[layer],
        )
        grad_normed = scatter_rows(
            lambda first, last: dot_nt(rows_of(grad_query, first, last), weight_query)
            + dot_nt(rows_of(grad_kv, first, last), weight_kv),
            work,
            str(layer) + "j",
        )
        grad_b_query = jnp.sum(grad_query, axis=0, dtype=F32)
        grad_b_value = jnp.sum(grad_kv[:, 2 * head_width :], axis=0, dtype=F32)
        grads_in = grad_normed
        grad_gain_attn = jnp.sum(grad_normed * unit, axis=0)
        grad_shift_attn = jnp.sum(grad_normed, axis=0)
        grad_stream = grad_middle + norm_back(grad_normed, unit, inverse, gain_attn[layer])

        def spread(values, total):
            width = values.shape[0] // 2
            result = jnp.zeros((total,), F32)
            for index, shard in enumerate(shards):
                result = lax.dynamic_update_slice_in_dim(
                    result, values[index * width : (index + 1) * width], shard * width, 0
                )
            return result

        whole = head_width * 2 * across
        packed = jnp.concatenate(
            [
                grad_gain_attn,
                grad_shift_attn,
                grad_b_out,
                grad_gain_ffn,
                grad_shift_ffn,
                grad_b_down,
                spread(grad_b_query, whole),
                spread(grad_b_value, whole),
                spread(grad_b_up, b_up.shape[1]),
            ]
        )
        small[layer] = packed.reshape(-1, 128)

    work.add(sum_small(work, results, jnp.stack([small[layer] for layer in range(LAYERS)])), SUM_SMALL)
    work.at("t1", grads_in)
    leaving = from_chunks(grad_stream.astype(BF16), None)
    next(leaving)
    input_grad = next(leaving)
    for step in range(2, 7):
        work.at("t" + str(step), work.latest)
    assert not work.tasks
    attn_outs, ffn_outs = results["attn"], results["ffn"]
    table = results["small"].reshape(LAYERS, -1)
    wide = gain_attn.shape[1]
    shared = [table[:, index * wide : (index + 1) * wide] for index in range(6)]
    begin = 6 * wide
    whole = head_width * 2 * across
    home = shards[0]
    all_b_query = lax.dynamic_slice_in_dim(table[:, begin : begin + whole], home * head_width, head_width, 1)
    begin += whole
    all_b_value = lax.dynamic_slice_in_dim(table[:, begin : begin + whole], home * head_width, head_width, 1)
    begin += whole
    all_b_up = lax.dynamic_slice_in_dim(table[:, begin:], home * hidden_width, hidden_width, 1)
    return (
        results["activations_out"],
        input_grad,
        shared[0],
        shared[1],
        attn_outs[0],
        all_b_query,
        attn_outs[1],
        attn_outs[2],
        all_b_value,
        attn_outs[3],
        shared[2],
        shared[3],
        shared[4],
        ffn_outs[0],
        all_b_up,
        ffn_outs[1],
        shared[5],
    )


def solution(mesh):
    groups, parts = mesh.shape["dp"], mesh.shape["mp"]
    fine = Mesh(
        mesh.devices.reshape(2, groups // 4, 2, 2, parts // 2), ("ky", "kx", "c", "b", "r")
    )
    dp, mp = ("ky", "kx", "c"), ("b", "r")
    rows, whole = P(dp + mp, None), P()
    columns3, columns2, rows3 = P(None, None, mp), P(None, mp), P(None, mp, None)
    return jax.shard_map(
        local,
        mesh=fine,
        in_specs=(
            rows,
            P(dp, None),
            rows,
            whole,
            whole,
            columns3,
            columns2,
            columns3,
            columns3,
            columns2,
            rows3,
            whole,
            whole,
            whole,
            columns3,
            whole,
            rows3,
            whole,
        ),
        out_specs=(
            rows,
            rows,
            whole,
            whole,
            columns3,
            columns2,
            columns3,
            columns3,
            columns2,
            rows3,
            whole,
            whole,
            whole,
            columns3,
            columns2,
            rows3,
            whole,
        ),
        check_vma=False,
    )
```

time: 1140 us -> 595 us (0.52)
  Pallas kernels: 422 us -> 61.2 us
  starting transfers between devices: 227 us -> 106 us
  matrix products: 113 us -> 82.5 us
  local copies, waits for them, and re-layouts: 69.6 us -> 44.1 us
    pallas_call x20 -> x12, Pallas kernels: 422 us -> 61.2 us  [the longest x4 19.5 us: reduce_weights(): pl.pallas_call(functools.partial(store_kernel, layout, len(mine), len(giv...]
    ppermute x163 -> x107, starting transfers between devices: 157 us -> 92.9 us  [swap(): return lax.ppermute(value, axis, [(0, 1), (1, 0)])]
    ppermute x49 -> x0, starting transfers between devices: 48.8 us -> none  [the longest x24 28.4 us: gather_axis(): lax.ppermute(piece, (axis, 'c'), [(1, 3), (3, 1)])]
    dot_general x24 -> x0, matrix products: 23.5 us -> none  [the longest x4 8.27 us: chunk_scores(): jnp.einsum('qhd,khd->hqk', query_heads, key_heads, preferred_element_type...]
    ppermute x49 -> x0, waiting for transfers between devices: 21.7 us -> none  [the longest x8 21.6 us: reduce_pair(): got = lax.ppermute(send, ('c', 'b'), [(2, 1), (3, 0), (0, 2), (1, 3)])]
    ppermute x163 -> x107, waiting for transfers between devices: 226 us -> 245 us  [swap(): return lax.ppermute(value, axis, [(0, 1), (1, 0)])]
    dot_general x16 -> x24, matrix products: 27.9 us -> 20.8 us  [dot_tn(): return jnp.einsum('ti,to->io', left, right, preferred_element_type=F32)]
    dot_general x16 -> x22, matrix products: 26.7 us -> 29.2 us  [dot_nt(): return jnp.einsum('ti,oi->to', left, right, preferred_element_type=F32)]
  transfers between devices with their start and end apart: 220 -> 115, of which waited for: 48 -> 50; matrix products, arithmetic and copies ran while one was open for 16% -> 20% of each run, Pallas kernels for 31% -> 7%
where the time goes in v2:
time: 595 us; the launch traced here: 591 us
  waiting for transfers between devices  245 us (41%)
  starting transfers between devices  106 us (18%)
  matrix products  82.5 us (14%)
  Pallas kernels  61.2 us (10%)
  other arithmetic  46.6 us (8%)
  local copies, waits for them, and re-layouts  44.1 us (7%)
    ppermute x107, waiting for transfers between devices, swap(): return lax.ppermute(value, axis, [(0, 1), (1, 0)])  245 us
    ppermute x107, starting transfers between devices, swap(): return lax.ppermute(value, axis, [(0, 1), (1, 0)])  92.9 us
    dot_general x20, matrix products, dot(): return jnp.dot(left, right, preferred_element_type=F32)  32.4 us
    dot_general x22, matrix products, dot_nt(): return jnp.einsum('ti,oi->to', left, right, preferred_element_type=F32)  29.2 us
    unnamed x414, local copies, waits for them, and re-layouts  22.5 us
    dot_general x24, matrix products, dot_tn(): return jnp.einsum('ti,to->io', left, right, preferred_element_type=F32)  20.8 us
    pallas_call x4, Pallas kernels, reduce_weights(): pl.pallas_call(functools.partial(store_kernel, layout, len(mine), len(giv...  19.5 us
    pallas_call x2, Pallas kernels, attend_back(): pl.pallas_call(functools.partial(attend_back_kernel, size), out_shape=[ja...  19.3 us
  transfers between devices with their start and end apart: 115, of which 50 were waited for; matrix products, arithmetic and copies ran while one was open for 20% of the time, Pallas kernels for 7%

profile of v2, /device:TPU:0, one launch (start us, length us, event | category | flops | bytes accessed | tf_op | source)
XLA Modules:
  0.0 590.5 jit_solution(14821919277547231966)
XLA Ops:
  5.8 7.0 %collective-permute-start.2 = (bf16[128,1024]{1,0:T(8,128)(2,1)S(1)}, bf16[128,1024]{1,0:T(8,128)(2,1)S(1)}, u32[]{:S(2)}, u32[]{:S(2)}) collective-permute-start(bf16[128,1024]{1,0:T(8,128)(2,1)S(1)} %maximum_maximum_fusion), channel_id=1, source_target_pairs={{0,2},{2,0},{1,3},{3,1},{4,6},{6,4},{5,7},{7,5},{8,10},{10,8},{9,1... | collective-permute-start | bytes 786440 | tf_op jit(solution)/shard_map/ppermute | solution.py:69
  22.3 7.7 %collective-permute-done.2 = bf16[128,1024]{1,0:T(8,128)(2,1)S(1)} collective-permute-done((bf16[128,1024]{1,0:T(8,128)(2,1)S(1)}, bf16[128,1024]{1,0:T(8,128)(2,1)S(1)}, u32[]{:S(2)}, u32[]{:S(2)}) %collective-permute-start.2) | collective-permute-done | bytes 262176 | tf_op jit(solution)/shard_map/ppermute | solution.py:69
  61.1 4.3 add_convert_fusion.11.mine
  67.0 8.1 %collective-permute-done.12 = bf16[128,2048]{1,0:T(8,128)(2,1)} collective-permute-done((bf16[128,2048]{1,0:T(8,128)(2,1)}, bf16[128,2048]{1,0:T(8,128)(2,1)}, u32[]{:S(2)}, u32[]{:S(2)}) %collective-permute-start.12) | collective-permute-done | bytes 524320 | tf_op jit(solution)/shard_map/ppermute | solution.py:69
  80.5 6.9 %shard_map.306 = (bf16[512,512]{1,0:T(8,128)(2,1)S(1)}, f32[512,4]{1,0:T(8,128)S(1)}) custom-call(f32[4]{0:T(128)S(1)} %fusion.192.slopes, f32[256,4]{1,0:T(8,128)S(1)} %convert_element_type.525.at_rows, f32[1,1024]{1,0:T(1,128)S(1)} %convert_element_type.526.at_keys, bf16[512,512]{1,0:T(8,128)(2,1)S(1)} %fusion.83.query, ...), custom_call_target="tpu_custom_call" | custom-call | flops 805306368 | bytes 4194304 | tf_op jit(solution)/shard_map/pallas_call | solution.py:625
  95.7 9.0 %collective-permute-done.19 = bf16[128,1024]{1,0:T(8,128)(2,1)S(1)} collective-permute-done((bf16[128,1024]{1,0:T(8,128)(2,1)S(1)}, bf16[128,1024]{1,0:T(8,128)(2,1)S(1)}, u32[]{:S(2)}, u32[]{:S(2)}) %collective-permute-start.19) | collective-permute-done | bytes 262176 | tf_op jit(solution)/shard_map/ppermute | solution.py:69
  116.5 5.5 collective-permute-done.20
  122.0 5.0 multiply_convert_fusion.3
  127.7 5.8 shard_map.307
  133.6 5.0 multiply_convert_fusion.2
  148.6 9.0 %collective-permute-done.25 = bf16[256,1024]{1,0:T(8,128)(2,1)S(1)} collective-permute-done((bf16[256,1024]{1,0:T(8,128)(2,1)S(1)}, bf16[256,1024]{1,0:T(8,128)(2,1)S(1)}, u32[]{:S(2)}, u32[]{:S(2)}) %collective-permute-start.25) | collective-permute-done | bytes 524320 | tf_op jit(solution)/shard_map/ppermute | solution.py:69
  159.9 9.5 %collective-permute-done.28 = bf16[128,2048]{1,0:T(8,128)(2,1)S(1)} collective-permute-done((bf16[128,2048]{1,0:T(8,128)(2,1)S(1)}, bf16[128,2048]{1,0:T(8,128)(2,1)S(1)}, u32[]{:S(2)}, u32[]{:S(2)}) %collective-permute-start.28) | collective-permute-done | bytes 524320 | tf_op jit(solution)/shard_map/ppermute | solution.py:69
  171.5 4.5 collective-permute-done.30
  183.0 5.7 shard_map.309
  191.9 4.1 collective-permute-start.39
  196.0 12.9 %collective-permute-done.35 = bf16[256,1024]{1,0:T(8,128)(2,1)S(1)} collective-permute-done((bf16[256,1024]{1,0:T(8,128)(2,1)S(1)}, bf16[256,1024]{1,0:T(8,128)(2,1)S(1)}, u32[]{:S(2)}, u32[]{:S(2)}) %collective-permute-start.35) | collective-permute-done | bytes 524320 | tf_op jit(solution)/shard_map/ppermute | solution.py:69
  211.1 12.2 %collective-permute-done.40 = bf16[256,1024]{1,0:T(8,128)(2,1)S(1)} collective-permute-done((bf16[256,1024]{1,0:T(8,128)(2,1)S(1)}, bf16[256,1024]{1,0:T(8,128)(2,1)S(1)}, u32[]{:S(2)}, u32[]{:S(2)}) %collective-permute-start.40) | collective-permute-done | bytes 524320 | tf_op jit(solution)/shard_map/ppermute | solution.py:69
  235.4 11.3 %collective-permute-done.43 = bf16[256,1024]{1,0:T(8,128)(2,1)S(1)} collective-permute-done((bf16[256,1024]{1,0:T(8,128)(2,1)S(1)}, bf16[256,1024]{1,0:T(8,128)(2,1)S(1)}, u32[]{:S(2)}, u32[]{:S(2)}) %collective-permute-start.43) | collective-permute-done | bytes 524320 | tf_op jit(solution)/shard_map/ppermute | solution.py:69
  248.4 3.6 collective-permute-start.44
  253.4 6.6 %collective-permute-done.46 = bf16[256,1024]{1,0:T(8,128)(2,1)} collective-permute-done((bf16[256,1024]{1,0:T(8,128)(2,1)S(1)}, bf16[256,1024]{1,0:T(8,128)(2,1)}, u32[]{:S(2)}, u32[]{:S(2)}) %collective-permute-start.46) | collective-permute-done | bytes 524320 | tf_op jit(solution)/shard_map/ppermute | solution.py:69
  261.3 5.3 convert_reduce_fusion.1
  269.2 4.3 convert_reduce_fusion
  277.1 4.6 collective-permute-start.48
  293.9 9.5 %collective-permute-done.47 = bf16[256,1024]{1,0:T(8,128)(2,1)S(1)} collective-permute-done((bf16[256,1024]{1,0:T(8,128)(2,1)S(1)}, bf16[256,1024]{1,0:T(8,128)(2,1)S(1)}, u32[]{:S(2)}, u32[]{:S(2)}) %collective-permute-start.47) | collective-permute-done | bytes 524320 | tf_op jit(solution)/shard_map/ppermute | solution.py:69
  315.0 3.8 collective-permute-done.50
  319.7 8.9 %shard_map.311 = (bf16[512,512]{1,0:T(8,128)(2,1)S(1)}, f32[512,1024]{1,0:T(8,128)}, bf16[512,1024]{1,0:T(8,128)(2,1)S(1)}) custom-call(f32[4]{0:T(128)S(1)} %fusion.192.slopes, f32[256,4]{1,0:T(8,128)S(1)} %convert_element_type.525.at_rows, f32[1,1024]{1,0:T(1,128)S(1)} %convert_element_type.526.at_keys, bf16[512,512]{1,0:T(8,128)(2,1)S(1)} %copy-done.44, ...), custom_call_target="tpu_custom_call" | custom-call | flops 2013265920 | bytes 4194304 | tf_op jit(solution)/shard_map/pallas_call | solution.py:640
  329.0 6.5 %collective-permute-done.51 = bf16[256,2048]{1,0:T(8,128)(2,1)S(1)} collective-permute-done((bf16[256,2048]{1,0:T(8,128)(2,1)}, bf16[256,2048]{1,0:T(8,128)(2,1)S(1)}, u32[]{:S(2)}, u32[]{:S(2)}) %collective-permute-start.51) | collective-permute-done | bytes 1048608 | tf_op jit(solution)/shard_map/ppermute | solution.py:69
  355.9 6.0 %collective-permute-done.54 = bf16[256,1024]{1,0:T(8,128)(2,1)S(1)} collective-permute-done((bf16[256,1024]{1,0:T(8,128)(2,1)S(1)}, bf16[256,1024]{1,0:T(8,128)(2,1)S(1)}, u32[]{:S(2)}, u32[]{:S(2)}) %collective-permute-start.54) | collective-permute-done | bytes 524320 | tf_op jit(solution)/shard_map/ppermute | solution.py:69
  369.5 15.3 %collective-permute-done.59 = bf16[256,1024]{1,0:T(8,128)(2,1)S(1)} collective-permute-done((bf16[256,1024]{1,0:T(8,128)(2,1)S(1)}, bf16[256,1024]{1,0:T(8,128)(2,1)S(1)}, u32[]{:S(2)}, u32[]{:S(2)}) %collective-permute-start.59) | collective-permute-done | bytes 524320 | tf_op jit(solution)/shard_map/ppermute | solution.py:69
  402.6 4.2 collective-permute-done.65
  414.6 9.0 %collective-permute-done.68 = bf16[128,1024]{1,0:T(8,128)(2,1)S(1)} collective-permute-done((bf16[128,1024]{1,0:T(8,128)(2,1)S(1)}, bf16[128,1024]{1,0:T(8,128)(2,1)S(1)}, u32[]{:S(2)}, u32[]{:S(2)}) %collective-permute-start.68) | collective-permute-done | bytes 262176 | tf_op jit(solution)/shard_map/ppermute | solution.py:69
  432.0 6.1 %collective-permute-done.71 = bf16[256,1024]{1,0:T(8,128)(2,1)S(1)} collective-permute-done((bf16[256,1024]{1,0:T(8,128)(2,1)S(1)}, bf16[256,1024]{1,0:T(8,128)(2,1)S(1)}, u32[]{:S(2)}, u32[]{:S(2)}) %collective-permute-start.71) | collective-permute-done | bytes 524320 | tf_op jit(solution)/shard_map/ppermute | solution.py:69
  442.7 10.4 %shard_map.312 = (bf16[512,512]{1,0:T(8,128)(2,1)S(1)}, f32[512,1024]{1,0:T(8,128)}, bf16[512,1024]{1,0:T(8,128)(2,1)S(1)}) custom-call(f32[4]{0:T(128)S(1)} %fusion.192.slopes, f32[256,4]{1,0:T(8,128)S(1)} %convert_element_type.525.at_rows, f32[1,1024]{1,0:T(1,128)S(1)} %convert_element_type.526.at_keys, bf16[512,512]{1,0:T(8,128)(2,1)S(1)} %copy-done.42, ...), custom_call_target="tpu_custom_call" | custom-call | flops 2013265920 | bytes 4194304 | tf_op jit(solution)/shard_map/pallas_call | solution.py:640
  458.1 4.8 collective-permute-done.75
  478.1 5.5 shard_map.313
  484.4 5.2 collective-permute-done.86
  496.8 3.4 collective-permute-done.89
  501.2 9.3 %collective-permute-done.91 = bf16[256,1024]{1,0:T(8,128)(2,1)S(1)} collective-permute-done((bf16[256,1024]{1,0:T(8,128)(2,1)S(1)}, bf16[256,1024]{1,0:T(8,128)(2,1)S(1)}, u32[]{:S(2)}, u32[]{:S(2)}) %collective-permute-start.91) | collective-permute-done | bytes 524320 | tf_op jit(solution)/shard_map/ppermute | solution.py:69
  510.8 9.1 %collective-permute-done.94 = bf16[128,2048]{1,0:T(8,128)(2,1)S(1)} collective-permute-done((bf16[128,2048]{1,0:T(8,128)(2,1)S(1)}, bf16[128,2048]{1,0:T(8,128)(2,1)S(1)}, u32[]{:S(2)}, u32[]{:S(2)}) %collective-permute-start.94) | collective-permute-done | bytes 524320 | tf_op jit(solution)/shard_map/ppermute | solution.py:69
  530.6 4.4 collective-permute-done.97
  544.1 4.4 shard_map.314
  548.5 3.4 collective-permute-done.102
  552.5 3.7 collective-permute-done.104
  558.0 3.6 collective-permute-done.106
  561.8 4.7 collective-permute-done.105
  572.4 5.1 collective-permute-done.108
  577.6 5.3 shard_map.315
  586.0 4.4 shard_map.316
  (897 shorter events, 271.9 us)
Async XLA Ops:
  1.8 20.4 %collective-permute-start.1 = (bf16[128,1024]{1,0:T(8,128)(2,1)S(1)}, bf16[128,1024]{1,0:T(8,128)(2,1)S(1)}, u32[]{:S(2)}, u32[]{:S(2)}) collective-permute-start(bf16[128,1024]{1,0:T(8,128)(2,1)S(1)} %get-tuple-element.553), channel_id=1, source_target_pairs={{0,4},{2,0},{4,6},{6,2},{1,5},{3,1},{5,7},{7,3},{8,12},{10,8},{12,... | collective-permute-start | bytes 786440 | tf_op jit(solution)/shard_map/ppermute | solution.py:112
  2.4 19.9 %collective-permute-start = (bf16[128,1024]{1,0:T(8,128)(2,1)S(1)}, bf16[128,1024]{1,0:T(8,128)(2,1)S(1)}, u32[]{:S(2)}, u32[]{:S(2)}) collective-permute-start(bf16[128,1024]{1,0:T(8,128)(2,1)S(1)} %get-tuple-element.552), channel_id=1, source_target_pairs={{0,0},{2,4},{4,2},{6,6},{1,1},{3,5},{5,3},{7,7},{8,8},{10,12},{12,... | collective-permute-start | bytes 786440 | tf_op jit(solution)/shard_map/ppermute | solution.py:111
  5.8 24.2 %collective-permute-start.2 = (bf16[128,1024]{1,0:T(8,128)(2,1)S(1)}, bf16[128,1024]{1,0:T(8,128)(2,1)S(1)}, u32[]{:S(2)}, u32[]{:S(2)}) collective-permute-start(bf16[128,1024]{1,0:T(8,128)(2,1)S(1)} %maximum_maximum_fusion), channel_id=1, source_target_pairs={{0,2},{2,0},{1,3},{3,1},{4,6},{6,4},{5,7},{7,5},{8,10},{10,8},{9,1... | collective-permute-start | bytes 786440 | tf_op jit(solution)/shard_map/ppermute | solution.py:69
  12.8 53.0 %collective-permute-start.3 = (s32[4]{0:T(128)}, s32[4]{0:T(128)}, u32[]{:S(2)}, u32[]{:S(2)}) collective-permute-start(s32[4]{0:T(128)} %bitcast.5), channel_id=1, source_target_pairs={{0,4},{4,0},{1,5},{5,1},{2,6},{6,2},{3,7},{7,3},{8,12},{12,8},{9,1... | collective-permute-start | bytes 56 | tf_op jit(solution)/shard_map/ppermute | solution.py:69
  13.4 34.6 %collective-permute-start.11 = (f32[2,512]{1,0:T(2,128)}, f32[2,512]{1,0:T(2,128)}, u32[]{:S(2)}, u32[]{:S(2)}) collective-permute-start(f32[2,512]{1,0:T(2,128)} %pad_maximum_fusion.52), channel_id=1, source_target_pairs={{0,2},{2,0},{1,3},{3,1},{4,6},{6,4},{5,7},{7,5},{8,10},{10,8},{9,1... | collective-permute-start | bytes 12296 | tf_op jit(solution)/shard_map/ppermute | solution.py:69
  49.9 25.2 %collective-permute-start.12 = (bf16[128,2048]{1,0:T(8,128)(2,1)}, bf16[128,2048]{1,0:T(8,128)(2,1)}, u32[]{:S(2)}, u32[]{:S(2)}) collective-permute-start(bf16[128,2048]{1,0:T(8,128)(2,1)} %pad_maximum_fusion.28), channel_id=1, source_target_pairs={{0,2},{2,0},{1,3},{3,1},{4,6},{6,4},{5,7},{7,5},{8,10},{10,8},{9,1... | collective-permute-start | bytes 1572872 | tf_op jit(solution)/shard_map/ppermute | solution.py:69
  65.3 15.2 %collective-permute-start.13 = (bf16[512,1024]{1,0:T(8,128)(2,1)}, bf16[512,1024]{1,0:T(8,128)(2,1)}, u32[]{:S(2)}, u32[]{:S(2)}) collective-permute-start(bf16[512,1024]{1,0:T(8,128)(2,1)} %add_convert_fusion.11.mine), channel_id=1, source_target_pairs={{0,4},{4,0},{1,5},{5,1},{2,6},{6,2},{3,7},{7,3},{8,12},{12,8},{9,1... | collective-permute-start | bytes 3145736 | tf_op jit(solution)/shard_map/ppermute | solution.py:69
  87.9 19.0 %collective-permute-start.16 = (bf16[256,1024]{1,0:T(8,128)(2,1)S(1)}, bf16[256,1024]{1,0:T(8,128)(2,1)S(1)}, u32[]{:S(2)}, u32[]{:S(2)}) collective-permute-start(bf16[256,1024]{1,0:T(8,128)(2,1)S(1)} %convolution_convert_fusion.25), channel_id=1, source_target_pairs={{0,1},{1,0},{2,3},{3,2},{4,5},{5,4},{6,7},{7,6},{8,9},{9,8},{10,11... | collective-permute-start | bytes 1572872 | tf_op jit(solution)/shard_map/ppermute | solution.py:69
  88.1 18.9 %collective-permute-start.17 = (bf16[2,128,1024]{2,1,0:T(8,128)(2,1)S(1)}, bf16[2,128,1024]{2,1,0:T(8,128)(2,1)S(1)}, u32[]{:S(2)}, u32[]{:S(2)}) collective-permute-start(bf16[2,128,1024]{2,1,0:T(8,128)(2,1)S(1)} %pad_maximum_fusion.29), channel_id=1, source_target_pairs={{0,16},{16,0},{1,17},{17,1},{2,18},{18,2},{3,19},{19,3},{4,20},{20... | collective-permute-start | bytes 1572872 | tf_op jit(solution)/shard_map/ppermute | solution.py:69
  89.6 17.3 %collective-permute-start.18 = (bf16[2,128,1024]{2,1,0:T(8,128)(2,1)S(1)}, bf16[2,128,1024]{2,1,0:T(8,128)(2,1)S(1)}, u32[]{:S(2)}, u32[]{:S(2)}) collective-permute-start(bf16[2,128,1024]{2,1,0:T(8,128)(2,1)S(1)} %pad_maximum_fusion.30), channel_id=1, source_target_pairs={{0,8},{8,0},{1,9},{9,1},{2,10},{10,2},{3,11},{11,3},{4,12},{12,4},... | collective-permute-start | bytes 1572872 | tf_op jit(solution)/shard_map/ppermute | solution.py:69
  139.3 18.3 %collective-permute-start.25 = (bf16[256,1024]{1,0:T(8,128)(2,1)S(1)}, bf16[256,1024]{1,0:T(8,128)(2,1)S(1)}, u32[]{:S(2)}, u32[]{:S(2)}) collective-permute-start(bf16[256,1024]{1,0:T(8,128)(2,1)S(1)} %fusion.87), channel_id=1, source_target_pairs={{0,1},{1,0},{2,3},{3,2},{4,5},{5,4},{6,7},{7,6},{8,9},{9,8},{10,11... | collective-permute-start | bytes 1572872 | tf_op jit(solution)/shard_map/ppermute | solution.py:69
  146.0 23.4 %collective-permute-start.28 = (bf16[128,2048]{1,0:T(8,128)(2,1)S(1)}, bf16[128,2048]{1,0:T(8,128)(2,1)S(1)}, u32[]{:S(2)}, u32[]{:S(2)}) collective-permute-start(bf16[128,2048]{1,0:T(8,128)(2,1)S(1)} %copy-done.83), channel_id=1, source_target_pairs={{0,2},{2,0},{1,3},{3,1},{4,6},{6,4},{5,7},{7,5},{8,10},{10,8},{9,1... | collective-permute-start | bytes 1572872 | tf_op jit(solution)/shard_map/ppermute | solution.py:69
  159.1 16.8 %collective-permute-start.29 = (bf16[256,1024]{1,0:T(8,128)(2,1)S(1)}, bf16[256,1024]{1,0:T(8,128)(2,1)S(1)}, u32[]{:S(2)}, u32[]{:S(2)}) collective-permute-start(bf16[256,1024]{1,0:T(8,128)(2,1)S(1)} %add_convert_fusion.26), channel_id=1, source_target_pairs={{0,1},{1,0},{2,3},{3,2},{4,5},{5,4},{6,7},{7,6},{8,9},{9,8},{10,11... | collective-permute-start | bytes 1572872 | tf_op jit(solution)/shard_map/ppermute | solution.py:69
  159.3 18.3 %collective-permute-start.32 = (bf16[4,128,512]{2,1,0:T(8,128)(2,1)S(1)}, bf16[4,128,512]{2,1,0:T(8,128)(2,1)S(1)}, u32[]{:S(2)}, u32[]{:S(2)}) collective-permute-start(bf16[4,128,512]{2,1,0:T(8,128)(2,1)S(1)} %constant_dynamic-update-slice_fusion.18.kv), channel_id=1, source_target_pairs={{0,4},{4,0},{1,5},{5,1},{2,6},{6,2},{3,7},{7,3},{8,12},{12,8},{9,1... | collective-permute-start | bytes 1572872 | tf_op jit(solution)/shard_map/ppermute | solution.py:69
  159.4 18.2 %collective-permute-start.33 = (bf16[4,128,512]{2,1,0:T(8,128)(2,1)S(1)}, bf16[4,128,512]{2,1,0:T(8,128)(2,1)S(1)}, u32[]{:S(2)}, u32[]{:S(2)}) collective-permute-start(bf16[4,128,512]{2,1,0:T(8,128)(2,1)S(1)} %constant_dynamic-update-slice_fusion.20.qo), channel_id=1, source_target_pairs={{0,4},{4,0},{1,5},{5,1},{2,6},{6,2},{3,7},{7,3},{8,12},{12,8},{9,1... | collective-permute-start | bytes 1572872 | tf_op jit(solution)/shard_map/ppermute | solution.py:69
  189.2 19.7 %collective-permute-start.35 = (bf16[256,1024]{1,0:T(8,128)(2,1)S(1)}, bf16[256,1024]{1,0:T(8,128)(2,1)S(1)}, u32[]{:S(2)}, u32[]{:S(2)}) collective-permute-start(bf16[256,1024]{1,0:T(8,128)(2,1)S(1)} %convolution_convert_fusion.24), channel_id=1, source_target_pairs={{0,1},{1,0},{2,3},{3,2},{4,5},{5,4},{6,7},{7,6},{8,9},{9,8},{10,11... | collective-permute-start | bytes 1572872 | tf_op jit(solution)/shard_map/ppermute | solution.py:69
  189.4 19.5 %collective-permute-start.36 = (bf16[2,128,1024]{2,1,0:T(8,128)(2,1)S(1)}, bf16[2,128,1024]{2,1,0:T(8,128)(2,1)S(1)}, u32[]{:S(2)}, u32[]{:S(2)}) collective-permute-start(bf16[2,128,1024]{2,1,0:T(8,128)(2,1)S(1)} %pad_maximum_fusion.32), channel_id=1, source_target_pairs={{0,16},{16,0},{1,17},{17,1},{2,18},{18,2},{3,19},{19,3},{4,20},{20... | collective-permute-start | bytes 1572872 | tf_op jit(solution)/shard_map/ppermute | solution.py:69
  189.8 19.1 %collective-permute-start.37 = (bf16[2,128,1024]{2,1,0:T(8,128)(2,1)S(1)}, bf16[2,128,1024]{2,1,0:T(8,128)(2,1)S(1)}, u32[]{:S(2)}, u32[]{:S(2)}) collective-permute-start(bf16[2,128,1024]{2,1,0:T(8,128)(2,1)S(1)} %pad_maximum_fusion.33), channel_id=1, source_target_pairs={{0,8},{8,0},{1,9},{9,1},{2,10},{10,2},{3,11},{11,3},{4,12},{12,4},... | collective-permute-start | bytes 1572872 | tf_op jit(solution)/shard_map/ppermute | solution.py:69
  191.2 17.7 %collective-permute-start.38 = (bf16[128,1024]{1,0:T(8,128)(2,1)S(1)}, bf16[128,1024]{1,0:T(8,128)(2,1)S(1)}, u32[]{:S(2)}, u32[]{:S(2)}) collective-permute-start(bf16[128,1024]{1,0:T(8,128)(2,1)S(1)} %get-tuple-element.547), channel_id=1, source_target_pairs={{0,0},{2,4},{4,2},{6,6},{1,1},{3,5},{5,3},{7,7},{8,8},{10,12},{12,... | collective-permute-start | bytes 786440 | tf_op jit(solution)/shard_map/ppermute | solution.py:111
  191.9 17.0 %collective-permute-start.39 = (bf16[128,1024]{1,0:T(8,128)(2,1)S(1)}, bf16[128,1024]{1,0:T(8,128)(2,1)S(1)}, u32[]{:S(2)}, u32[]{:S(2)}) collective-permute-start(bf16[128,1024]{1,0:T(8,128)(2,1)S(1)} %get-tuple-element.546), channel_id=1, source_target_pairs={{0,4},{2,0},{4,6},{6,2},{1,5},{3,1},{5,7},{7,3},{8,12},{10,8},{12,... | collective-permute-start | bytes 786440 | tf_op jit(solution)/shard_map/ppermute | solution.py:112
  210.4 16.6 %collective-permute-start.41 = (bf16[4,128,1024]{2,1,0:T(8,128)(2,1)S(1)}, bf16[4,128,1024]{2,1,0:T(8,128)(2,1)S(1)}, u32[]{:S(2)}, u32[]{:S(2)}) collective-permute-start(bf16[4,128,1024]{2,1,0:T(8,128)(2,1)S(1)} %constant_dynamic-update-slice_fusion.22.up), channel_id=1, source_target_pairs={{0,4},{4,0},{1,5},{5,1},{2,6},{6,2},{3,7},{7,3},{8,12},{12,8},{9,1... | collective-permute-start | bytes 3145736 | tf_op jit(solution)/shard_map/ppermute | solution.py:69
  210.6 16.5 %collective-permute-start.42 = (bf16[4,128,1024]{2,1,0:T(8,128)(2,1)S(1)}, bf16[4,128,1024]{2,1,0:T(8,128)(2,1)S(1)}, u32[]{:S(2)}, u32[]{:S(2)}) collective-permute-start(bf16[4,128,1024]{2,1,0:T(8,128)(2,1)S(1)} %constant_dynamic-update-slice_fusion.24.down), channel_id=1, source_target_pairs={{0,4},{4,0},{1,5},{5,1},{2,6},{6,2},{3,7},{7,3},{8,12},{12,8},{9,1... | collective-permute-start | bytes 3145736 | tf_op jit(solution)/shard_map/ppermute | solution.py:69
  233.0 27.1 %collective-permute-start.46 = (bf16[256,1024]{1,0:T(8,128)(2,1)S(1)}, bf16[256,1024]{1,0:T(8,128)(2,1)}, u32[]{:S(2)}, u32[]{:S(2)}) collective-permute-start(bf16[256,1024]{1,0:T(8,128)(2,1)S(1)} %get-tuple-element.522), channel_id=1, source_target_pairs={{0,1},{1,0},{2,3},{3,2},{4,5},{5,4},{6,7},{7,6},{8,9},{9,8},{10,11... | collective-permute-start | bytes 1572872 | tf_op jit(solution)/shard_map/ppermute | solution.py:69
  277.1 26.3 %collective-permute-start.48 = (bf16[512,2048]{1,0:T(8,128)(2,1)}, bf16[512,2048]{1,0:T(8,128)(2,1)}, u32[]{:S(2)}, u32[]{:S(2)}) collective-permute-start(bf16[512,2048]{1,0:T(8,128)(2,1)} %convolution_convert_fusion.5), channel_id=1, source_target_pairs={{0,4},{4,0},{1,5},{5,1},{2,6},{6,2},{3,7},{7,3},{8,12},{12,8},{9,1... | collective-permute-start | bytes 6291464 | tf_op jit(solution)/shard_map/ppermute | solution.py:69
  284.3 19.1 %collective-permute-start.49 = (bf16[512,2048]{1,0:T(8,128)(2,1)}, bf16[512,2048]{1,0:T(8,128)(2,1)}, u32[]{:S(2)}, u32[]{:S(2)}) collective-permute-start(bf16[512,2048]{1,0:T(8,128)(2,1)} %convolution_convert_fusion.4), channel_id=1, source_target_pairs={{0,4},{4,0},{1,5},{5,1},{2,6},{6,2},{3,7},{7,3},{8,12},{12,8},{9,1... | collective-permute-start | bytes 6291464 | tf_op jit(solution)/shard_map/ppermute | solution.py:69
  310.5 25.0 %collective-permute-start.51 = (bf16[256,2048]{1,0:T(8,128)(2,1)}, bf16[256,2048]{1,0:T(8,128)(2,1)S(1)}, u32[]{:S(2)}, u32[]{:S(2)}) collective-permute-start(bf16[256,2048]{1,0:T(8,128)(2,1)} %add_convert_fusion.9), channel_id=1, source_target_pairs={{0,8},{8,0},{1,9},{9,1},{2,10},{10,2},{3,11},{11,3},{4,12},{12,4},... | collective-permute-start | bytes 3145736 | tf_op jit(solution)/shard_map/ppermute | solution.py:69
  313.8 24.8 %collective-permute-start.52 = (bf16[256,2048]{1,0:T(8,128)(2,1)}, bf16[256,2048]{1,0:T(8,128)(2,1)S(1)}, u32[]{:S(2)}, u32[]{:S(2)}) collective-permute-start(bf16[256,2048]{1,0:T(8,128)(2,1)} %add_convert_fusion.8), channel_id=1, source_target_pairs={{0,16},{16,0},{1,17},{17,1},{2,18},{18,2},{3,19},{19,3},{4,20},{20... | collective-permute-start | bytes 3145736 | tf_op jit(solution)/shard_map/ppermute | solution.py:69
  340.8 15.1 %collective-permute-start.55 = (bf16[128,2048]{1,0:T(8,128)(2,1)S(1)}, bf16[128,2048]{1,0:T(8,128)(2,1)S(1)}, u32[]{:S(2)}, u32[]{:S(2)}) collective-permute-start(bf16[128,2048]{1,0:T(8,128)(2,1)S(1)} %constant_dynamic-slice_fusion.10), channel_id=1, source_target_pairs={{0,16},{16,0},{1,17},{17,1},{2,18},{18,2},{3,19},{19,3},{4,20},{20... | collective-permute-start | bytes 1572872 | tf_op jit(solution)/shard_map/ppermute | solution.py:69
  344.2 17.7 %collective-permute-start.56 = (bf16[128,2048]{1,0:T(8,128)(2,1)S(1)}, bf16[128,2048]{1,0:T(8,128)(2,1)S(1)}, u32[]{:S(2)}, u32[]{:S(2)}) collective-permute-start(bf16[128,2048]{1,0:T(8,128)(2,1)S(1)} %constant_dynamic-slice_fusion.9), channel_id=1, source_target_pairs={{0,8},{8,0},{1,9},{9,1},{2,10},{10,2},{3,11},{11,3},{4,12},{12,4},... | collective-permute-start | bytes 1572872 | tf_op jit(solution)/shard_map/ppermute | solution.py:69
  363.9 21.0 %collective-permute-start.59 = (bf16[256,1024]{1,0:T(8,128)(2,1)S(1)}, bf16[256,1024]{1,0:T(8,128)(2,1)S(1)}, u32[]{:S(2)}, u32[]{:S(2)}) collective-permute-start(bf16[256,1024]{1,0:T(8,128)(2,1)S(1)} %get-tuple-element.516), channel_id=1, source_target_pairs={{0,1},{1,0},{2,3},{3,2},{4,5},{5,4},{6,7},{7,6},{8,9},{9,8},{10,11... | collective-permute-start | bytes 1572872 | tf_op jit(solution)/shard_map/ppermute | solution.py:69
  365.1 19.7 %collective-permute-start.60 = (bf16[256,1024]{1,0:T(8,128)(2,1)S(1)}, bf16[256,1024]{1,0:T(8,128)(2,1)S(1)}, u32[]{:S(2)}, u32[]{:S(2)}) collective-permute-start(bf16[256,1024]{1,0:T(8,128)(2,1)S(1)} %add_convert_fusion.24), channel_id=1, source_target_pairs={{0,8},{8,0},{1,9},{9,1},{2,10},{10,2},{3,11},{11,3},{4,12},{12,4},... | collective-permute-start | bytes 1572872 | tf_op jit(solution)/shard_map/ppermute | solution.py:69
  366.6 18.3 %collective-permute-start.61 = (bf16[256,1024]{1,0:T(8,128)(2,1)S(1)}, bf16[256,1024]{1,0:T(8,128)(2,1)S(1)}, u32[]{:S(2)}, u32[]{:S(2)}) collective-permute-start(bf16[256,1024]{1,0:T(8,128)(2,1)S(1)} %add_convert_fusion.23), channel_id=1, source_target_pairs={{0,16},{16,0},{1,17},{17,1},{2,18},{18,2},{3,19},{19,3},{4,20},{20... | collective-permute-start | bytes 1572872 | tf_op jit(solution)/shard_map/ppermute | solution.py:69
  367.9 30.6 %collective-permute-start.63 = (bf16[128,2048]{1,0:T(8,128)(2,1)S(1)}, bf16[128,2048]{1,0:T(8,128)(2,1)S(1)}, u32[]{:S(2)}, u32[]{:S(2)}) collective-permute-start(bf16[128,2048]{1,0:T(8,128)(2,1)S(1)} %pad_maximum_fusion.34), channel_id=1, source_target_pairs={{0,2},{2,0},{1,3},{3,1},{4,6},{6,4},{5,7},{7,5},{8,10},{10,8},{9,1... | collective-permute-start | bytes 1572872 | tf_op jit(solution)/shard_map/ppermute | solution.py:69
  393.1 17.0 %collective-permute-start.62 = (bf16[256,1024]{1,0:T(8,128)(2,1)S(1)}, bf16[256,1024]{1,0:T(8,128)(2,1)S(1)}, u32[]{:S(2)}, u32[]{:S(2)}) collective-permute-start(bf16[256,1024]{1,0:T(8,128)(2,1)S(1)} %fusion.90), channel_id=1, source_target_pairs={{0,1},{1,0},{2,3},{3,2},{4,5},{5,4},{6,7},{7,6},{8,9},{9,8},{10,11... | collective-permute-start | bytes 1572872 | tf_op jit(solution)/shard_map/ppermute | solution.py:69
  396.0 27.5 %collective-permute-start.69 = (bf16[512,2048]{1,0:T(8,128)(2,1)S(1)}, bf16[512,2048]{1,0:T(8,128)(2,1)S(1)}, u32[]{:S(2)}, u32[]{:S(2)}) collective-permute-start(bf16[512,2048]{1,0:T(8,128)(2,1)S(1)} %convolution_convert_fusion.1), channel_id=1, source_target_pairs={{0,4},{4,0},{1,5},{5,1},{2,6},{6,2},{3,7},{7,3},{8,12},{12,8},{9,1... | collective-permute-start | bytes 6291464 | tf_op jit(solution)/shard_map/ppermute | solution.py:69
  397.4 26.1 %collective-permute-start.70 = (bf16[512,2048]{1,0:T(8,128)(2,1)S(1)}, bf16[512,2048]{1,0:T(8,128)(2,1)S(1)}, u32[]{:S(2)}, u32[]{:S(2)}) collective-permute-start(bf16[512,2048]{1,0:T(8,128)(2,1)S(1)} %convolution_convert_fusion), channel_id=1, source_target_pairs={{0,4},{4,0},{1,5},{5,1},{2,6},{6,2},{3,7},{7,3},{8,12},{12,8},{9,1... | collective-permute-start | bytes 6291464 | tf_op jit(solution)/shard_map/ppermute | solution.py:69
  425.9 14.9 %collective-permute-start.72 = (bf16[2,128,1024]{2,1,0:T(8,128)(2,1)S(1)}, bf16[2,128,1024]{2,1,0:T(8,128)(2,1)S(1)}, u32[]{:S(2)}, u32[]{:S(2)}) collective-permute-start(bf16[2,128,1024]{2,1,0:T(8,128)(2,1)S(1)} %pad_maximum_fusion.35), channel_id=1, source_target_pairs={{0,16},{16,0},{1,17},{17,1},{2,18},{18,2},{3,19},{19,3},{4,20},{20... | collective-permute-start | bytes 1572872 | tf_op jit(solution)/shard_map/ppermute | solution.py:69
  426.9 14.9 %collective-permute-start.73 = (bf16[2,128,1024]{2,1,0:T(8,128)(2,1)S(1)}, bf16[2,128,1024]{2,1,0:T(8,128)(2,1)S(1)}, u32[]{:S(2)}, u32[]{:S(2)}) collective-permute-start(bf16[2,128,1024]{2,1,0:T(8,128)(2,1)S(1)} %pad_maximum_fusion.36), channel_id=1, source_target_pairs={{0,8},{8,0},{1,9},{9,1},{2,10},{10,2},{3,11},{11,3},{4,12},{12,4},... | collective-permute-start | bytes 1572872 | tf_op jit(solution)/shard_map/ppermute | solution.py:69
  428.8 34.1 %collective-permute-start.75 = (bf16[256,2048]{1,0:T(8,128)(2,1)S(1)}, bf16[256,2048]{1,0:T(8,128)(2,1)S(1)}, u32[]{:S(2)}, u32[]{:S(2)}) collective-permute-start(bf16[256,2048]{1,0:T(8,128)(2,1)S(1)} %add_convert_fusion.3), channel_id=1, source_target_pairs={{0,8},{8,0},{1,9},{9,1},{2,10},{10,2},{3,11},{11,3},{4,12},{12,4},... | collective-permute-start | bytes 3145736 | tf_op jit(solution)/shard_map/ppermute | solution.py:69
  430.9 32.1 %collective-permute-start.76 = (bf16[256,2048]{1,0:T(8,128)(2,1)}, bf16[256,2048]{1,0:T(8,128)(2,1)S(1)}, u32[]{:S(2)}, u32[]{:S(2)}) collective-permute-start(bf16[256,2048]{1,0:T(8,128)(2,1)} %add_convert_fusion.2), channel_id=1, source_target_pairs={{0,16},{16,0},{1,17},{17,1},{2,18},{18,2},{3,19},{19,3},{4,20},{20... | collective-permute-start | bytes 3145736 | tf_op jit(solution)/shard_map/ppermute | solution.py:69
  464.3 19.3 %collective-permute-start.79 = (bf16[256,1024]{1,0:T(8,128)(2,1)S(1)}, bf16[256,1024]{1,0:T(8,128)(2,1)S(1)}, u32[]{:S(2)}, u32[]{:S(2)}) collective-permute-start(bf16[256,1024]{1,0:T(8,128)(2,1)S(1)} %fusion.86), channel_id=1, source_target_pairs={{0,1},{1,0},{2,3},{3,2},{4,5},{5,4},{6,7},{7,6},{8,9},{9,8},{10,11... | collective-permute-start | bytes 1572872 | tf_op jit(solution)/shard_map/ppermute | solution.py:69
  493.6 16.9 %collective-permute-start.91 = (bf16[256,1024]{1,0:T(8,128)(2,1)S(1)}, bf16[256,1024]{1,0:T(8,128)(2,1)S(1)}, u32[]{:S(2)}, u32[]{:S(2)}) collective-permute-start(bf16[256,1024]{1,0:T(8,128)(2,1)S(1)} %add_convert_fusion.16), channel_id=1, source_target_pairs={{0,8},{8,0},{1,9},{9,1},{2,10},{10,2},{3,11},{11,3},{4,12},{12,4},... | collective-permute-start | bytes 1572872 | tf_op jit(solution)/shard_map/ppermute | solution.py:69
  494.5 16.0 %collective-permute-start.92 = (bf16[256,1024]{1,0:T(8,128)(2,1)S(1)}, bf16[256,1024]{1,0:T(8,128)(2,1)S(1)}, u32[]{:S(2)}, u32[]{:S(2)}) collective-permute-start(bf16[256,1024]{1,0:T(8,128)(2,1)S(1)} %add_convert_fusion.15), channel_id=1, source_target_pairs={{0,16},{16,0},{1,17},{17,1},{2,18},{18,2},{3,19},{19,3},{4,20},{20... | collective-permute-start | bytes 1572872 | tf_op jit(solution)/shard_map/ppermute | solution.py:69
  495.9 24.0 %collective-permute-start.94 = (bf16[128,2048]{1,0:T(8,128)(2,1)S(1)}, bf16[128,2048]{1,0:T(8,128)(2,1)S(1)}, u32[]{:S(2)}, u32[]{:S(2)}) collective-permute-start(bf16[128,2048]{1,0:T(8,128)(2,1)S(1)} %pad_maximum_fusion.37), channel_id=1, source_target_pairs={{0,2},{2,0},{1,3},{3,1},{4,6},{6,4},{5,7},{7,5},{8,10},{10,8},{9,1... | collective-permute-start | bytes 1572872 | tf_op jit(solution)/shard_map/ppermute | solution.py:69
  539.6 16.5 %collective-permute-start.104 = (bf16[128,1024]{1,0:T(8,128)(2,1)S(1)}, bf16[128,1024]{1,0:T(8,128)(2,1)S(1)}, u32[]{:S(2)}, u32[]{:S(2)}) collective-permute-start(bf16[128,1024]{1,0:T(8,128)(2,1)S(1)} %pad_maximum_fusion.47), channel_id=1, source_target_pairs={{0,2},{2,0},{1,3},{3,1},{4,6},{6,4},{5,7},{7,5},{8,10},{10,8},{9,1... | collective-permute-start | bytes 786440 | tf_op jit(solution)/shard_map/ppermute | solution.py:69
  540.1 16.0 %collective-permute-start.99 = (f32[2,96,128]{2,1,0:T(8,128)S(1)}, f32[2,96,128]{2,1,0:T(8,128)S(1)}, u32[]{:S(2)}, u32[]{:S(2)}) collective-permute-start(f32[2,96,128]{2,1,0:T(8,128)S(1)} %add.1261), channel_id=1, source_target_pairs={{0,16},{16,0},{1,17},{17,1},{2,18},{18,2},{3,19},{19,3},{4,20},{20... | collective-permute-start | bytes 294920 | tf_op jit(solution)/shard_map/ppermute | solution.py:69
  541.1 28.3 %collective-permute-start.85 = (bf16[128,1024]{1,0:T(8,128)(2,1)S(1)}, bf16[128,1024]{1,0:T(8,128)(2,1)S(1)}, u32[]{:S(2)}, u32[]{:S(2)}) collective-permute-start(bf16[128,1024]{1,0:T(8,128)(2,1)S(1)} %get-tuple-element.541), channel_id=1, source_target_pairs={{4,0},{0,2},{6,4},{2,6},{5,1},{1,3},{7,5},{3,7},{12,8},{8,10},{14,... | collective-permute-start | bytes 786440 | tf_op jit(solution)/shard_map/ppermute | solution.py:125
  551.8 17.6 %collective-permute-start.84 = (bf16[128,1024]{1,0:T(8,128)(2,1)S(1)}, bf16[128,1024]{1,0:T(8,128)(2,1)S(1)}, u32[]{:S(2)}, u32[]{:S(2)}) collective-permute-start(bf16[128,1024]{1,0:T(8,128)(2,1)S(1)} %get-tuple-element.540), channel_id=1, source_target_pairs={{0,0},{4,2},{2,4},{6,6},{1,1},{5,3},{3,5},{7,7},{8,8},{12,10},{10,... | collective-permute-start | bytes 786440 | tf_op jit(solution)/shard_map/ppermute | solution.py:124
  (256 other events, 2376.9 us)

commit v3 on v2

--- a/solution.py
+++ b/solution.py
@@ -16,7 +16,7 @@
 BF16 = jnp.bfloat16
 PLANE = ("c", "kx", "ky")
 FETCH_ATTN = ("r", "0a", None, None), ("0c", "0d", "0e", "1a")
-FETCH_FFN = (("s", 3), "0b", "0c", "0c2"), ("0e", "1a", "1c", "1c2")
+FETCH_FFN = (("s", 3), "0b", "0c", "0d", "0d2"), ("0e", (None, 1), "1a", "1c", "1c2")
 COTANGENT = "1c"
 ACTIVATIONS_OUT = "1f"
 REDUCE_FFN = (
@@ -285,7 +285,7 @@
     return pl.BlockSpec(block, lambda step, spots: (lead, spots[order * 8 + step], 0))
 
 
-def place_call(kernel, mine, beside, owns, own_specs, outs, out_specs):
+def place_call(kernel, memory, mine, beside, owns, own_specs, outs, out_specs):
     size = sum(math_prod(shape) for shape in outs)
     return pl.pallas_call(
         kernel,
@@ -296,7 +296,7 @@
             in_specs=piece_specs(mine) + own_specs,
             out_specs=out_specs,
         ),
-        compiler_params=pltpu.CompilerParams(vmem_limit_bytes=24 << 20),
+        compiler_params=pltpu.CompilerParams(vmem_limit_bytes=memory << 20),
         cost_estimate=pl.CostEstimate(flops=0, bytes_accessed=size * 4, transcendentals=0),
     )(plane_places(False), *mine, *beside, *owns)
 
@@ -324,6 +324,7 @@
         mine, beside = yield from spread_steps(work, pieces, token)
         query, kv, out = place_call(
             place_attn_kernel,
+            24 if layer else 56,
             mine,
             beside,
             (w_query, w_key, w_value, w_out),
@@ -352,18 +353,16 @@
     depth, width = w_up.shape[1], w_up.shape[2]
     rows, down_rows = depth // count, width // count
     pieces = [cut_piece(weight, layer) for weight in (w_up, w_down)]
-    token, span = yield
-    if width == depth:
-        moved = swap(after(jnp.concatenate(pieces, 1), token), "b")
-        pieces = [moved[:, :width], moved[:, width:]]
-    else:
-        pieces = [swap(piece, "b") for piece in after_all(pieces, token)]
-    work.expect(pieces, span)
+    for index, piece in enumerate(pieces):
+        token, span = yield
+        pieces[index] = swap(after(piece, token), "b")
+        work.expect(pieces[index : index + 1], span)
     token = yield
     if small_plane() and width == depth:
         mine, beside = yield from spread_steps(work, pieces, token)
         used["ffn", layer] = place_call(
             place_ffn_kernel,
+            24,
             mine,
             beside,
             (),
@@ -428,10 +427,13 @@
         kept, beside = after_all(kept, token), after_all(beside, token)
         got = [swap(cut(half, True).astype(BF16), ORDERS[half][0]) for half in range(2)]
         work.expect(got, span)
-        near = [cut(half, False) for half in range(2)]
+        near = [cut(half, False).astype(BF16) for half in range(2)]
         token, span = yield
         size = size // 4
-        totals = [(value + part.astype(F32)).astype(BF16) for value, part in zip(near, after_all(got, token))]
+        totals = [
+            (value.astype(F32) + part.astype(F32)).astype(BF16)
+            for value, part in zip(near, after_all(got, token))
+        ]
         work.latest = totals[0]
         index = [lax.axis_index(order[1]) for order in ORDERS]
         got = [
@@ -465,8 +467,8 @@
     work.latest = pieces[0]
     rows = depth // plane_count()
     shapes = [(LAYERS, w, depth) if turn else (LAYERS, depth, w) for _, _, w, turn in layout]
-    before = results.get(name)
     if not (small_plane() and rows % 128 == 0):
+        before = results.get(name)
         stored = []
         for index, (half, begin, width, turn) in enumerate(layout):
             block = lax.all_gather(pieces[half][:, begin : begin + width], PLANE, axis=0, tiled=True)
@@ -477,7 +479,7 @@
         results[name] = stored
         return
     mine, beside = yield from spread_steps(work, pieces, token)
-    given = list(before or [])
+    given = list(results.get(name) or [])
     size = sum(math_prod(shape) for shape in shapes) // LAYERS
 
     def out_spec(half, width, turn):
@@ -512,14 +514,23 @@
     return jnp.concatenate([halves(mine, size, columns, odd), halves(beside, size, columns, odd)], 0)
 
 
-def tile_scores(query, keys, at_query, at_keys, slope):
+LOG2_E = 1.4426950408889634
+
+
+def fill_bias(at_rows, at_keys, biases):
+    for odd, bias in enumerate(biases):
+        place, start = at_rows[:, 2 * odd : 2 * odd + 1], at_rows[:, 2 * odd + 1 : 2 * odd + 2]
+        spots = at_keys[:, : bias.shape[1]]
+        bias[...] = jnp.where((spots <= place) & (spots >= start), 0.0, -1e30)
+
+
+def tile_scores(query, keys, bias, spots, slope):
     scores = lax.dot_general(query, keys, (((1,), (1,)), ((), ())), preferred_element_type=F32)
-    place, start = at_query
-    scores = scores * HD ** (-0.5) - slope * (place - at_keys)
-    return jnp.where((at_keys <= place) & (at_keys >= start), scores, -1e30)
-
-
-def attend_kernel(size, slopes, at_rows, at_keys, query, mine, beside, mixed, log_totals):
+    return (scores * (HD ** (-0.5) * LOG2_E) + spots * (slope * LOG2_E)) + bias[...]
+
+
+def attend_kernel(size, slopes, at_rows, at_keys, query, mine, beside, mixed, log_totals, *biases):
+    fill_bias(at_rows, at_keys, biases)
     heads = query.shape[1] // HD
     for head in range(heads):
         columns = slice(head * HD, (head + 1) * HD)
@@ -531,18 +542,14 @@
             value_rows = values[0] if odd == 0 else jnp.concatenate(values, 0)
             spots = at_keys[:, : key_rows.shape[0]]
             scores = tile_scores(
-                halves(query, size, columns, odd),
-                key_rows,
-                (at_rows[:, 2 * odd : 2 * odd + 1], at_rows[:, 2 * odd + 1 : 2 * odd + 2]),
-                spots,
-                slopes[head],
+                halves(query, size, columns, odd), key_rows, biases[odd], spots, slopes[head]
             )
             row_max = jnp.max(scores, axis=-1, keepdims=True)
-            weights = jnp.exp(scores - row_max)
+            weights = jnp.exp2(scores - row_max)
             totals = jnp.sum(weights, axis=-1, keepdims=True)
             probabilities = (weights * (1.0 / totals)).astype(BF16)
             result = jnp.dot(probabilities, value_rows, preferred_element_type=F32).astype(BF16)
-            logs = row_max + jnp.log(totals)
+            logs = row_max + jnp.log2(totals)
             for index in range(result.shape[0] // size):
                 rows = slice((2 * index + odd) * size, (2 * index + odd + 1) * size)
                 mixed[rows, columns] = result[index * size : (index + 1) * size]
@@ -550,8 +557,9 @@
 
 
 def attend_back_kernel(
-    size, slopes, at_rows, at_keys, query, mine, beside, log_totals, grad, to_query, to_mine, to_beside
+    size, slopes, at_rows, at_keys, query, mine, beside, log_totals, grad, to_query, to_mine, to_beside, *biases
 ):
+    fill_bias(at_rows, at_keys, biases)
     heads = query.shape[1] // HD
     scale = HD ** (-0.5)
     for head in range(heads):
@@ -567,13 +575,9 @@
             query_rows = halves(query, size, columns, odd)
             grad_rows = halves(grad, size, columns, odd)
             scores = tile_scores(
-                query_rows,
-                key_rows,
-                (at_rows[:, 2 * odd : 2 * odd + 1], at_rows[:, 2 * odd + 1 : 2 * odd + 2]),
-                at_keys[:, : key_rows.shape[0]],
-                slopes[head],
+                query_rows, key_rows, biases[odd], at_keys[:, : key_rows.shape[0]], slopes[head]
             )
-            probabilities = jnp.exp(scores - halves(log_totals, size, one, odd))
+            probabilities = jnp.exp2(scores - halves(log_totals, size, one, odd))
             grad_probs = lax.dot_general(
                 grad_rows, value_rows, (((1,), (1,)), ((), ())), preferred_element_type=F32
             )
@@ -616,6 +620,10 @@
     )
 
 
+def bias_shapes(query, keys):
+    return [pltpu.VMEM((query.shape[0] // 2, keys * (odd + 1) // 2), F32) for odd in range(2)]
+
+
 def attention_specs(count):
     return [pl.BlockSpec(memory_space=pltpu.SMEM)] + [pl.BlockSpec(memory_space=pltpu.VMEM)] * count
 
@@ -630,6 +638,7 @@
         ],
         in_specs=attention_specs(5),
         out_specs=[pl.BlockSpec(memory_space=pltpu.VMEM)] * 2,
+        scratch_shapes=bias_shapes(query, at_keys.shape[1]),
         compiler_params=pltpu.CompilerParams(vmem_limit_bytes=48 << 20),
         cost_estimate=attention_cost(query, 2),
     )(slopes, at_rows, at_keys, query, mine, beside)
@@ -646,6 +655,7 @@
         ],
         in_specs=attention_specs(7),
         out_specs=[pl.BlockSpec(memory_space=pltpu.VMEM)] * 3,
+        scratch_shapes=bias_shapes(query, at_keys.shape[1]),
         compiler_params=pltpu.CompilerParams(vmem_limit_bytes=48 << 20),
         cost_estimate=attention_cost(query, 5),
     )(slopes, at_rows, at_keys, query, mine, beside, log_totals, grad_mixed)
@@ -755,6 +765,7 @@
         ups, downs = zip((w_up[layer], w_down[layer]), used["ffn", layer])
         hidden = [dot(inputs_mid, up) + bias for up, bias in zip(ups, bias_up)]
         active = [gelu_tanh(value).astype(BF16) for value in hidden]
+        hidden = [value.astype(BF16) for value in hidden]
         stream = middle + (
             scatter_rows(lambda first, last: sum(dot(rows_of(value, first, last), down) for value, down in zip(active, downs)),
                 work, str(layer) + "e") + b_down[layer]
@@ -801,7 +812,7 @@
         grad_b_down = jnp.sum(grad_branch, axis=0, dtype=F32)
         branch_all = gather_rows(grad_branch, work, str(layer) + "f")
         grad_hidden = [
-            jax.vjp(gelu_tanh, value)[1](dot_nt(branch_all, down))[0].astype(BF16)
+            jax.vjp(gelu_tanh, value.astype(F32))[1](dot_nt(branch_all, down))[0].astype(BF16)
             for value, down in zip(hidden, downs)
         ]
         work.add(

time: 595 us -> 588 us (0.988)
  starting transfers between devices: 106 us -> 114 us
  local copies, waits for them, and re-layouts: 44.1 us -> 36.3 us
    unnamed x414 -> x394, local copies, waits for them, and re-layouts: 22.5 us -> 12.4 us
    ppermute x107 -> x109, starting transfers between devices: 92.9 us -> 103 us  [swap(): return lax.ppermute(value, axis, [(0, 1), (1, 0)])]
    convert_element_type x8 -> x16, other arithmetic: 0.79 us -> 7.42 us  [reduce_weights(): (value.astype(F32) + part.astype(F32)).astype(BF16)]
    convert_element_type x8 -> x0, other arithmetic: 6.6 us -> none  [reduce_weights(): (value + part.astype(F32)).astype(BF16)]
    ppermute x107 -> x109, waiting for transfers between devices: 245 us -> 241 us  [swap(): return lax.ppermute(value, axis, [(0, 1), (1, 0)])]
  transfers between devices with their start and end apart: 115 -> 117, of which waited for: 50 -> 54; matrix products, arithmetic and copies ran while one was open for 20% -> 21% of each run, Pallas kernels for 7% -> 8%
where the time goes in v3:
time: 588 us; the launch traced here: 584 us
  waiting for transfers between devices  241 us (41%)
  starting transfers between devices  114 us (19%)
  matrix products  80.9 us (14%)
  Pallas kernels  57.7 us (10%)
  other arithmetic  49 us (8%)
  local copies, waits for them, and re-layouts  36.3 us (6%)
    ppermute x109, waiting for transfers between devices, swap(): return lax.ppermute(value, axis, [(0, 1), (1, 0)])  241 us
    ppermute x109, starting transfers between devices, swap(): return lax.ppermute(value, axis, [(0, 1), (1, 0)])  103 us
    dot_general x22, matrix products, dot_nt(): return jnp.einsum('ti,oi->to', left, right, preferred_element_type=F32)  30.5 us
    dot_general x20, matrix products, dot(): return jnp.dot(left, right, preferred_element_type=F32)  29.6 us
    dot_general x24, matrix products, dot_tn(): return jnp.einsum('ti,to->io', left, right, preferred_element_type=F32)  20.9 us
    pallas_call x4, Pallas kernels, reduce_weights(): pl.pallas_call(functools.partial(store_kernel, layout, len(mine), len(giv...  19.5 us
    pallas_call x2, Pallas kernels, attend_back(): pl.pallas_call(functools.partial(attend_back_kernel, size), out_shape=[ja...  16.4 us
    unnamed x394, local copies, waits for them, and re-layouts  12.4 us
  transfers between devices with their start and end apart: 117, of which 54 were waited for; matrix products, arithmetic and copies ran while one was open for 21% of the time, Pallas kernels for 8%

profile of v3, /device:TPU:0, one launch (start us, length us, event | category | flops | bytes accessed | tf_op | source)
XLA Modules:
  0.0 584.1 jit_solution(4478141165775337522)
XLA Ops:
  7.7 7.0 %collective-permute-start.2 = (bf16[128,1024]{1,0:T(8,128)(2,1)S(1)}, bf16[128,1024]{1,0:T(8,128)(2,1)S(1)}, u32[]{:S(2)}, u32[]{:S(2)}) collective-permute-start(bf16[128,1024]{1,0:T(8,128)(2,1)S(1)} %maximum_maximum_fusion), channel_id=1, source_target_pairs={{0,2},{2,0},{1,3},{3,1},{4,6},{6,4},{5,7},{7,5},{8,10},{10,8},{9,1... | collective-permute-start | bytes 786440 | tf_op jit(solution)/shard_map/ppermute | solution.py:69
  24.9 5.2 collective-permute-done.2
  52.5 7.6 %shard_map.305 = (bf16[1024,512]{1,0:T(8,128)(2,1)}, bf16[1024,1024]{1,0:T(8,128)(2,1)}, bf16[2,256,1024]{2,1,0:T(8,128)(2,1)}) custom-call(s32[16]{0:T(128)} %stack.61.spots, bf16[4,128,512]{2,1,0:T(8,128)(2,1)} %copy-done.76, bf16[4,128,512]{2,1,0:T(8,128)(2,1)} %copy-done.77, bf16[4,128,512]{2,1,0:T(8,128)(2,1)} %copy-done.78, ...), custom_call_target="tpu_custom_call" | custom-call | bytes 8388608 | tf_op jit(solution)/shard_map/pallas_call | solution.py:290
  60.2 3.2 add_convert_fusion.15.mine
  71.3 5.1 shard_map.306
  76.9 5.8 collective-permute-done.14
  84.9 3.2 collective-permute-start.18
  90.9 11.1 %collective-permute-done.15 = bf16[256,1024]{1,0:T(8,128)(2,1)S(1)} collective-permute-done((bf16[256,1024]{1,0:T(8,128)(2,1)S(1)}, bf16[256,1024]{1,0:T(8,128)(2,1)S(1)}, u32[]{:S(2)}, u32[]{:S(2)}) %collective-permute-start.15) | collective-permute-done | bytes 524320 | tf_op jit(solution)/shard_map/ppermute | solution.py:69
  111.9 5.5 collective-permute-done.19
  125.1 4.1 fusion.23
  131.6 4.4 fusion.31
  140.7 4.4 collective-permute-done.27
  145.2 11.1 %collective-permute-done.26 = bf16[256,1024]{1,0:T(8,128)(2,1)S(1)} collective-permute-done((bf16[256,1024]{1,0:T(8,128)(2,1)S(1)}, bf16[256,1024]{1,0:T(8,128)(2,1)S(1)}, u32[]{:S(2)}, u32[]{:S(2)}) %collective-permute-start.26) | collective-permute-done | bytes 524320 | tf_op jit(solution)/shard_map/ppermute | solution.py:69
  161.2 7.1 %collective-permute-done.32 = bf16[1,128,1024]{2,1,0:T(8,128)(2,1)S(1)} collective-permute-done((bf16[1,128,1024]{2,1,0:T(8,128)(2,1)S(1)}, bf16[1,128,1024]{2,1,0:T(8,128)(2,1)S(1)}, u32[]{:S(2)}, u32[]{:S(2)}) %collective-permute-start.32) | collective-permute-done | bytes 262176 | tf_op jit(solution)/shard_map/ppermute | solution.py:69
  176.4 5.1 shard_map.309
  187.7 14.0 %collective-permute-done.37 = bf16[256,1024]{1,0:T(8,128)(2,1)S(1)} collective-permute-done((bf16[256,1024]{1,0:T(8,128)(2,1)S(1)}, bf16[256,1024]{1,0:T(8,128)(2,1)S(1)}, u32[]{:S(2)}, u32[]{:S(2)}) %collective-permute-start.37) | collective-permute-done | bytes 524320 | tf_op jit(solution)/shard_map/ppermute | solution.py:69
  204.9 11.2 %collective-permute-done.42 = bf16[256,1024]{1,0:T(8,128)(2,1)S(1)} collective-permute-done((bf16[256,1024]{1,0:T(8,128)(2,1)S(1)}, bf16[256,1024]{1,0:T(8,128)(2,1)S(1)}, u32[]{:S(2)}, u32[]{:S(2)}) %collective-permute-start.42) | collective-permute-done | bytes 524320 | tf_op jit(solution)/shard_map/ppermute | solution.py:69
  228.9 10.6 %collective-permute-done.45 = bf16[256,1024]{1,0:T(8,128)(2,1)S(1)} collective-permute-done((bf16[256,1024]{1,0:T(8,128)(2,1)S(1)}, bf16[256,1024]{1,0:T(8,128)(2,1)S(1)}, u32[]{:S(2)}, u32[]{:S(2)}) %collective-permute-start.45) | collective-permute-done | bytes 524320 | tf_op jit(solution)/shard_map/ppermute | solution.py:69
  241.2 3.6 collective-permute-start.46
  246.2 6.6 %collective-permute-done.48 = bf16[256,1024]{1,0:T(8,128)(2,1)} collective-permute-done((bf16[256,1024]{1,0:T(8,128)(2,1)}, bf16[256,1024]{1,0:T(8,128)(2,1)}, u32[]{:S(2)}, u32[]{:S(2)}) %collective-permute-start.48) | collective-permute-done | bytes 524320 | tf_op jit(solution)/shard_map/ppermute | solution.py:69
  254.1 5.5 convert_reduce_fusion.1
  262.2 4.4 convert_reduce_fusion
  270.9 4.2 collective-permute-start.50
  288.2 8.6 %collective-permute-done.49 = bf16[256,1024]{1,0:T(8,128)(2,1)S(1)} collective-permute-done((bf16[256,1024]{1,0:T(8,128)(2,1)S(1)}, bf16[256,1024]{1,0:T(8,128)(2,1)S(1)}, u32[]{:S(2)}, u32[]{:S(2)}) %collective-permute-start.49) | collective-permute-done | bytes 524320 | tf_op jit(solution)/shard_map/ppermute | solution.py:69
  310.1 3.3 collective-permute-done.52
  314.3 8.2 %shard_map.311 = (bf16[512,512]{1,0:T(8,128)(2,1)S(1)}, f32[512,1024]{1,0:T(8,128)}, bf16[512,1024]{1,0:T(8,128)(2,1)S(1)}) custom-call(f32[4]{0:T(128)S(1)} %fusion.230.slopes, f32[256,4]{1,0:T(8,128)S(1)} %convert_element_type.597.at_rows, f32[1,1024]{1,0:T(1,128)S(1)} %convert_element_type.598.at_keys, bf16[512,512]{1,0:T(8,128)(2,1)S(1)} %copy-done.31, ...), custom_call_target="tpu_custom_call" | custom-call | flops 2013265920 | bytes 4194304 | tf_op jit(solution)/shard_map/pallas_call | solution.py:649
  322.9 6.8 %collective-permute-done.53 = bf16[256,2048]{1,0:T(8,128)(2,1)S(1)} collective-permute-done((bf16[256,2048]{1,0:T(8,128)(2,1)}, bf16[256,2048]{1,0:T(8,128)(2,1)S(1)}, u32[]{:S(2)}, u32[]{:S(2)}) %collective-permute-start.53) | collective-permute-done | bytes 1048608 | tf_op jit(solution)/shard_map/ppermute | solution.py:69
  329.7 3.2 collective-permute-done.54
  350.9 5.3 collective-permute-done.56
  364.3 14.8 %collective-permute-done.61 = bf16[256,1024]{1,0:T(8,128)(2,1)S(1)} collective-permute-done((bf16[256,1024]{1,0:T(8,128)(2,1)S(1)}, bf16[256,1024]{1,0:T(8,128)(2,1)S(1)}, u32[]{:S(2)}, u32[]{:S(2)}) %collective-permute-start.61) | collective-permute-done | bytes 524320 | tf_op jit(solution)/shard_map/ppermute | solution.py:69
  396.9 3.5 collective-permute-done.67
  408.8 9.2 %collective-permute-done.70 = bf16[128,1024]{1,0:T(8,128)(2,1)S(1)} collective-permute-done((bf16[128,1024]{1,0:T(8,128)(2,1)S(1)}, bf16[128,1024]{1,0:T(8,128)(2,1)S(1)}, u32[]{:S(2)}, u32[]{:S(2)}) %collective-permute-start.70) | collective-permute-done | bytes 262176 | tf_op jit(solution)/shard_map/ppermute | solution.py:69
  425.6 7.0 %collective-permute-done.73 = bf16[256,1024]{1,0:T(8,128)(2,1)S(1)} collective-permute-done((bf16[256,1024]{1,0:T(8,128)(2,1)S(1)}, bf16[256,1024]{1,0:T(8,128)(2,1)S(1)}, u32[]{:S(2)}, u32[]{:S(2)}) %collective-permute-start.73) | collective-permute-done | bytes 524320 | tf_op jit(solution)/shard_map/ppermute | solution.py:69
  437.0 8.2 %shard_map.312 = (bf16[512,512]{1,0:T(8,128)(2,1)S(1)}, f32[512,1024]{1,0:T(8,128)}, bf16[512,1024]{1,0:T(8,128)(2,1)S(1)}) custom-call(f32[4]{0:T(128)S(1)} %fusion.230.slopes, f32[256,4]{1,0:T(8,128)S(1)} %convert_element_type.597.at_rows, f32[1,1024]{1,0:T(1,128)S(1)} %convert_element_type.598.at_keys, bf16[512,512]{1,0:T(8,128)(2,1)S(1)} %copy-done.29, ...), custom_call_target="tpu_custom_call" | custom-call | flops 2013265920 | bytes 4194304 | tf_op jit(solution)/shard_map/pallas_call | solution.py:649
  453.5 4.1 collective-permute-done.77
  471.6 5.5 shard_map.313
  478.0 6.2 %collective-permute-done.88 = bf16[128,2048]{1,0:T(8,128)(2,1)S(1)} collective-permute-done((bf16[128,2048]{1,0:T(8,128)(2,1)S(1)}, bf16[128,2048]{1,0:T(8,128)(2,1)S(1)}, u32[]{:S(2)}, u32[]{:S(2)}) %collective-permute-start.88) | collective-permute-done | bytes 524320 | tf_op jit(solution)/shard_map/ppermute | solution.py:69
  495.7 9.3 %collective-permute-done.93 = bf16[256,1024]{1,0:T(8,128)(2,1)S(1)} collective-permute-done((bf16[256,1024]{1,0:T(8,128)(2,1)S(1)}, bf16[256,1024]{1,0:T(8,128)(2,1)S(1)}, u32[]{:S(2)}, u32[]{:S(2)}) %collective-permute-start.93) | collective-permute-done | bytes 524320 | tf_op jit(solution)/shard_map/ppermute | solution.py:69
  505.3 9.2 %collective-permute-done.96 = bf16[128,2048]{1,0:T(8,128)(2,1)S(1)} collective-permute-done((bf16[128,2048]{1,0:T(8,128)(2,1)S(1)}, bf16[128,2048]{1,0:T(8,128)(2,1)S(1)}, u32[]{:S(2)}, u32[]{:S(2)}) %collective-permute-start.96) | collective-permute-done | bytes 524320 | tf_op jit(solution)/shard_map/ppermute | solution.py:69
  519.8 4.2 collective-permute-done.97
  524.3 4.4 collective-permute-done.99
  534.8 3.0 collective-permute-start.87
  537.8 4.4 shard_map.314
  542.2 4.2 collective-permute-done.104
  556.4 3.5 collective-permute-done.107
  567.5 3.5 collective-permute-done.110
  571.2 5.3 shard_map.315
  579.6 4.4 shard_map.316
  (878 shorter events, 279.8 us)
Async XLA Ops:
  1.8 22.9 %collective-permute-start.1 = (bf16[128,1024]{1,0:T(8,128)(2,1)S(1)}, bf16[128,1024]{1,0:T(8,128)(2,1)S(1)}, u32[]{:S(2)}, u32[]{:S(2)}) collective-permute-start(bf16[128,1024]{1,0:T(8,128)(2,1)S(1)} %get-tuple-element.551), channel_id=1, source_target_pairs={{0,4},{2,0},{4,6},{6,2},{1,5},{3,1},{5,7},{7,3},{8,12},{10,8},{12,... | collective-permute-start | bytes 786440 | tf_op jit(solution)/shard_map/ppermute | solution.py:112
  2.3 22.4 %collective-permute-start = (bf16[128,1024]{1,0:T(8,128)(2,1)S(1)}, bf16[128,1024]{1,0:T(8,128)(2,1)S(1)}, u32[]{:S(2)}, u32[]{:S(2)}) collective-permute-start(bf16[128,1024]{1,0:T(8,128)(2,1)S(1)} %get-tuple-element.550), channel_id=1, source_target_pairs={{0,0},{2,4},{4,2},{6,6},{1,1},{3,5},{5,3},{7,7},{8,8},{10,12},{12,... | collective-permute-start | bytes 786440 | tf_op jit(solution)/shard_map/ppermute | solution.py:111
  7.7 22.4 %collective-permute-start.2 = (bf16[128,1024]{1,0:T(8,128)(2,1)S(1)}, bf16[128,1024]{1,0:T(8,128)(2,1)S(1)}, u32[]{:S(2)}, u32[]{:S(2)}) collective-permute-start(bf16[128,1024]{1,0:T(8,128)(2,1)S(1)} %maximum_maximum_fusion), channel_id=1, source_target_pairs={{0,2},{2,0},{1,3},{3,1},{4,6},{6,4},{5,7},{7,5},{8,10},{10,8},{9,1... | collective-permute-start | bytes 786440 | tf_op jit(solution)/shard_map/ppermute | solution.py:69
  14.6 50.8 %collective-permute-start.3 = (s32[4]{0:T(128)}, s32[4]{0:T(128)}, u32[]{:S(2)}, u32[]{:S(2)}) collective-permute-start(s32[4]{0:T(128)} %bitcast.5), channel_id=1, source_target_pairs={{0,4},{4,0},{1,5},{5,1},{2,6},{6,2},{3,7},{7,3},{8,12},{12,8},{9,1... | collective-permute-start | bytes 56 | tf_op jit(solution)/shard_map/ppermute | solution.py:69
  15.2 33.0 %collective-permute-start.11 = (f32[2,512]{1,0:T(2,128)}, f32[2,512]{1,0:T(2,128)}, u32[]{:S(2)}, u32[]{:S(2)}) collective-permute-start(f32[2,512]{1,0:T(2,128)} %pad_maximum_fusion.50), channel_id=1, source_target_pairs={{0,2},{2,0},{1,3},{3,1},{4,6},{6,4},{5,7},{7,5},{8,10},{10,8},{9,1... | collective-permute-start | bytes 12296 | tf_op jit(solution)/shard_map/ppermute | solution.py:69
  34.4 16.5 %collective-permute-start.4 = (bf16[256,1024]{1,0:T(8,128)(2,1)S(1)}, bf16[256,1024]{1,0:T(8,128)(2,1)S(1)}, u32[]{:S(2)}, u32[]{:S(2)}) collective-permute-start(bf16[256,1024]{1,0:T(8,128)(2,1)S(1)} %add_convert_fusion.40), channel_id=1, source_target_pairs={{0,1},{1,0},{2,3},{3,2},{4,5},{5,4},{6,7},{7,6},{8,9},{9,8},{10,11... | collective-permute-start | bytes 1572872 | tf_op jit(solution)/shard_map/ppermute | solution.py:69
  67.3 15.4 %collective-permute-start.14 = (bf16[128,1024]{1,0:T(8,128)(2,1)}, bf16[128,1024]{1,0:T(8,128)(2,1)S(1)}, u32[]{:S(2)}, u32[]{:S(2)}) collective-permute-start(bf16[128,1024]{1,0:T(8,128)(2,1)} %get-tuple-element.272), channel_id=1, source_target_pairs={{0,2},{2,0},{1,3},{3,1},{4,6},{6,4},{5,7},{7,5},{8,10},{10,8},{9,1... | collective-permute-start | bytes 786440 | tf_op jit(solution)/shard_map/ppermute | solution.py:69
  82.7 19.3 %collective-permute-start.15 = (bf16[256,1024]{1,0:T(8,128)(2,1)S(1)}, bf16[256,1024]{1,0:T(8,128)(2,1)S(1)}, u32[]{:S(2)}, u32[]{:S(2)}) collective-permute-start(bf16[256,1024]{1,0:T(8,128)(2,1)S(1)} %convolution_convert_fusion.25), channel_id=1, source_target_pairs={{0,1},{1,0},{2,3},{3,2},{4,5},{5,4},{6,7},{7,6},{8,9},{9,8},{10,11... | collective-permute-start | bytes 1572872 | tf_op jit(solution)/shard_map/ppermute | solution.py:69
  84.2 17.8 %collective-permute-start.17 = (bf16[1,128,1024]{2,1,0:T(8,128)(2,1)S(1)}, bf16[1,128,1024]{2,1,0:T(8,128)(2,1)S(1)}, u32[]{:S(2)}, u32[]{:S(2)}) collective-permute-start(bf16[1,128,1024]{2,1,0:T(8,128)(2,1)S(1)} %bitcast.219), channel_id=1, source_target_pairs={{0,16},{16,0},{1,17},{17,1},{2,18},{18,2},{3,19},{19,3},{4,20},{20... | collective-permute-start | bytes 786440 | tf_op jit(solution)/shard_map/ppermute | solution.py:69
  84.9 17.1 %collective-permute-start.18 = (bf16[128,1024]{1,0:T(8,128)(2,1)S(1)}, bf16[128,1024]{1,0:T(8,128)(2,1)S(1)}, u32[]{:S(2)}, u32[]{:S(2)}) collective-permute-start(bf16[128,1024]{1,0:T(8,128)(2,1)S(1)} %maximum_maximum_fusion.1), channel_id=1, source_target_pairs={{0,2},{2,0},{1,3},{3,1},{4,6},{6,4},{5,7},{7,5},{8,10},{10,8},{9,1... | collective-permute-start | bytes 786440 | tf_op jit(solution)/shard_map/ppermute | solution.py:69
  117.5 38.8 %collective-permute-start.30 = (bf16[128,1024]{1,0:T(8,128)(2,1)S(1)}, bf16[128,1024]{1,0:T(8,128)(2,1)S(1)}, u32[]{:S(2)}, u32[]{:S(2)}) collective-permute-start(bf16[128,1024]{1,0:T(8,128)(2,1)S(1)} %copy-done.91), channel_id=1, source_target_pairs={{0,2},{2,0},{1,3},{3,1},{4,6},{6,4},{5,7},{7,5},{8,10},{10,8},{9,1... | collective-permute-start | bytes 786440 | tf_op jit(solution)/shard_map/ppermute | solution.py:69
  136.7 19.5 %collective-permute-start.26 = (bf16[256,1024]{1,0:T(8,128)(2,1)S(1)}, bf16[256,1024]{1,0:T(8,128)(2,1)S(1)}, u32[]{:S(2)}, u32[]{:S(2)}) collective-permute-start(bf16[256,1024]{1,0:T(8,128)(2,1)S(1)} %fusion.125), channel_id=1, source_target_pairs={{0,1},{1,0},{2,3},{3,2},{4,5},{5,4},{6,7},{7,6},{8,9},{9,8},{10,11... | collective-permute-start | bytes 1572872 | tf_op jit(solution)/shard_map/ppermute | solution.py:69
  137.6 18.7 %collective-permute-start.28 = (bf16[2,128,512]{2,1,0:T(8,128)(2,1)S(1)}, bf16[2,128,512]{2,1,0:T(8,128)(2,1)S(1)}, u32[]{:S(2)}, u32[]{:S(2)}) collective-permute-start(bf16[2,128,512]{2,1,0:T(8,128)(2,1)S(1)} %pad_maximum_fusion.41), channel_id=1, source_target_pairs={{0,8},{8,0},{1,9},{9,1},{2,10},{10,2},{3,11},{11,3},{4,12},{12,4},... | collective-permute-start | bytes 786440 | tf_op jit(solution)/shard_map/ppermute | solution.py:69
  138.5 17.8 %collective-permute-start.29 = (bf16[128,1024]{1,0:T(8,128)(2,1)S(1)}, bf16[128,1024]{1,0:T(8,128)(2,1)S(1)}, u32[]{:S(2)}, u32[]{:S(2)}) collective-permute-start(bf16[128,1024]{1,0:T(8,128)(2,1)S(1)} %copy-done.92), channel_id=1, source_target_pairs={{0,2},{2,0},{1,3},{3,1},{4,6},{6,4},{5,7},{7,5},{8,10},{10,8},{9,1... | collective-permute-start | bytes 786440 | tf_op jit(solution)/shard_map/ppermute | solution.py:69
  182.1 19.6 %collective-permute-start.37 = (bf16[256,1024]{1,0:T(8,128)(2,1)S(1)}, bf16[256,1024]{1,0:T(8,128)(2,1)S(1)}, u32[]{:S(2)}, u32[]{:S(2)}) collective-permute-start(bf16[256,1024]{1,0:T(8,128)(2,1)S(1)} %convolution_convert_fusion.24), channel_id=1, source_target_pairs={{0,1},{1,0},{2,3},{3,2},{4,5},{5,4},{6,7},{7,6},{8,9},{9,8},{10,11... | collective-permute-start | bytes 1572872 | tf_op jit(solution)/shard_map/ppermute | solution.py:69
  183.6 18.1 %collective-permute-start.38 = (bf16[2,128,1024]{2,1,0:T(8,128)(2,1)S(1)}, bf16[2,128,1024]{2,1,0:T(8,128)(2,1)S(1)}, u32[]{:S(2)}, u32[]{:S(2)}) collective-permute-start(bf16[2,128,1024]{2,1,0:T(8,128)(2,1)S(1)} %pad_maximum_fusion.30), channel_id=1, source_target_pairs={{0,16},{16,0},{1,17},{17,1},{2,18},{18,2},{3,19},{19,3},{4,20},{20... | collective-permute-start | bytes 1572872 | tf_op jit(solution)/shard_map/ppermute | solution.py:69
  184.1 17.6 %collective-permute-start.39 = (bf16[2,128,1024]{2,1,0:T(8,128)(2,1)S(1)}, bf16[2,128,1024]{2,1,0:T(8,128)(2,1)S(1)}, u32[]{:S(2)}, u32[]{:S(2)}) collective-permute-start(bf16[2,128,1024]{2,1,0:T(8,128)(2,1)S(1)} %pad_maximum_fusion.31), channel_id=1, source_target_pairs={{0,8},{8,0},{1,9},{9,1},{2,10},{10,2},{3,11},{11,3},{4,12},{12,4},... | collective-permute-start | bytes 1572872 | tf_op jit(solution)/shard_map/ppermute | solution.py:69
  185.0 16.7 %collective-permute-start.40 = (bf16[128,1024]{1,0:T(8,128)(2,1)S(1)}, bf16[128,1024]{1,0:T(8,128)(2,1)S(1)}, u32[]{:S(2)}, u32[]{:S(2)}) collective-permute-start(bf16[128,1024]{1,0:T(8,128)(2,1)S(1)} %get-tuple-element.549), channel_id=1, source_target_pairs={{0,0},{2,4},{4,2},{6,6},{1,1},{3,5},{5,3},{7,7},{8,8},{10,12},{12,... | collective-permute-start | bytes 786440 | tf_op jit(solution)/shard_map/ppermute | solution.py:111
  185.6 16.1 %collective-permute-start.41 = (bf16[128,1024]{1,0:T(8,128)(2,1)S(1)}, bf16[128,1024]{1,0:T(8,128)(2,1)S(1)}, u32[]{:S(2)}, u32[]{:S(2)}) collective-permute-start(bf16[128,1024]{1,0:T(8,128)(2,1)S(1)} %get-tuple-element.548), channel_id=1, source_target_pairs={{0,4},{2,0},{4,6},{6,2},{1,5},{3,1},{5,7},{7,3},{8,12},{10,8},{12,... | collective-permute-start | bytes 786440 | tf_op jit(solution)/shard_map/ppermute | solution.py:112
  204.2 15.6 %collective-permute-start.43 = (bf16[4,128,1024]{2,1,0:T(8,128)(2,1)S(1)}, bf16[4,128,1024]{2,1,0:T(8,128)(2,1)S(1)}, u32[]{:S(2)}, u32[]{:S(2)}) collective-permute-start(bf16[4,128,1024]{2,1,0:T(8,128)(2,1)S(1)} %constant_dynamic-update-slice_fusion.22.up), channel_id=1, source_target_pairs={{0,4},{4,0},{1,5},{5,1},{2,6},{6,2},{3,7},{7,3},{8,12},{12,8},{9,1... | collective-permute-start | bytes 3145736 | tf_op jit(solution)/shard_map/ppermute | solution.py:69
  204.4 15.4 %collective-permute-start.44 = (bf16[4,128,1024]{2,1,0:T(8,128)(2,1)S(1)}, bf16[4,128,1024]{2,1,0:T(8,128)(2,1)S(1)}, u32[]{:S(2)}, u32[]{:S(2)}) collective-permute-start(bf16[4,128,1024]{2,1,0:T(8,128)(2,1)S(1)} %constant_dynamic-update-slice_fusion.24.down), channel_id=1, source_target_pairs={{0,4},{4,0},{1,5},{5,1},{2,6},{6,2},{3,7},{7,3},{8,12},{12,8},{9,1... | collective-permute-start | bytes 3145736 | tf_op jit(solution)/shard_map/ppermute | solution.py:69
  224.6 14.9 %collective-permute-start.45 = (bf16[256,1024]{1,0:T(8,128)(2,1)S(1)}, bf16[256,1024]{1,0:T(8,128)(2,1)S(1)}, u32[]{:S(2)}, u32[]{:S(2)}) collective-permute-start(bf16[256,1024]{1,0:T(8,128)(2,1)S(1)} %fusion.126), channel_id=1, source_target_pairs={{0,1},{1,0},{2,3},{3,2},{4,5},{5,4},{6,7},{7,6},{8,9},{9,8},{10,11... | collective-permute-start | bytes 1572872 | tf_op jit(solution)/shard_map/ppermute | solution.py:69
  226.5 26.3 %collective-permute-start.48 = (bf16[256,1024]{1,0:T(8,128)(2,1)}, bf16[256,1024]{1,0:T(8,128)(2,1)}, u32[]{:S(2)}, u32[]{:S(2)}) collective-permute-start(bf16[256,1024]{1,0:T(8,128)(2,1)} %get-tuple-element.524), channel_id=1, source_target_pairs={{0,1},{1,0},{2,3},{3,2},{4,5},{5,4},{6,7},{7,6},{8,9},{9,8},{10,11... | collective-permute-start | bytes 1572872 | tf_op jit(solution)/shard_map/ppermute | solution.py:69
  270.9 25.9 %collective-permute-start.50 = (bf16[512,2048]{1,0:T(8,128)(2,1)}, bf16[512,2048]{1,0:T(8,128)(2,1)}, u32[]{:S(2)}, u32[]{:S(2)}) collective-permute-start(bf16[512,2048]{1,0:T(8,128)(2,1)} %convolution_convert_fusion.5), channel_id=1, source_target_pairs={{0,4},{4,0},{1,5},{5,1},{2,6},{6,2},{3,7},{7,3},{8,12},{12,8},{9,1... | collective-permute-start | bytes 6291464 | tf_op jit(solution)/shard_map/ppermute | solution.py:69
  277.7 19.1 %collective-permute-start.51 = (bf16[512,2048]{1,0:T(8,128)(2,1)}, bf16[512,2048]{1,0:T(8,128)(2,1)}, u32[]{:S(2)}, u32[]{:S(2)}) collective-permute-start(bf16[512,2048]{1,0:T(8,128)(2,1)} %convolution_convert_fusion.4), channel_id=1, source_target_pairs={{0,4},{4,0},{1,5},{5,1},{2,6},{6,2},{3,7},{7,3},{8,12},{12,8},{9,1... | collective-permute-start | bytes 6291464 | tf_op jit(solution)/shard_map/ppermute | solution.py:69
  305.5 24.2 %collective-permute-start.53 = (bf16[256,2048]{1,0:T(8,128)(2,1)}, bf16[256,2048]{1,0:T(8,128)(2,1)S(1)}, u32[]{:S(2)}, u32[]{:S(2)}) collective-permute-start(bf16[256,2048]{1,0:T(8,128)(2,1)} %add_convert_fusion.13), channel_id=1, source_target_pairs={{0,8},{8,0},{1,9},{9,1},{2,10},{10,2},{3,11},{11,3},{4,12},{12,4},... | collective-permute-start | bytes 3145736 | tf_op jit(solution)/shard_map/ppermute | solution.py:69
  308.5 24.3 %collective-permute-start.54 = (bf16[256,2048]{1,0:T(8,128)(2,1)}, bf16[256,2048]{1,0:T(8,128)(2,1)S(1)}, u32[]{:S(2)}, u32[]{:S(2)}) collective-permute-start(bf16[256,2048]{1,0:T(8,128)(2,1)} %add_convert_fusion.12), channel_id=1, source_target_pairs={{0,16},{16,0},{1,17},{17,1},{2,18},{18,2},{3,19},{19,3},{4,20},{20... | collective-permute-start | bytes 3145736 | tf_op jit(solution)/shard_map/ppermute | solution.py:69
  335.1 15.8 %collective-permute-start.57 = (bf16[128,2048]{1,0:T(8,128)(2,1)S(1)}, bf16[128,2048]{1,0:T(8,128)(2,1)S(1)}, u32[]{:S(2)}, u32[]{:S(2)}) collective-permute-start(bf16[128,2048]{1,0:T(8,128)(2,1)S(1)} %constant_dynamic-slice_fusion.10), channel_id=1, source_target_pairs={{0,16},{16,0},{1,17},{17,1},{2,18},{18,2},{3,19},{19,3},{4,20},{20... | collective-permute-start | bytes 1572872 | tf_op jit(solution)/shard_map/ppermute | solution.py:69
  339.0 17.2 %collective-permute-start.58 = (bf16[128,2048]{1,0:T(8,128)(2,1)S(1)}, bf16[128,2048]{1,0:T(8,128)(2,1)S(1)}, u32[]{:S(2)}, u32[]{:S(2)}) collective-permute-start(bf16[128,2048]{1,0:T(8,128)(2,1)S(1)} %constant_dynamic-slice_fusion.9), channel_id=1, source_target_pairs={{0,8},{8,0},{1,9},{9,1},{2,10},{10,2},{3,11},{11,3},{4,12},{12,4},... | collective-permute-start | bytes 1572872 | tf_op jit(solution)/shard_map/ppermute | solution.py:69
  357.6 21.5 %collective-permute-start.61 = (bf16[256,1024]{1,0:T(8,128)(2,1)S(1)}, bf16[256,1024]{1,0:T(8,128)(2,1)S(1)}, u32[]{:S(2)}, u32[]{:S(2)}) collective-permute-start(bf16[256,1024]{1,0:T(8,128)(2,1)S(1)} %get-tuple-element.518), channel_id=1, source_target_pairs={{0,1},{1,0},{2,3},{3,2},{4,5},{5,4},{6,7},{7,6},{8,9},{9,8},{10,11... | collective-permute-start | bytes 1572872 | tf_op jit(solution)/shard_map/ppermute | solution.py:69
  359.5 19.6 %collective-permute-start.62 = (bf16[256,1024]{1,0:T(8,128)(2,1)S(1)}, bf16[256,1024]{1,0:T(8,128)(2,1)S(1)}, u32[]{:S(2)}, u32[]{:S(2)}) collective-permute-start(bf16[256,1024]{1,0:T(8,128)(2,1)S(1)} %add_convert_fusion.36), channel_id=1, source_target_pairs={{0,8},{8,0},{1,9},{9,1},{2,10},{10,2},{3,11},{11,3},{4,12},{12,4},... | collective-permute-start | bytes 1572872 | tf_op jit(solution)/shard_map/ppermute | solution.py:69
  361.5 17.6 %collective-permute-start.63 = (bf16[256,1024]{1,0:T(8,128)(2,1)S(1)}, bf16[256,1024]{1,0:T(8,128)(2,1)S(1)}, u32[]{:S(2)}, u32[]{:S(2)}) collective-permute-start(bf16[256,1024]{1,0:T(8,128)(2,1)S(1)} %add_convert_fusion.35), channel_id=1, source_target_pairs={{0,16},{16,0},{1,17},{17,1},{2,18},{18,2},{3,19},{19,3},{4,20},{20... | collective-permute-start | bytes 1572872 | tf_op jit(solution)/shard_map/ppermute | solution.py:69
  362.4 29.6 %collective-permute-start.65 = (bf16[128,2048]{1,0:T(8,128)(2,1)S(1)}, bf16[128,2048]{1,0:T(8,128)(2,1)S(1)}, u32[]{:S(2)}, u32[]{:S(2)}) collective-permute-start(bf16[128,2048]{1,0:T(8,128)(2,1)S(1)} %pad_maximum_fusion.32), channel_id=1, source_target_pairs={{0,2},{2,0},{1,3},{3,1},{4,6},{6,4},{5,7},{7,5},{8,10},{10,8},{9,1... | collective-permute-start | bytes 1572872 | tf_op jit(solution)/shard_map/ppermute | solution.py:69
  386.7 17.8 %collective-permute-start.64 = (bf16[256,1024]{1,0:T(8,128)(2,1)S(1)}, bf16[256,1024]{1,0:T(8,128)(2,1)S(1)}, u32[]{:S(2)}, u32[]{:S(2)}) collective-permute-start(bf16[256,1024]{1,0:T(8,128)(2,1)S(1)} %fusion.128), channel_id=1, source_target_pairs={{0,1},{1,0},{2,3},{3,2},{4,5},{5,4},{6,7},{7,6},{8,9},{9,8},{10,11... | collective-permute-start | bytes 1572872 | tf_op jit(solution)/shard_map/ppermute | solution.py:69
  389.5 28.4 %collective-permute-start.71 = (bf16[512,2048]{1,0:T(8,128)(2,1)S(1)}, bf16[512,2048]{1,0:T(8,128)(2,1)S(1)}, u32[]{:S(2)}, u32[]{:S(2)}) collective-permute-start(bf16[512,2048]{1,0:T(8,128)(2,1)S(1)} %convolution_convert_fusion.1), channel_id=1, source_target_pairs={{0,4},{4,0},{1,5},{5,1},{2,6},{6,2},{3,7},{7,3},{8,12},{12,8},{9,1... | collective-permute-start | bytes 6291464 | tf_op jit(solution)/shard_map/ppermute | solution.py:69
  391.0 27.0 %collective-permute-start.72 = (bf16[512,2048]{1,0:T(8,128)(2,1)S(1)}, bf16[512,2048]{1,0:T(8,128)(2,1)S(1)}, u32[]{:S(2)}, u32[]{:S(2)}) collective-permute-start(bf16[512,2048]{1,0:T(8,128)(2,1)S(1)} %convolution_convert_fusion), channel_id=1, source_target_pairs={{0,4},{4,0},{1,5},{5,1},{2,6},{6,2},{3,7},{7,3},{8,12},{12,8},{9,1... | collective-permute-start | bytes 6291464 | tf_op jit(solution)/shard_map/ppermute | solution.py:69
  420.4 14.9 %collective-permute-start.74 = (bf16[2,128,1024]{2,1,0:T(8,128)(2,1)S(1)}, bf16[2,128,1024]{2,1,0:T(8,128)(2,1)S(1)}, u32[]{:S(2)}, u32[]{:S(2)}) collective-permute-start(bf16[2,128,1024]{2,1,0:T(8,128)(2,1)S(1)} %pad_maximum_fusion.33), channel_id=1, source_target_pairs={{0,16},{16,0},{1,17},{17,1},{2,18},{18,2},{3,19},{19,3},{4,20},{20... | collective-permute-start | bytes 1572872 | tf_op jit(solution)/shard_map/ppermute | solution.py:69
  421.2 14.9 %collective-permute-start.75 = (bf16[2,128,1024]{2,1,0:T(8,128)(2,1)S(1)}, bf16[2,128,1024]{2,1,0:T(8,128)(2,1)S(1)}, u32[]{:S(2)}, u32[]{:S(2)}) collective-permute-start(bf16[2,128,1024]{2,1,0:T(8,128)(2,1)S(1)} %pad_maximum_fusion.34), channel_id=1, source_target_pairs={{0,8},{8,0},{1,9},{9,1},{2,10},{10,2},{3,11},{11,3},{4,12},{12,4},... | collective-permute-start | bytes 1572872 | tf_op jit(solution)/shard_map/ppermute | solution.py:69
  422.4 35.1 %collective-permute-start.77 = (bf16[256,2048]{1,0:T(8,128)(2,1)S(1)}, bf16[256,2048]{1,0:T(8,128)(2,1)S(1)}, u32[]{:S(2)}, u32[]{:S(2)}) collective-permute-start(bf16[256,2048]{1,0:T(8,128)(2,1)S(1)} %add_convert_fusion.5), channel_id=1, source_target_pairs={{0,8},{8,0},{1,9},{9,1},{2,10},{10,2},{3,11},{11,3},{4,12},{12,4},... | collective-permute-start | bytes 3145736 | tf_op jit(solution)/shard_map/ppermute | solution.py:69
  424.2 33.3 %collective-permute-start.78 = (bf16[256,2048]{1,0:T(8,128)(2,1)S(1)}, bf16[256,2048]{1,0:T(8,128)(2,1)S(1)}, u32[]{:S(2)}, u32[]{:S(2)}) collective-permute-start(bf16[256,2048]{1,0:T(8,128)(2,1)S(1)} %add_convert_fusion.4), channel_id=1, source_target_pairs={{0,16},{16,0},{1,17},{17,1},{2,18},{18,2},{3,19},{19,3},{4,20},{20... | collective-permute-start | bytes 3145736 | tf_op jit(solution)/shard_map/ppermute | solution.py:69
  458.9 18.1 %collective-permute-start.81 = (bf16[256,1024]{1,0:T(8,128)(2,1)S(1)}, bf16[256,1024]{1,0:T(8,128)(2,1)S(1)}, u32[]{:S(2)}, u32[]{:S(2)}) collective-permute-start(bf16[256,1024]{1,0:T(8,128)(2,1)S(1)} %fusion.124), channel_id=1, source_target_pairs={{0,1},{1,0},{2,3},{3,2},{4,5},{5,4},{6,7},{7,6},{8,9},{9,8},{10,11... | collective-permute-start | bytes 1572872 | tf_op jit(solution)/shard_map/ppermute | solution.py:69
  487.0 18.0 %collective-permute-start.93 = (bf16[256,1024]{1,0:T(8,128)(2,1)S(1)}, bf16[256,1024]{1,0:T(8,128)(2,1)S(1)}, u32[]{:S(2)}, u32[]{:S(2)}) collective-permute-start(bf16[256,1024]{1,0:T(8,128)(2,1)S(1)} %add_convert_fusion.26), channel_id=1, source_target_pairs={{0,8},{8,0},{1,9},{9,1},{2,10},{10,2},{3,11},{11,3},{4,12},{12,4},... | collective-permute-start | bytes 1572872 | tf_op jit(solution)/shard_map/ppermute | solution.py:69
  489.0 16.0 %collective-permute-start.94 = (bf16[256,1024]{1,0:T(8,128)(2,1)S(1)}, bf16[256,1024]{1,0:T(8,128)(2,1)S(1)}, u32[]{:S(2)}, u32[]{:S(2)}) collective-permute-start(bf16[256,1024]{1,0:T(8,128)(2,1)S(1)} %add_convert_fusion.25), channel_id=1, source_target_pairs={{0,16},{16,0},{1,17},{17,1},{2,18},{18,2},{3,19},{19,3},{4,20},{20... | collective-permute-start | bytes 1572872 | tf_op jit(solution)/shard_map/ppermute | solution.py:69
  490.2 24.3 %collective-permute-start.96 = (bf16[128,2048]{1,0:T(8,128)(2,1)S(1)}, bf16[128,2048]{1,0:T(8,128)(2,1)S(1)}, u32[]{:S(2)}, u32[]{:S(2)}) collective-permute-start(bf16[128,2048]{1,0:T(8,128)(2,1)S(1)} %pad_maximum_fusion.35), channel_id=1, source_target_pairs={{0,2},{2,0},{1,3},{3,1},{4,6},{6,4},{5,7},{7,5},{8,10},{10,8},{9,1... | collective-permute-start | bytes 1572872 | tf_op jit(solution)/shard_map/ppermute | solution.py:69
  533.1 16.4 %collective-permute-start.106 = (bf16[128,1024]{1,0:T(8,128)(2,1)S(1)}, bf16[128,1024]{1,0:T(8,128)(2,1)S(1)}, u32[]{:S(2)}, u32[]{:S(2)}) collective-permute-start(bf16[128,1024]{1,0:T(8,128)(2,1)S(1)} %pad_maximum_fusion.45), channel_id=1, source_target_pairs={{0,2},{2,0},{1,3},{3,1},{4,6},{6,4},{5,7},{7,5},{8,10},{10,8},{9,1... | collective-permute-start | bytes 786440 | tf_op jit(solution)/shard_map/ppermute | solution.py:69
  533.6 15.9 %collective-permute-start.101 = (f32[2,96,128]{2,1,0:T(8,128)S(1)}, f32[2,96,128]{2,1,0:T(8,128)S(1)}, u32[]{:S(2)}, u32[]{:S(2)}) collective-permute-start(f32[2,96,128]{2,1,0:T(8,128)S(1)} %add.1285), channel_id=1, source_target_pairs={{0,16},{16,0},{1,17},{17,1},{2,18},{18,2},{3,19},{19,3},{4,20},{20... | collective-permute-start | bytes 294920 | tf_op jit(solution)/shard_map/ppermute | solution.py:69
  534.8 27.9 %collective-permute-start.87 = (bf16[128,1024]{1,0:T(8,128)(2,1)S(1)}, bf16[128,1024]{1,0:T(8,128)(2,1)S(1)}, u32[]{:S(2)}, u32[]{:S(2)}) collective-permute-start(bf16[128,1024]{1,0:T(8,128)(2,1)S(1)} %get-tuple-element.543), channel_id=1, source_target_pairs={{4,0},{0,2},{6,4},{2,6},{5,1},{1,3},{7,5},{3,7},{12,8},{8,10},{14,... | collective-permute-start | bytes 786440 | tf_op jit(solution)/shard_map/ppermute | solution.py:125
  546.4 16.4 %collective-permute-start.86 = (bf16[128,1024]{1,0:T(8,128)(2,1)S(1)}, bf16[128,1024]{1,0:T(8,128)(2,1)S(1)}, u32[]{:S(2)}, u32[]{:S(2)}) collective-permute-start(bf16[128,1024]{1,0:T(8,128)(2,1)S(1)} %get-tuple-element.542), channel_id=1, source_target_pairs={{0,0},{4,2},{2,4},{6,6},{1,1},{5,3},{3,5},{7,7},{8,8},{12,10},{10,... | collective-permute-start | bytes 786440 | tf_op jit(solution)/shard_map/ppermute | solution.py:124
  (248 other events, 2429.8 us)

commit v4 on v3

--- a/solution.py
+++ b/solution.py
@@ -900,10 +900,8 @@
         small[layer] = packed.reshape(-1, 128)
 
     work.add(sum_small(work, results, jnp.stack([small[layer] for layer in range(LAYERS)])), SUM_SMALL)
+    work.add(move("input_grad", from_chunks, grad_stream.astype(BF16)), ("t3",))
     work.at("t1", grads_in)
-    leaving = from_chunks(grad_stream.astype(BF16), None)
-    next(leaving)
-    input_grad = next(leaving)
     for step in range(2, 7):
         work.at("t" + str(step), work.latest)
     assert not work.tasks
@@ -921,7 +919,7 @@
     all_b_up = lax.dynamic_slice_in_dim(table[:, begin:], home * hidden_width, hidden_width, 1)
     return (
         results["activations_out"],
-        input_grad,
+        results["input_grad"],
         shared[0],
         shared[1],
         attn_outs[0],

time: 588 us -> 618 us (1.051)
  waiting for transfers between devices: 241 us -> 264 us
  starting transfers between devices: 114 us -> 124 us
    ppermute x109, waiting for transfers between devices: 241 us -> 255 us  [swap(): return lax.ppermute(value, axis, [(0, 1), (1, 0)])]
    ppermute x109, starting transfers between devices: 103 us -> 113 us  [swap(): return lax.ppermute(value, axis, [(0, 1), (1, 0)])]
    ppermute x2, waiting for transfers between devices: 0.01 us -> 9.66 us  [to_chunks(): second = lax.ppermute(second, ('c', 'b'), [(0, 2), (1, 0), (2, 3), (3, 1)])]
    unnamed x394 -> x414, local copies, waits for them, and re-layouts: 12.4 us -> 14.2 us
  transfers between devices with their start and end apart: 117 -> 117, of which waited for: 54 -> 47; matrix products, arithmetic and copies ran while one was open for 21% -> 18% of each run, Pallas kernels for 8% -> 7%
where the time goes in v4:
time: 618 us; the launch traced here: 613 us
  waiting for transfers between devices  264 us (43%)
  starting transfers between devices  124 us (20%)
  matrix products  82.1 us (13%)
  Pallas kernels  57.7 us (9%)
  other arithmetic  43.5 us (7%)
  local copies, waits for them, and re-layouts  36.9 us (6%)
    ppermute x109, waiting for transfers between devices, swap(): return lax.ppermute(value, axis, [(0, 1), (1, 0)])  255 us
    ppermute x109, starting transfers between devices, swap(): return lax.ppermute(value, axis, [(0, 1), (1, 0)])  113 us
    dot_general x22, matrix products, dot_nt(): return jnp.einsum('ti,oi->to', left, right, preferred_element_type=F32)  31.6 us
    dot_general x20, matrix products, dot(): return jnp.dot(left, right, preferred_element_type=F32)  29.6 us
    dot_general x24, matrix products, dot_tn(): return jnp.einsum('ti,to->io', left, right, preferred_element_type=F32)  20.9 us
    pallas_call x4, Pallas kernels, reduce_weights(): pl.pallas_call(functools.partial(store_kernel, layout, len(mine), len(giv...  19.5 us
    pallas_call x2, Pallas kernels, attend_back(): pl.pallas_call(functools.partial(attend_back_kernel, size), out_shape=[ja...  16.4 us
    unnamed x414, local copies, waits for them, and re-layouts  14.2 us
  transfers between devices with their start and end apart: 117, of which 47 were waited for; matrix products, arithmetic and copies ran while one was open for 18% of the time, Pallas kernels for 7%

profile of v4, /device:TPU:0, one launch (start us, length us, event | category | flops | bytes accessed | tf_op | source)
XLA Modules:
  0.0 613.4 jit_solution(16198462813898194372)
XLA Ops:
  7.1 5.3 collective-permute-start.2
  22.2 9.7 %collective-permute-done.1 = bf16[128,1024]{1,0:T(8,128)(2,1)S(1)} collective-permute-done((bf16[128,1024]{1,0:T(8,128)(2,1)S(1)}, bf16[128,1024]{1,0:T(8,128)(2,1)S(1)}, u32[]{:S(2)}, u32[]{:S(2)}) %collective-permute-start.1) | collective-permute-done | bytes 262176 | tf_op jit(solution)/shard_map/ppermute | solution.py:112
  41.8 4.4 collective-permute-done.8
  54.2 7.7 %shard_map.305 = (bf16[1024,512]{1,0:T(8,128)(2,1)}, bf16[1024,1024]{1,0:T(8,128)(2,1)}, bf16[2,256,1024]{2,1,0:T(8,128)(2,1)}) custom-call(s32[16]{0:T(128)} %stack.61.spots, bf16[4,128,512]{2,1,0:T(8,128)(2,1)} %copy-done.77, bf16[4,128,512]{2,1,0:T(8,128)(2,1)} %copy-done.76, bf16[4,128,512]{2,1,0:T(8,128)(2,1)} %copy-done.79, ...), custom_call_target="tpu_custom_call" | custom-call | bytes 8388608 | tf_op jit(solution)/shard_map/pallas_call | solution.py:290
  61.9 3.2 add_convert_fusion.15.mine
  71.3 5.1 shard_map.306
  76.9 7.2 %collective-permute-done.14 = bf16[128,1024]{1,0:T(8,128)(2,1)S(1)} collective-permute-done((bf16[128,1024]{1,0:T(8,128)(2,1)}, bf16[128,1024]{1,0:T(8,128)(2,1)S(1)}, u32[]{:S(2)}, u32[]{:S(2)}) %collective-permute-start.14) | collective-permute-done | bytes 262176 | tf_op jit(solution)/shard_map/ppermute | solution.py:69
  89.4 5.5 collective-permute-done.16
  94.9 8.6 %collective-permute-done.15 = bf16[256,1024]{1,0:T(8,128)(2,1)S(1)} collective-permute-done((bf16[256,1024]{1,0:T(8,128)(2,1)S(1)}, bf16[256,1024]{1,0:T(8,128)(2,1)S(1)}, u32[]{:S(2)}, u32[]{:S(2)}) %collective-permute-start.15) | collective-permute-done | bytes 524320 | tf_op jit(solution)/shard_map/ppermute | solution.py:69
  112.0 9.6 %collective-permute-done.20 = bf16[2,128,1024]{2,1,0:T(8,128)(2,1)} collective-permute-done((bf16[2,128,1024]{2,1,0:T(8,128)(2,1)S(1)}, bf16[2,128,1024]{2,1,0:T(8,128)(2,1)}, u32[]{:S(2)}, u32[]{:S(2)}) %collective-permute-start.20) | collective-permute-done | bytes 524320 | tf_op jit(solution)/shard_map/ppermute | solution.py:69
  124.9 4.1 fusion.23
  131.4 4.4 fusion.31
  142.8 3.9 collective-permute-done.27
  146.8 9.3 %collective-permute-done.26 = bf16[256,1024]{1,0:T(8,128)(2,1)S(1)} collective-permute-done((bf16[256,1024]{1,0:T(8,128)(2,1)S(1)}, bf16[256,1024]{1,0:T(8,128)(2,1)S(1)}, u32[]{:S(2)}, u32[]{:S(2)}) %collective-permute-start.26) | collective-permute-done | bytes 524320 | tf_op jit(solution)/shard_map/ppermute | solution.py:69
  162.2 6.0 collective-permute-done.32
  176.2 5.1 shard_map.309
  186.6 3.1 collective-permute-start.41
  189.7 7.5 %collective-permute-done.38 = bf16[2,128,1024]{2,1,0:T(8,128)(2,1)S(1)} collective-permute-done((bf16[2,128,1024]{2,1,0:T(8,128)(2,1)S(1)}, bf16[2,128,1024]{2,1,0:T(8,128)(2,1)S(1)}, u32[]{:S(2)}, u32[]{:S(2)}) %collective-permute-start.38) | collective-permute-done | bytes 524320 | tf_op jit(solution)/shard_map/ppermute | solution.py:69
  197.2 4.3 collective-permute-done.37
  206.0 10.7 %collective-permute-done.42 = bf16[256,1024]{1,0:T(8,128)(2,1)S(1)} collective-permute-done((bf16[256,1024]{1,0:T(8,128)(2,1)S(1)}, bf16[256,1024]{1,0:T(8,128)(2,1)S(1)}, u32[]{:S(2)}, u32[]{:S(2)}) %collective-permute-start.42) | collective-permute-done | bytes 524320 | tf_op jit(solution)/shard_map/ppermute | solution.py:69
  229.5 10.6 %collective-permute-done.45 = bf16[256,1024]{1,0:T(8,128)(2,1)S(1)} collective-permute-done((bf16[256,1024]{1,0:T(8,128)(2,1)S(1)}, bf16[256,1024]{1,0:T(8,128)(2,1)S(1)}, u32[]{:S(2)}, u32[]{:S(2)}) %collective-permute-start.45) | collective-permute-done | bytes 524320 | tf_op jit(solution)/shard_map/ppermute | solution.py:69
  241.7 3.6 collective-permute-start.46
  246.9 7.5 %collective-permute-done.48 = bf16[256,1024]{1,0:T(8,128)(2,1)} collective-permute-done((bf16[256,1024]{1,0:T(8,128)(2,1)}, bf16[256,1024]{1,0:T(8,128)(2,1)}, u32[]{:S(2)}, u32[]{:S(2)}) %collective-permute-start.48) | collective-permute-done | bytes 524320 | tf_op jit(solution)/shard_map/ppermute | solution.py:69
  255.8 5.4 convert_reduce_fusion
  261.2 4.7 convert_reduce_fusion.1
  280.0 3.3 collective-permute-start.49
  287.6 7.8 %collective-permute-done.49 = bf16[256,1024]{1,0:T(8,128)(2,1)S(1)} collective-permute-done((bf16[256,1024]{1,0:T(8,128)(2,1)S(1)}, bf16[256,1024]{1,0:T(8,128)(2,1)S(1)}, u32[]{:S(2)}, u32[]{:S(2)}) %collective-permute-start.49) | collective-permute-done | bytes 524320 | tf_op jit(solution)/shard_map/ppermute | solution.py:69
  313.6 8.2 %shard_map.311 = (bf16[512,512]{1,0:T(8,128)(2,1)S(1)}, f32[512,1024]{1,0:T(8,128)}, bf16[512,1024]{1,0:T(8,128)(2,1)S(1)}) custom-call(f32[4]{0:T(128)S(1)} %fusion.230.slopes, f32[256,4]{1,0:T(8,128)S(1)} %convert_element_type.597.at_rows, f32[1,1024]{1,0:T(1,128)S(1)} %convert_element_type.598.at_keys, bf16[512,512]{1,0:T(8,128)(2,1)S(1)} %copy-done.31, ...), custom_call_target="tpu_custom_call" | custom-call | flops 2013265920 | bytes 4194304 | tf_op jit(solution)/shard_map/pallas_call | solution.py:649
  322.2 12.6 %collective-permute-done.53 = bf16[256,2048]{1,0:T(8,128)(2,1)S(1)} collective-permute-done((bf16[256,2048]{1,0:T(8,128)(2,1)}, bf16[256,2048]{1,0:T(8,128)(2,1)S(1)}, u32[]{:S(2)}, u32[]{:S(2)}) %collective-permute-start.53) | collective-permute-done | bytes 1048608 | tf_op jit(solution)/shard_map/ppermute | solution.py:69
  354.4 8.1 %collective-permute-done.56 = bf16[256,1024]{1,0:T(8,128)(2,1)S(1)} collective-permute-done((bf16[256,1024]{1,0:T(8,128)(2,1)S(1)}, bf16[256,1024]{1,0:T(8,128)(2,1)S(1)}, u32[]{:S(2)}, u32[]{:S(2)}) %collective-permute-start.56) | collective-permute-done | bytes 524320 | tf_op jit(solution)/shard_map/ppermute | solution.py:69
  371.2 8.7 %collective-permute-done.62 = bf16[256,1024]{1,0:T(8,128)(2,1)S(1)} collective-permute-done((bf16[256,1024]{1,0:T(8,128)(2,1)S(1)}, bf16[256,1024]{1,0:T(8,128)(2,1)S(1)}, u32[]{:S(2)}, u32[]{:S(2)}) %collective-permute-start.62) | collective-permute-done | bytes 524320 | tf_op jit(solution)/shard_map/ppermute | solution.py:69
  379.8 4.9 collective-permute-done.61
  415.4 9.0 %collective-permute-done.70 = bf16[128,1024]{1,0:T(8,128)(2,1)S(1)} collective-permute-done((bf16[128,1024]{1,0:T(8,128)(2,1)S(1)}, bf16[128,1024]{1,0:T(8,128)(2,1)S(1)}, u32[]{:S(2)}, u32[]{:S(2)}) %collective-permute-start.70) | collective-permute-done | bytes 262176 | tf_op jit(solution)/shard_map/ppermute | solution.py:69
  432.1 10.7 %collective-permute-done.74 = bf16[2,128,1024]{2,1,0:T(8,128)(2,1)S(1)} collective-permute-done((bf16[2,128,1024]{2,1,0:T(8,128)(2,1)S(1)}, bf16[2,128,1024]{2,1,0:T(8,128)(2,1)S(1)}, u32[]{:S(2)}, u32[]{:S(2)}) %collective-permute-start.74) | collective-permute-done | bytes 524320 | tf_op jit(solution)/shard_map/ppermute | solution.py:69
  443.6 8.2 %shard_map.312 = (bf16[512,512]{1,0:T(8,128)(2,1)S(1)}, f32[512,1024]{1,0:T(8,128)}, bf16[512,1024]{1,0:T(8,128)(2,1)S(1)}) custom-call(f32[4]{0:T(128)S(1)} %fusion.230.slopes, f32[256,4]{1,0:T(8,128)S(1)} %convert_element_type.597.at_rows, f32[1,1024]{1,0:T(1,128)S(1)} %convert_element_type.598.at_keys, bf16[512,512]{1,0:T(8,128)(2,1)S(1)} %copy-done.29, ...), custom_call_target="tpu_custom_call" | custom-call | flops 2013265920 | bytes 4194304 | tf_op jit(solution)/shard_map/pallas_call | solution.py:649
  457.9 5.8 collective-permute-done.77
  479.8 5.5 shard_map.313
  486.2 4.9 collective-permute-done.87
  497.8 15.0 %collective-permute-done.89 = bf16[2,128,512]{2,1,0:T(8,128)(2,1)S(1)} collective-permute-done((bf16[2,128,512]{2,1,0:T(8,128)(2,1)S(1)}, bf16[2,128,512]{2,1,0:T(8,128)(2,1)S(1)}, u32[]{:S(2)}, u32[]{:S(2)}) %collective-permute-start.89) | collective-permute-done | bytes 262176 | tf_op jit(solution)/shard_map/ppermute | solution.py:69
  514.8 23.5 %collective-permute-done.93 = bf16[128,2048]{1,0:T(8,128)(2,1)S(1)} collective-permute-done((bf16[128,2048]{1,0:T(8,128)(2,1)S(1)}, bf16[128,2048]{1,0:T(8,128)(2,1)S(1)}, u32[]{:S(2)}, u32[]{:S(2)}) %collective-permute-start.93) | collective-permute-done | bytes 524320 | tf_op jit(solution)/shard_map/ppermute | solution.py:69
  543.5 4.7 collective-permute-done.94
  548.2 4.2 collective-permute-done.96
  555.4 11.2 %collective-permute-done.104 = bf16[2,128,1024]{2,1,0:T(8,128)(2,1)S(1)} collective-permute-done((bf16[2,128,1024]{2,1,0:T(8,128)(2,1)S(1)}, bf16[2,128,1024]{2,1,0:T(8,128)(2,1)S(1)}, u32[]{:S(2)}, u32[]{:S(2)}) %collective-permute-start.104) | collective-permute-done | bytes 524320 | tf_op jit(solution)/shard_map/ppermute | solution.py:69
  569.8 4.4 shard_map.314
  576.8 6.3 %collective-permute-start.107 = (f32[2,96,128]{2,1,0:T(8,128)S(1)}, f32[2,96,128]{2,1,0:T(8,128)S(1)}, u32[]{:S(2)}, u32[]{:S(2)}) collective-permute-start(f32[2,96,128]{2,1,0:T(8,128)S(1)} %add.1293), channel_id=1, source_target_pairs={{0,1},{1,0},{2,3},{3,2},{4,5},{5,4},{6,7},{7,6},{8,9},{9,8},{10,11... | collective-permute-start | bytes 294920 | tf_op jit(solution)/shard_map/ppermute | solution.py:69
  595.6 4.7 collective-permute-done.110
  600.4 5.3 shard_map.315
  608.8 4.4 shard_map.316
  (898 shorter events, 271.0 us)
Async XLA Ops:
  1.8 20.4 %collective-permute-start = (bf16[128,1024]{1,0:T(8,128)(2,1)S(1)}, bf16[128,1024]{1,0:T(8,128)(2,1)S(1)}, u32[]{:S(2)}, u32[]{:S(2)}) collective-permute-start(bf16[128,1024]{1,0:T(8,128)(2,1)S(1)} %get-tuple-element.556), channel_id=1, source_target_pairs={{0,0},{2,4},{4,2},{6,6},{1,1},{3,5},{5,3},{7,7},{8,8},{10,12},{12,... | collective-permute-start | bytes 786440 | tf_op jit(solution)/shard_map/ppermute | solution.py:111
  7.1 24.9 %collective-permute-start.2 = (bf16[128,1024]{1,0:T(8,128)(2,1)S(1)}, bf16[128,1024]{1,0:T(8,128)(2,1)S(1)}, u32[]{:S(2)}, u32[]{:S(2)}) collective-permute-start(bf16[128,1024]{1,0:T(8,128)(2,1)S(1)} %maximum_maximum_fusion), channel_id=1, source_target_pairs={{0,2},{2,0},{1,3},{3,1},{4,6},{6,4},{5,7},{7,5},{8,10},{10,8},{9,1... | collective-permute-start | bytes 786440 | tf_op jit(solution)/shard_map/ppermute | solution.py:69
  12.5 19.4 %collective-permute-start.1 = (bf16[128,1024]{1,0:T(8,128)(2,1)S(1)}, bf16[128,1024]{1,0:T(8,128)(2,1)S(1)}, u32[]{:S(2)}, u32[]{:S(2)}) collective-permute-start(bf16[128,1024]{1,0:T(8,128)(2,1)S(1)} %get-tuple-element.557), channel_id=1, source_target_pairs={{0,4},{2,0},{4,6},{6,2},{1,5},{3,1},{5,7},{7,3},{8,12},{10,8},{12,... | collective-permute-start | bytes 786440 | tf_op jit(solution)/shard_map/ppermute | solution.py:112
  13.3 36.4 %collective-permute-start.11 = (f32[2,512]{1,0:T(2,128)}, f32[2,512]{1,0:T(2,128)S(1)}, u32[]{:S(2)}, u32[]{:S(2)}) collective-permute-start(f32[2,512]{1,0:T(2,128)} %pad_maximum_fusion.50), channel_id=1, source_target_pairs={{0,2},{2,0},{1,3},{3,1},{4,6},{6,4},{5,7},{7,5},{8,10},{10,8},{9,1... | collective-permute-start | bytes 12296 | tf_op jit(solution)/shard_map/ppermute | solution.py:69
  16.0 51.5 %collective-permute-start.3 = (s32[4]{0:T(128)}, s32[4]{0:T(128)}, u32[]{:S(2)}, u32[]{:S(2)}) collective-permute-start(s32[4]{0:T(128)} %bitcast.5), channel_id=1, source_target_pairs={{0,4},{4,0},{1,5},{5,1},{2,6},{6,2},{3,7},{7,3},{8,12},{12,8},{9,1... | collective-permute-start | bytes 56 | tf_op jit(solution)/shard_map/ppermute | solution.py:69
  32.8 19.8 %collective-permute-start.4 = (bf16[256,1024]{1,0:T(8,128)(2,1)S(1)}, bf16[256,1024]{1,0:T(8,128)(2,1)S(1)}, u32[]{:S(2)}, u32[]{:S(2)}) collective-permute-start(bf16[256,1024]{1,0:T(8,128)(2,1)S(1)} %add_convert_fusion.40), channel_id=1, source_target_pairs={{0,1},{1,0},{2,3},{3,2},{4,5},{5,4},{6,7},{7,6},{8,9},{9,8},{10,11... | collective-permute-start | bytes 1572872 | tf_op jit(solution)/shard_map/ppermute | solution.py:69
  51.5 15.4 %collective-permute-start.12 = (bf16[128,1024]{1,0:T(8,128)(2,1)}, bf16[128,1024]{1,0:T(8,128)(2,1)S(1)}, u32[]{:S(2)}, u32[]{:S(2)}) collective-permute-start(bf16[128,1024]{1,0:T(8,128)(2,1)} %get-tuple-element.271), channel_id=1, source_target_pairs={{0,2},{2,0},{1,3},{3,1},{4,6},{6,4},{5,7},{7,5},{8,10},{10,8},{9,1... | collective-permute-start | bytes 786440 | tf_op jit(solution)/shard_map/ppermute | solution.py:69
  68.6 15.5 %collective-permute-start.14 = (bf16[128,1024]{1,0:T(8,128)(2,1)}, bf16[128,1024]{1,0:T(8,128)(2,1)S(1)}, u32[]{:S(2)}, u32[]{:S(2)}) collective-permute-start(bf16[128,1024]{1,0:T(8,128)(2,1)} %get-tuple-element.275), channel_id=1, source_target_pairs={{0,2},{2,0},{1,3},{3,1},{4,6},{6,4},{5,7},{7,5},{8,10},{10,8},{9,1... | collective-permute-start | bytes 786440 | tf_op jit(solution)/shard_map/ppermute | solution.py:69
  84.1 19.4 %collective-permute-start.15 = (bf16[256,1024]{1,0:T(8,128)(2,1)S(1)}, bf16[256,1024]{1,0:T(8,128)(2,1)S(1)}, u32[]{:S(2)}, u32[]{:S(2)}) collective-permute-start(bf16[256,1024]{1,0:T(8,128)(2,1)S(1)} %convolution_convert_fusion.25), channel_id=1, source_target_pairs={{0,1},{1,0},{2,3},{3,2},{4,5},{5,4},{6,7},{7,6},{8,9},{9,8},{10,11... | collective-permute-start | bytes 1572872 | tf_op jit(solution)/shard_map/ppermute | solution.py:69
  84.2 19.3 %collective-permute-start.18 = (bf16[128,1024]{1,0:T(8,128)(2,1)S(1)}, bf16[128,1024]{1,0:T(8,128)(2,1)S(1)}, u32[]{:S(2)}, u32[]{:S(2)}) collective-permute-start(bf16[128,1024]{1,0:T(8,128)(2,1)S(1)} %maximum_maximum_fusion.1), channel_id=1, source_target_pairs={{0,2},{2,0},{1,3},{3,1},{4,6},{6,4},{5,7},{7,5},{8,10},{10,8},{9,1... | collective-permute-start | bytes 786440 | tf_op jit(solution)/shard_map/ppermute | solution.py:69
  86.0 17.5 %collective-permute-start.17 = (bf16[1,128,1024]{2,1,0:T(8,128)(2,1)S(1)}, bf16[1,128,1024]{2,1,0:T(8,128)(2,1)S(1)}, u32[]{:S(2)}, u32[]{:S(2)}) collective-permute-start(bf16[1,128,1024]{2,1,0:T(8,128)(2,1)S(1)} %bitcast.219), channel_id=1, source_target_pairs={{0,16},{16,0},{1,17},{17,1},{2,18},{18,2},{3,19},{19,3},{4,20},{20... | collective-permute-start | bytes 786440 | tf_op jit(solution)/shard_map/ppermute | solution.py:69
  105.7 17.3 %collective-permute-start.19 = (bf16[256,1024]{1,0:T(8,128)(2,1)S(1)}, bf16[256,1024]{1,0:T(8,128)(2,1)}, u32[]{:S(2)}, u32[]{:S(2)}) collective-permute-start(bf16[256,1024]{1,0:T(8,128)(2,1)S(1)} %add_convert_fusion.39), channel_id=1, source_target_pairs={{0,1},{1,0},{2,3},{3,2},{4,5},{5,4},{6,7},{7,6},{8,9},{9,8},{10,11... | collective-permute-start | bytes 1572872 | tf_op jit(solution)/shard_map/ppermute | solution.py:69
  105.9 17.1 %collective-permute-start.21 = (bf16[2,128,1024]{2,1,0:T(8,128)(2,1)S(1)}, bf16[2,128,1024]{2,1,0:T(8,128)(2,1)S(1)}, u32[]{:S(2)}, u32[]{:S(2)}) collective-permute-start(bf16[2,128,1024]{2,1,0:T(8,128)(2,1)S(1)} %pad_maximum_fusion.29), channel_id=1, source_target_pairs={{0,8},{8,0},{1,9},{9,1},{2,10},{10,2},{3,11},{11,3},{4,12},{12,4},... | collective-permute-start | bytes 1572872 | tf_op jit(solution)/shard_map/ppermute | solution.py:69
  121.5 34.5 %collective-permute-start.30 = (bf16[128,1024]{1,0:T(8,128)(2,1)S(1)}, bf16[128,1024]{1,0:T(8,128)(2,1)S(1)}, u32[]{:S(2)}, u32[]{:S(2)}) collective-permute-start(bf16[128,1024]{1,0:T(8,128)(2,1)S(1)} %copy-done.93), channel_id=1, source_target_pairs={{0,2},{2,0},{1,3},{3,1},{4,6},{6,4},{5,7},{7,5},{8,10},{10,8},{9,1... | collective-permute-start | bytes 786440 | tf_op jit(solution)/shard_map/ppermute | solution.py:69
  136.5 19.6 %collective-permute-start.26 = (bf16[256,1024]{1,0:T(8,128)(2,1)S(1)}, bf16[256,1024]{1,0:T(8,128)(2,1)S(1)}, u32[]{:S(2)}, u32[]{:S(2)}) collective-permute-start(bf16[256,1024]{1,0:T(8,128)(2,1)S(1)} %fusion.125), channel_id=1, source_target_pairs={{0,1},{1,0},{2,3},{3,2},{4,5},{5,4},{6,7},{7,6},{8,9},{9,8},{10,11... | collective-permute-start | bytes 1572872 | tf_op jit(solution)/shard_map/ppermute | solution.py:69
  137.6 18.5 %collective-permute-start.28 = (bf16[2,128,512]{2,1,0:T(8,128)(2,1)S(1)}, bf16[2,128,512]{2,1,0:T(8,128)(2,1)S(1)}, u32[]{:S(2)}, u32[]{:S(2)}) collective-permute-start(bf16[2,128,512]{2,1,0:T(8,128)(2,1)S(1)} %pad_maximum_fusion.41), channel_id=1, source_target_pairs={{0,8},{8,0},{1,9},{9,1},{2,10},{10,2},{3,11},{11,3},{4,12},{12,4},... | collective-permute-start | bytes 786440 | tf_op jit(solution)/shard_map/ppermute | solution.py:69
  140.6 15.5 %collective-permute-start.29 = (bf16[128,1024]{1,0:T(8,128)(2,1)S(1)}, bf16[128,1024]{1,0:T(8,128)(2,1)S(1)}, u32[]{:S(2)}, u32[]{:S(2)}) collective-permute-start(bf16[128,1024]{1,0:T(8,128)(2,1)S(1)} %copy-done.94), channel_id=1, source_target_pairs={{0,2},{2,0},{1,3},{3,1},{4,6},{6,4},{5,7},{7,5},{8,10},{10,8},{9,1... | collective-permute-start | bytes 786440 | tf_op jit(solution)/shard_map/ppermute | solution.py:69
  181.9 19.6 %collective-permute-start.37 = (bf16[256,1024]{1,0:T(8,128)(2,1)S(1)}, bf16[256,1024]{1,0:T(8,128)(2,1)S(1)}, u32[]{:S(2)}, u32[]{:S(2)}) collective-permute-start(bf16[256,1024]{1,0:T(8,128)(2,1)S(1)} %convolution_convert_fusion.24), channel_id=1, source_target_pairs={{0,1},{1,0},{2,3},{3,2},{4,5},{5,4},{6,7},{7,6},{8,9},{9,8},{10,11... | collective-permute-start | bytes 1572872 | tf_op jit(solution)/shard_map/ppermute | solution.py:69
  184.5 17.0 %collective-permute-start.39 = (bf16[2,128,1024]{2,1,0:T(8,128)(2,1)S(1)}, bf16[2,128,1024]{2,1,0:T(8,128)(2,1)S(1)}, u32[]{:S(2)}, u32[]{:S(2)}) collective-permute-start(bf16[2,128,1024]{2,1,0:T(8,128)(2,1)S(1)} %pad_maximum_fusion.31), channel_id=1, source_target_pairs={{0,8},{8,0},{1,9},{9,1},{2,10},{10,2},{3,11},{11,3},{4,12},{12,4},... | collective-permute-start | bytes 1572872 | tf_op jit(solution)/shard_map/ppermute | solution.py:69
  185.9 15.6 %collective-permute-start.40 = (bf16[128,1024]{1,0:T(8,128)(2,1)S(1)}, bf16[128,1024]{1,0:T(8,128)(2,1)S(1)}, u32[]{:S(2)}, u32[]{:S(2)}) collective-permute-start(bf16[128,1024]{1,0:T(8,128)(2,1)S(1)} %get-tuple-element.555), channel_id=1, source_target_pairs={{0,0},{2,4},{4,2},{6,6},{1,1},{3,5},{5,3},{7,7},{8,8},{10,12},{12,... | collective-permute-start | bytes 786440 | tf_op jit(solution)/shard_map/ppermute | solution.py:111
  228.5 26.0 %collective-permute-start.48 = (bf16[256,1024]{1,0:T(8,128)(2,1)}, bf16[256,1024]{1,0:T(8,128)(2,1)}, u32[]{:S(2)}, u32[]{:S(2)}) collective-permute-start(bf16[256,1024]{1,0:T(8,128)(2,1)} %get-tuple-element.530), channel_id=1, source_target_pairs={{0,1},{1,0},{2,3},{3,2},{4,5},{5,4},{6,7},{7,6},{8,9},{9,8},{10,11... | collective-permute-start | bytes 1572872 | tf_op jit(solution)/shard_map/ppermute | solution.py:69
  272.1 23.3 %collective-permute-start.50 = (bf16[512,2048]{1,0:T(8,128)(2,1)}, bf16[512,2048]{1,0:T(8,128)(2,1)}, u32[]{:S(2)}, u32[]{:S(2)}) collective-permute-start(bf16[512,2048]{1,0:T(8,128)(2,1)} %convolution_convert_fusion.5), channel_id=1, source_target_pairs={{0,4},{4,0},{1,5},{5,1},{2,6},{6,2},{3,7},{7,3},{8,12},{12,8},{9,1... | collective-permute-start | bytes 6291464 | tf_op jit(solution)/shard_map/ppermute | solution.py:69
  274.8 20.7 %collective-permute-start.51 = (bf16[512,2048]{1,0:T(8,128)(2,1)}, bf16[512,2048]{1,0:T(8,128)(2,1)}, u32[]{:S(2)}, u32[]{:S(2)}) collective-permute-start(bf16[512,2048]{1,0:T(8,128)(2,1)} %convolution_convert_fusion.4), channel_id=1, source_target_pairs={{0,4},{4,0},{1,5},{5,1},{2,6},{6,2},{3,7},{7,3},{8,12},{12,8},{9,1... | collective-permute-start | bytes 6291464 | tf_op jit(solution)/shard_map/ppermute | solution.py:69
  280.0 15.4 %collective-permute-start.49 = (bf16[256,1024]{1,0:T(8,128)(2,1)S(1)}, bf16[256,1024]{1,0:T(8,128)(2,1)S(1)}, u32[]{:S(2)}, u32[]{:S(2)}) collective-permute-start(bf16[256,1024]{1,0:T(8,128)(2,1)S(1)} %copy-done.89), channel_id=1, source_target_pairs={{0,1},{1,0},{2,3},{3,2},{4,5},{5,4},{6,7},{7,6},{8,9},{9,8},{10,11... | collective-permute-start | bytes 1572872 | tf_op jit(solution)/shard_map/ppermute | solution.py:69
  305.3 29.5 %collective-permute-start.54 = (bf16[256,2048]{1,0:T(8,128)(2,1)}, bf16[256,2048]{1,0:T(8,128)(2,1)S(1)}, u32[]{:S(2)}, u32[]{:S(2)}) collective-permute-start(bf16[256,2048]{1,0:T(8,128)(2,1)} %add_convert_fusion.12), channel_id=1, source_target_pairs={{0,16},{16,0},{1,17},{17,1},{2,18},{18,2},{3,19},{19,3},{4,20},{20... | collective-permute-start | bytes 3145736 | tf_op jit(solution)/shard_map/ppermute | solution.py:69
  310.6 24.2 %collective-permute-start.53 = (bf16[256,2048]{1,0:T(8,128)(2,1)}, bf16[256,2048]{1,0:T(8,128)(2,1)S(1)}, u32[]{:S(2)}, u32[]{:S(2)}) collective-permute-start(bf16[256,2048]{1,0:T(8,128)(2,1)} %add_convert_fusion.13), channel_id=1, source_target_pairs={{0,8},{8,0},{1,9},{9,1},{2,10},{10,2},{3,11},{11,3},{4,12},{12,4},... | collective-permute-start | bytes 3145736 | tf_op jit(solution)/shard_map/ppermute | solution.py:69
  337.1 25.4 %collective-permute-start.58 = (bf16[128,2048]{1,0:T(8,128)(2,1)S(1)}, bf16[128,2048]{1,0:T(8,128)(2,1)S(1)}, u32[]{:S(2)}, u32[]{:S(2)}) collective-permute-start(bf16[128,2048]{1,0:T(8,128)(2,1)S(1)} %constant_dynamic-slice_fusion.9), channel_id=1, source_target_pairs={{0,8},{8,0},{1,9},{9,1},{2,10},{10,2},{3,11},{11,3},{4,12},{12,4},... | collective-permute-start | bytes 1572872 | tf_op jit(solution)/shard_map/ppermute | solution.py:69
  363.9 20.9 %collective-permute-start.61 = (bf16[256,1024]{1,0:T(8,128)(2,1)S(1)}, bf16[256,1024]{1,0:T(8,128)(2,1)S(1)}, u32[]{:S(2)}, u32[]{:S(2)}) collective-permute-start(bf16[256,1024]{1,0:T(8,128)(2,1)S(1)} %get-tuple-element.524), channel_id=1, source_target_pairs={{0,1},{1,0},{2,3},{3,2},{4,5},{5,4},{6,7},{7,6},{8,9},{9,8},{10,11... | collective-permute-start | bytes 1572872 | tf_op jit(solution)/shard_map/ppermute | solution.py:69
  365.8 19.0 %collective-permute-start.63 = (bf16[256,1024]{1,0:T(8,128)(2,1)S(1)}, bf16[256,1024]{1,0:T(8,128)(2,1)S(1)}, u32[]{:S(2)}, u32[]{:S(2)}) collective-permute-start(bf16[256,1024]{1,0:T(8,128)(2,1)S(1)} %add_convert_fusion.35), channel_id=1, source_target_pairs={{0,16},{16,0},{1,17},{17,1},{2,18},{18,2},{3,19},{19,3},{4,20},{20... | collective-permute-start | bytes 1572872 | tf_op jit(solution)/shard_map/ppermute | solution.py:69
  369.2 31.2 %collective-permute-start.65 = (bf16[128,2048]{1,0:T(8,128)(2,1)S(1)}, bf16[128,2048]{1,0:T(8,128)(2,1)S(1)}, u32[]{:S(2)}, u32[]{:S(2)}) collective-permute-start(bf16[128,2048]{1,0:T(8,128)(2,1)S(1)} %pad_maximum_fusion.32), channel_id=1, source_target_pairs={{0,2},{2,0},{1,3},{3,1},{4,6},{6,4},{5,7},{7,5},{8,10},{10,8},{9,1... | collective-permute-start | bytes 1572872 | tf_op jit(solution)/shard_map/ppermute | solution.py:69
  392.7 18.3 %collective-permute-start.64 = (bf16[256,1024]{1,0:T(8,128)(2,1)S(1)}, bf16[256,1024]{1,0:T(8,128)(2,1)S(1)}, u32[]{:S(2)}, u32[]{:S(2)}) collective-permute-start(bf16[256,1024]{1,0:T(8,128)(2,1)S(1)} %fusion.128), channel_id=1, source_target_pairs={{0,1},{1,0},{2,3},{3,2},{4,5},{5,4},{6,7},{7,6},{8,9},{9,8},{10,11... | collective-permute-start | bytes 1572872 | tf_op jit(solution)/shard_map/ppermute | solution.py:69
  394.8 29.7 %collective-permute-start.72 = (bf16[512,2048]{1,0:T(8,128)(2,1)S(1)}, bf16[512,2048]{1,0:T(8,128)(2,1)S(1)}, u32[]{:S(2)}, u32[]{:S(2)}) collective-permute-start(bf16[512,2048]{1,0:T(8,128)(2,1)S(1)} %convolution_convert_fusion), channel_id=1, source_target_pairs={{0,4},{4,0},{1,5},{5,1},{2,6},{6,2},{3,7},{7,3},{8,12},{12,8},{9,1... | collective-permute-start | bytes 6291464 | tf_op jit(solution)/shard_map/ppermute | solution.py:69
  396.2 28.3 %collective-permute-start.71 = (bf16[512,2048]{1,0:T(8,128)(2,1)S(1)}, bf16[512,2048]{1,0:T(8,128)(2,1)S(1)}, u32[]{:S(2)}, u32[]{:S(2)}) collective-permute-start(bf16[512,2048]{1,0:T(8,128)(2,1)S(1)} %convolution_convert_fusion.1), channel_id=1, source_target_pairs={{0,4},{4,0},{1,5},{5,1},{2,6},{6,2},{3,7},{7,3},{8,12},{12,8},{9,1... | collective-permute-start | bytes 6291464 | tf_op jit(solution)/shard_map/ppermute | solution.py:69
  426.7 16.1 %collective-permute-start.73 = (bf16[256,1024]{1,0:T(8,128)(2,1)S(1)}, bf16[256,1024]{1,0:T(8,128)(2,1)S(1)}, u32[]{:S(2)}, u32[]{:S(2)}) collective-permute-start(bf16[256,1024]{1,0:T(8,128)(2,1)S(1)} %get-tuple-element.527), channel_id=1, source_target_pairs={{0,1},{1,0},{2,3},{3,2},{4,5},{5,4},{6,7},{7,6},{8,9},{9,8},{10,11... | collective-permute-start | bytes 1572872 | tf_op jit(solution)/shard_map/ppermute | solution.py:69
  426.8 16.0 %collective-permute-start.75 = (bf16[2,128,1024]{2,1,0:T(8,128)(2,1)S(1)}, bf16[2,128,1024]{2,1,0:T(8,128)(2,1)S(1)}, u32[]{:S(2)}, u32[]{:S(2)}) collective-permute-start(bf16[2,128,1024]{2,1,0:T(8,128)(2,1)S(1)} %pad_maximum_fusion.34), channel_id=1, source_target_pairs={{0,8},{8,0},{1,9},{9,1},{2,10},{10,2},{3,11},{11,3},{4,12},{12,4},... | collective-permute-start | bytes 1572872 | tf_op jit(solution)/shard_map/ppermute | solution.py:69
  428.9 35.5 %collective-permute-start.78 = (bf16[256,2048]{1,0:T(8,128)(2,1)S(1)}, bf16[256,2048]{1,0:T(8,128)(2,1)S(1)}, u32[]{:S(2)}, u32[]{:S(2)}) collective-permute-start(bf16[256,2048]{1,0:T(8,128)(2,1)S(1)} %add_convert_fusion.4), channel_id=1, source_target_pairs={{0,16},{16,0},{1,17},{17,1},{2,18},{18,2},{3,19},{19,3},{4,20},{20... | collective-permute-start | bytes 3145736 | tf_op jit(solution)/shard_map/ppermute | solution.py:69
  430.8 32.9 %collective-permute-start.77 = (bf16[256,2048]{1,0:T(8,128)(2,1)S(1)}, bf16[256,2048]{1,0:T(8,128)(2,1)S(1)}, u32[]{:S(2)}, u32[]{:S(2)}) collective-permute-start(bf16[256,2048]{1,0:T(8,128)(2,1)S(1)} %add_convert_fusion.5), channel_id=1, source_target_pairs={{0,8},{8,0},{1,9},{9,1},{2,10},{10,2},{3,11},{11,3},{4,12},{12,4},... | collective-permute-start | bytes 3145736 | tf_op jit(solution)/shard_map/ppermute | solution.py:69
  469.3 15.9 %collective-permute-start.81 = (bf16[256,1024]{1,0:T(8,128)(2,1)S(1)}, bf16[256,1024]{1,0:T(8,128)(2,1)S(1)}, u32[]{:S(2)}, u32[]{:S(2)}) collective-permute-start(bf16[256,1024]{1,0:T(8,128)(2,1)S(1)} %fusion.124), channel_id=1, source_target_pairs={{0,1},{1,0},{2,3},{3,2},{4,5},{5,4},{6,7},{7,6},{8,9},{9,8},{10,11... | collective-permute-start | bytes 1572872 | tf_op jit(solution)/shard_map/ppermute | solution.py:69
  492.6 20.7 %collective-permute-start.92 = (f32[2,96,128]{2,1,0:T(8,128)S(1)}, f32[2,96,128]{2,1,0:T(8,128)S(1)}, u32[]{:S(2)}, u32[]{:S(2)}) collective-permute-start(f32[2,96,128]{2,1,0:T(8,128)S(1)} %pad_maximum_fusion.47), channel_id=1, source_target_pairs={{0,4},{4,0},{1,5},{5,1},{2,6},{6,2},{3,7},{7,3},{8,12},{12,8},{9,1... | collective-permute-start | bytes 294920 | tf_op jit(solution)/shard_map/ppermute | solution.py:69
  492.9 20.4 %collective-permute-start.91 = (bf16[256,1024]{1,0:T(8,128)(2,1)S(1)}, bf16[256,1024]{1,0:T(8,128)(2,1)S(1)}, u32[]{:S(2)}, u32[]{:S(2)}) collective-permute-start(bf16[256,1024]{1,0:T(8,128)(2,1)S(1)} %add_convert_fusion.24), channel_id=1, source_target_pairs={{0,16},{16,0},{1,17},{17,1},{2,18},{18,2},{3,19},{19,3},{4,20},{20... | collective-permute-start | bytes 1572872 | tf_op jit(solution)/shard_map/ppermute | solution.py:69
  493.6 19.3 %collective-permute-start.90 = (bf16[2,128,512]{2,1,0:T(8,128)(2,1)S(1)}, bf16[2,128,512]{2,1,0:T(8,128)(2,1)S(1)}, u32[]{:S(2)}, u32[]{:S(2)}) collective-permute-start(bf16[2,128,512]{2,1,0:T(8,128)(2,1)S(1)} %pad_maximum_fusion.44), channel_id=1, source_target_pairs={{0,8},{8,0},{1,9},{9,1},{2,10},{10,2},{3,11},{11,3},{4,12},{12,4},... | collective-permute-start | bytes 786440 | tf_op jit(solution)/shard_map/ppermute | solution.py:69
  494.8 18.1 %collective-permute-start.89 = (bf16[2,128,512]{2,1,0:T(8,128)(2,1)S(1)}, bf16[2,128,512]{2,1,0:T(8,128)(2,1)S(1)}, u32[]{:S(2)}, u32[]{:S(2)}) collective-permute-start(bf16[2,128,512]{2,1,0:T(8,128)(2,1)S(1)} %pad_maximum_fusion.43), channel_id=1, source_target_pairs={{0,16},{16,0},{1,17},{17,1},{2,18},{18,2},{3,19},{19,3},{4,20},{20... | collective-permute-start | bytes 786440 | tf_op jit(solution)/shard_map/ppermute | solution.py:69
  496.6 16.7 %collective-permute-start.86 = (bf16[256,1024]{1,0:T(8,128)(2,1)S(1)}, bf16[256,1024]{1,0:T(8,128)(2,1)S(1)}, u32[]{:S(2)}, u32[]{:S(2)}) collective-permute-start(bf16[256,1024]{1,0:T(8,128)(2,1)S(1)} %add_convert_fusion.26), channel_id=1, source_target_pairs={{0,8},{8,0},{1,9},{9,1},{2,10},{10,2},{3,11},{11,3},{4,12},{12,4},... | collective-permute-start | bytes 1572872 | tf_op jit(solution)/shard_map/ppermute | solution.py:69
  512.9 25.4 %collective-permute-start.93 = (bf16[128,2048]{1,0:T(8,128)(2,1)S(1)}, bf16[128,2048]{1,0:T(8,128)(2,1)S(1)}, u32[]{:S(2)}, u32[]{:S(2)}) collective-permute-start(bf16[128,2048]{1,0:T(8,128)(2,1)S(1)} %pad_maximum_fusion.35), channel_id=1, source_target_pairs={{0,2},{2,0},{1,3},{3,1},{4,6},{6,4},{5,7},{7,5},{8,10},{10,8},{9,1... | collective-permute-start | bytes 1572872 | tf_op jit(solution)/shard_map/ppermute | solution.py:69
  513.6 38.8 %collective-permute-start.97 = (bf16[128,1024]{1,0:T(8,128)(2,1)S(1)}, bf16[128,1024]{1,0:T(8,128)(2,1)S(1)}, u32[]{:S(2)}, u32[]{:S(2)}) collective-permute-start(bf16[128,1024]{1,0:T(8,128)(2,1)S(1)} %constant_dynamic-slice_fusion.8), channel_id=1, source_target_pairs={{0,8},{8,0},{1,9},{9,1},{2,10},{10,2},{3,11},{11,3},{4,12},{12,4},... | collective-permute-start | bytes 786440 | tf_op jit(solution)/shard_map/ppermute | solution.py:69
  552.6 21.5 %collective-permute-start.105 = (bf16[2,128,1024]{2,1,0:T(8,128)(2,1)S(1)}, bf16[2,128,1024]{2,1,0:T(8,128)(2,1)S(1)}, u32[]{:S(2)}, u32[]{:S(2)}) collective-permute-start(bf16[2,128,1024]{2,1,0:T(8,128)(2,1)S(1)} %pad_maximum_fusion.37), channel_id=1, source_target_pairs={{0,8},{8,0},{1,9},{9,1},{2,10},{10,2},{3,11},{11,3},{4,12},{12,4},... | collective-permute-start | bytes 1572872 | tf_op jit(solution)/shard_map/ppermute | solution.py:69
  555.3 18.9 %collective-permute-start.106 = (bf16[128,1024]{1,0:T(8,128)(2,1)S(1)}, bf16[128,1024]{1,0:T(8,128)(2,1)S(1)}, u32[]{:S(2)}, u32[]{:S(2)}) collective-permute-start(bf16[128,1024]{1,0:T(8,128)(2,1)S(1)} %pad_maximum_fusion.45), channel_id=1, source_target_pairs={{0,2},{2,0},{1,3},{3,1},{4,6},{6,4},{5,7},{7,5},{8,10},{10,8},{9,1... | collective-permute-start | bytes 786440 | tf_op jit(solution)/shard_map/ppermute | solution.py:69
  590.0 15.8 %collective-permute-start.114 = (bf16[2,128,512]{2,1,0:T(8,128)(2,1)S(1)}, bf16[2,128,512]{2,1,0:T(8,128)(2,1)S(1)}, u32[]{:S(2)}, u32[]{:S(2)}) collective-permute-start(bf16[2,128,512]{2,1,0:T(8,128)(2,1)S(1)} %pad_maximum_fusion.46), channel_id=1, source_target_pairs={{0,8},{8,0},{1,9},{9,1},{2,10},{10,2},{3,11},{11,3},{4,12},{12,4},... | collective-permute-start | bytes 786440 | tf_op jit(solution)/shard_map/ppermute | solution.py:69
  (258 other events, 2510.8 us)
